TPU v7x, 32 devices: a whole 2x2x4 slice. The times are simulated.
32 devices in a mesh: design: 2 (over y), gx: 4 (over z), gy: 4 (over x, core).
Axes of the slice: x: 2, y: 2, z: 4, core: 2. Of those that a mesh axis runs over, the one named last changes fastest.
Arguments:
- e_field: float32 [6, 8, 64, 1024], P('design', None, 'gx', 'gy'), parts along dimension 0, may hold values from -6 to 6
- h_field: float32 [6, 8, 64, 1024], P('design', None, 'gx', 'gy'), parts along dimension 0, may hold values from -6 to 6
- pol_now: float32 [6, 8, 64, 1024], P('design', None, 'gx', 'gy'), parts along dimension 0, may hold values from -3 to 3
- pol_old: float32 [6, 8, 64, 1024], P('design', None, 'gx', 'gy'), parts along dimension 0, may hold values from -3 to 3
- eps_inf: float32 [16, 64, 1024], P('design', 'gx', 'gy'), parts along dimension 0, may hold values from 1 to 4
- materials: int32 [16, 64, 1024], P('design', 'gx', 'gy'), parts along dimension 0, may hold values from 0 to 15
- surface: int32 [4, 64, 1024], P('design', 'gx', 'gy'), parts along dimension 0, may hold values 0 or 1
- poles: float32 [3, 16], replicated, may hold values from 0.2 to 0.9
- directions: float32 [4096, 2], replicated, may hold values from -0.7 to 0.7
Outputs:
- e_final: float32 [6, 8, 64, 1024], P('design', None, 'gx', 'gy'), parts along dimension 0
- h_final: float32 [6, 8, 64, 1024], P('design', None, 'gx', 'gy'), parts along dimension 0
- far_field: float32 [4096, 32], P(('gx', 'gy'), 'design'), parts along dimension 1
There are 2 independent parts, one for each index of `design`. A program takes and returns all parts, laid end to end along the dimension named above; an argument that names none is the same for every part. Nothing has to cross between parts.
All inputs are finite; a program needn't handle non-finite values. No bound on the sum of `surface` on one device may be relied on, other than what follows from the above.
Results may differ from a plain program's by a relative error of at most 0.0003.
Values sent between devices are 32-bit elements; how exact they have to be, the bound alone decides.
No kernel may reach another device: no remote copies, remote signals or barrier semaphores. Data moves between devices by JAX's collectives and lax.ppermute only.
A program may use at most 64 MiB of HBM per device.

v0:
```python
from functools import partial
import math

import jax
import jax.numpy as jnp
from jax import lax
from jax.sharding import PartitionSpec as P

STEPS = 2


COURANT = 0.5
WAVE = 0.3
OMEGA = 0.25


def from_behind(array, axis, by):
    devices = lax.axis_size(axis)
    pairs = [(i, i + by) for i in range(devices) if 0 <= i + by < devices]
    return lax.ppermute(array, axis, pairs)


def pole_table(poles, materials):
    omega_dt = poles[0]
    gamma_dt = poles[1]
    strength = poles[2]
    denominator = 1.0 + 0.5 * gamma_dt
    table_a = (2.0 - omega_dt * omega_dt) / denominator
    table_b = -(1.0 - 0.5 * gamma_dt) / denominator
    table_c = strength * omega_dt * omega_dt / denominator
    coef_a = jnp.zeros(materials.shape, poles.dtype)
    coef_b = jnp.zeros(materials.shape, poles.dtype)
    coef_c = jnp.zeros(materials.shape, poles.dtype)
    for number in range(poles.shape[1]):
        selected = materials == number
        coef_a = jnp.where(selected, table_a[number], coef_a)
        coef_b = jnp.where(selected, table_b[number], coef_b)
        coef_c = jnp.where(selected, table_c[number], coef_c)
    return (coef_a, coef_b, coef_c)


def curl_e(field, next_x, next_y):
    along_x = jnp.concatenate([field[:, :, 1:, :], next_x[:, :, None, :]], axis=2)
    along_y = jnp.concatenate([field[:, :, :, 1:], next_y[:, :, :, None]], axis=3)
    along_z = jnp.concatenate([field[:, 1:], jnp.zeros_like(field[:, :1])], axis=1)
    return jnp.stack(
        [
            along_y[2] - field[2] - (along_z[1] - field[1]),
            along_z[0] - field[0] - (along_x[2] - field[2]),
            along_x[1] - field[1] - (along_y[0] - field[0]),
        ]
    )


def curl_h(field, prev_x, prev_y):
    along_x = jnp.concatenate([prev_x[:, :, None, :], field[:, :, :-1, :]], axis=2)
    along_y = jnp.concatenate([prev_y[:, :, :, None], field[:, :, :, :-1]], axis=3)
    along_z = jnp.concatenate([jnp.zeros_like(field[:, :1]), field[:, :-1]], axis=1)
    return jnp.stack(
        [
            field[2] - along_y[2] - (field[1] - along_z[1]),
            field[0] - along_z[0] - (field[2] - along_x[2]),
            field[1] - along_x[1] - (field[0] - along_y[0]),
        ]
    )


def next_faces(field):
    face_x = from_behind(field[:, :, 0, :], "gx", -1)
    face_y = from_behind(field[:, :, :, 0], "gy", -1)
    return (face_x, face_y)


def prev_faces(field):
    face_x = from_behind(field[:, :, -1, :], "gx", 1)
    face_y = from_behind(field[:, :, :, -1], "gy", 1)
    return (face_x, face_y)


def surface_plane(e_now, h_now, surface):
    rows = []
    for layer, level in ((0, 0), (1, e_now.shape[1] - 1)):
        weight = surface[layer].astype(e_now.dtype)
        rows = rows + [
            e_now[0, level] * weight,
            e_now[1, level] * weight,
            h_now[0, level] * weight,
            h_now[1, level] * weight,
        ]
    return jnp.stack(rows)


def project(items, chosen, x_coords, y_coords, scale):
    count = chosen.shape[0]
    width_x = x_coords.shape[0]
    width_y = y_coords.shape[0]
    angle_y = WAVE * chosen[:, 1:2] * y_coords[None, :]
    table_y = jnp.concatenate([jnp.cos(angle_y), jnp.sin(angle_y)], axis=0)
    real_sum = jnp.zeros((8, count), jnp.float32)
    imag_sum = jnp.zeros((8, count), jnp.float32)
    for plane, number in items:
        partial_rows = lax.dot_general(
            plane.reshape(8 * width_x, width_y),
            table_y,
            (((1,), (1,)), ((), ())),
            precision=lax.Precision.HIGHEST,
            preferred_element_type=jnp.float32,
        )
        partial_rows = partial_rows.reshape(8, width_x, 2, count)
        part_cos = partial_rows[:, :, 0]
        part_sin = partial_rows[:, :, 1]
        angle_x = WAVE * chosen[:, 0:1] * x_coords[None, :] - OMEGA * number
        cos_x = jnp.cos(angle_x).T[None]
        sin_x = jnp.sin(angle_x).T[None]
        real_sum = jnp.sum(cos_x * part_cos - sin_x * part_sin, axis=1)
        imag_sum = jnp.sum(sin_x * part_cos + cos_x * part_sin, axis=1)
    return jnp.concatenate([real_sum.T, imag_sum.T], axis=1) * scale


def block_terms(items, directions, x_coords, y_coords, scale, start, count):
    return project(items, directions, x_coords, y_coords, scale)


def local(e_field, h_field, pol_now, pol_old, eps_inf, materials, surface, poles, directions):
    width_x = e_field.shape[2]
    width_y = e_field.shape[3]
    scale = 1.0 / math.sqrt(width_x * lax.axis_size("gx") * width_y * lax.axis_size("gy"))
    x_coords = (lax.axis_index("gx") * width_x + jnp.arange(width_x, dtype=jnp.int32)).astype(
        jnp.float32
    )
    y_coords = (lax.axis_index("gy") * width_y + jnp.arange(width_y, dtype=jnp.int32)).astype(
        jnp.float32
    )
    owned = directions.shape[0] // (lax.axis_size("gx") * lax.axis_size("gy"))
    coef_a, coef_b, coef_c = pole_table(poles, materials)
    e_now, h_now, keep_now, keep_old = (e_field, h_field, pol_now, pol_old)
    far_field = jnp.zeros((owned, 16), jnp.float32)
    for number in range(1, STEPS + 1):
        face_x, face_y = next_faces(e_now)
        h_now = h_now - COURANT * curl_e(e_now, face_x, face_y)
        keep_next = coef_a * keep_now + coef_b * keep_old + coef_c * e_now
        back_x, back_y = prev_faces(h_now)
        e_now = e_now + (COURANT * curl_h(h_now, back_x, back_y) - (keep_next - keep_now)) / eps_inf
        keep_old, keep_now = (keep_now, keep_next)
        plane = surface_plane(e_now, h_now, surface)
        terms = partial(block_terms, [(plane, number)], directions, x_coords, y_coords, scale)
        far_field = far_field + lax.psum_scatter(
            terms(jnp.int32(0), lax.axis_size(("gx", "gy")) * owned),
            ("gx", "gy"),
            scatter_dimension=0,
            tiled=True,
        )
    return (e_now, h_now, far_field)


def solution(mesh):
    placed = (
        P("design", None, "gx", "gy"),
        P("design", None, "gx", "gy"),
        P("design", None, "gx", "gy"),
        P("design", None, "gx", "gy"),
        P("design", "gx", "gy"),
        P("design", "gx", "gy"),
        P("design", "gx", "gy"),
        P(),
        P(),
    )
    return jax.shard_map(
        local,
        mesh=mesh,
        in_specs=placed,
        out_specs=(
            P("design", None, "gx", "gy"),
            P("design", None, "gx", "gy"),
            P(("gx", "gy"), "design"),
        ),
        check_vma=False,
    )
```

profile of v0, /device:TPU:0, one launch (start us, length us, event | category | flops | bytes accessed | tf_op | source)
XLA Modules:
  0.0 194.9 jit_solution(17700669352860454003)
XLA Ops:
  7.2 0.9 slice.410
  8.3 1.3 collective-permute-start
  9.7 0.9 slice.419
  10.6 1.3 collective-permute-start.1
  11.9 0.8 bitcast_divide_fusion
  12.7 0.7 fusion.65
  13.4 0.7 fusion.63
  14.2 0.9 slice_multiply_fusion.1
  15.1 14.7 %multiply_cosine_fusion = (f32[4096,256]{1,0:T(8,128)S(1)}, f32[4096,256]{1,0:T(8,128)S(1)}) fusion(f32[256]{0:T(256)S(1)} %add_convert_fusion, f32[4096]{0:T(1024)S(1)} %bitcast.243), kind=kLoop, calls=%fused_computation.2 | loop fusion | flops 1048576 | bytes 8406016 | tf_op jit(solution)/shard_map/cos | solution.py:98
  29.8 3.9 %pad_maximum_fusion = f32[8192,256]{1,0:T(8,128)} fusion(f32[4096,256]{1,0:T(8,128)S(1)} %get-tuple-element.47, f32[4096,256]{1,0:T(8,128)S(1)} %get-tuple-element.46), kind=kLoop, calls=%fused_computation | loop fusion | flops 2097152 | bytes 16777216 | tf_op jit(solution)/shard_map/concatenate | solution.py:98
  33.7 10.6 %select_select_fusion.2 = (f32[8,16,256]{2,1,0:T(8,128)S(1)}, pred[8,16,256]{2,1,0:T(8,128)(4,1)S(1)}, pred[8,16,256]{2,1,0:T(8,128)(4,1)S(1)}, pred[8,16,256]{2...) fusion(f32[]{:T(128)} %bitcast.22, f32[]{:T(128)} %bitcast.21, ...), kind=kLoop, calls=%fused_computation.93 | loop fusion | flops 1048576 | bytes 786496 | tf_op jit(solution)/shard_map/jit(_where)/select_n | solution.py:36
  44.5 10.5 %select_select_fusion.1 = f32[8,16,256]{2,1,0:T(8,128)S(1)} fusion(pred[8,16,256]{2,1,0:T(8,128)(4,1)S(1)} %get-tuple-element.23, pred[8,16,256]{2,1,0:T(8,128)(4,1)S(1)} %get-tuple-element.22, pred[8,16,256]{2,1,0:T(8,128)(4,1)S(1)} %get-tuple-element.21, pred[8,16,256]{2,1,0:T(8,128)(4,1)S(1)} %get-tuple-element.20, ...), kind=kLoop, calls=%fused_computation.92 | loop fusion | flops 524288 | bytes 655424 | tf_op jit(solution)/shard_map/jit(_where)/select_n | solution.py:37
  55.0 0.7 fusion.64
  56.1 0.9 copy.33
  57.0 1.0 fusion.14
  58.2 0.2 slice_reduce_fusion.2
  58.4 3.0 %collective-permute-start.2 = (f32[3,8,16]{2,1,0:T(8,128)S(1)}, f32[3,8,16]{2,1,0:T(8,128)S(1)}, u32[]{:S(2)}, u32[]{:S(2)}) collective-permute-start(f32[3,8,16]{2,1,0:T(8,128)S(1)} %slice_reduce_fusion.2), channel_id=1, source_target_pairs={{0,1},{1,2},{2,3},{4,5},{5,6},{6,7},{8,9},{9,10},{10,11},{12,13},{... | collective-permute-start | bytes 4616 | tf_op jit(solution)/shard_map/ppermute | solution.py:20
  61.5 5.6 %collective-permute-start.3 = (f32[3,8,256]{2,1,0:T(8,128)S(1)}, f32[3,8,256]{2,1,0:T(8,128)S(1)}, u32[]{:S(2)}, u32[]{:S(2)}) collective-permute-start(f32[3,8,256]{2,1,0:T(8,128)S(1)} %bitcast.245), channel_id=1, source_target_pairs={{0,4},{4,8},{8,12},{1,5},{5,9},{9,13},{2,6},{6,10},{10,14},{3,7},{... | collective-permute-start | bytes 73736 | tf_op jit(solution)/shard_map/ppermute | solution.py:20
  67.0 11.2 %select_select_fusion = f32[8,16,256]{2,1,0:T(8,128)S(1)} fusion(pred[8,16,256]{2,1,0:T(8,128)(4,1)} %copy-done.41, pred[8,16,256]{2,1,0:T(8,128)(4,1)} %copy-done.40, pred[8,16,256]{2,1,0:T(8,128)(4,1)} %copy-done.39, pred[8,16,256]{2,1,0:T(8,128)(4,1)} %copy-done.38, pred[8,16,256]{2,1,0:T(8,128)(4,1)} %copy-done.37, pred[8,16,256]{2,1,0:T(8,128)(4,1)} %copy-done.36, ...), kind=kLoop, calls=%fused_computation.91 | loop fusion | flops 524288 | bytes 655424 | tf_op jit(solution)/shard_map/jit(_where)/select_n | solution.py:38
  78.3 0.2 copy.35
  78.5 0.2 fusion.18
  78.8 1.2 fusion.3
  80.2 1.5 collective-permute-start.4
  81.7 0.6 copy.57
  82.3 1.3 collective-permute-start.5
  83.6 0.5 add_convert_fusion.1
  84.4 0.6 copy-done.44
  85.0 1.6 copy.37
  86.6 1.7 collective-permute-done.5
  88.3 0.8 broadcast_in_dim.238
  89.1 1.0 fusion.22
  90.1 1.2 fusion.4
  91.4 0.2 slice_reduce_fusion
  91.6 2.8 %collective-permute-start.6 = (f32[3,8,16]{2,1,0:T(8,128)S(1)}, f32[3,8,16]{2,1,0:T(8,128)S(1)}, u32[]{:S(2)}, u32[]{:S(2)}) collective-permute-start(f32[3,8,16]{2,1,0:T(8,128)S(1)} %slice_reduce_fusion), channel_id=1, source_target_pairs={{0,1},{1,2},{2,3},{4,5},{5,6},{6,7},{8,9},{9,10},{10,11},{12,13},{... | collective-permute-start | bytes 4616 | tf_op jit(solution)/shard_map/ppermute | solution.py:20
  94.4 0.6 copy.56
  95.0 4.3 %collective-permute-start.7 = (f32[3,8,256]{2,1,0:T(8,128)}, f32[3,8,256]{2,1,0:T(8,128)}, u32[]{:S(2)}, u32[]{:S(2)}) collective-permute-start(f32[3,8,256]{2,1,0:T(8,128)} %bitcast.222), channel_id=1, source_target_pairs={{0,4},{4,8},{8,12},{1,5},{5,9},{9,13},{2,6},{6,10},{10,14},{3,7},{... | collective-permute-start | bytes 73736 | tf_op jit(solution)/shard_map/ppermute | solution.py:20
  99.3 3.4 %fusion.11 = (f32[16,4096]{1,0:T(8,128)}, f32[16,4096]{1,0:T(8,128)}, f32[16,4096]{1,0:T(8,128)}, f32[16,4096]{1,0:T(8,128)}) fusion(f32[16]{0:T(128)} %add_convert_fusion.1, f32[4096]{0:T(1024)S(1)} %bitcast.242), kind=kLoop, calls=%fused_computation.37 | loop fusion | flops 196608 | bytes 1065024 | tf_op jit(solution)/shard_map/cos | solution.py:113
  102.8 0.6 copy-done.43
  103.4 1.6 copy.39
  104.9 0.8 broadcast_in_dim.240
  105.7 1.0 fusion.26
  106.8 1.2 fusion.7
  108.2 0.5 copy-done.25
  108.8 11.4 %fusion.43 = f32[8,16,2,4096]{3,1,2,0:T(8,128)S(1)} fusion(f32[2,4096,256,1]{2,1,0,3:T(8,128)} %bitcast.234, f32[8,16,256]{2,1,0:T(8,128)S(1)} %constant_dynamic-update-slice_fusion), kind=kOutput, calls=%fused_computation.89 | convolution fusion | flops 3221225472 | bytes 12713984 | tf_op jit(solution)/shard_map/dot_general | solution.py:102
  120.2 8.9 %fusion.41 = f32[8,16,2,4096]{3,1,2,0:T(8,128)S(1)} fusion(f32[2,4096,256,1]{2,1,0,3:T(8,128)S(1)} %bitcast.237, f32[8,16,256]{2,1,0:T(8,128)S(1)} %get-tuple-element.36), kind=kOutput, calls=%fused_computation.87 | convolution fusion | flops 3221225472 | bytes 12713984 | tf_op jit(solution)/shard_map/dot_general | solution.py:102
  129.2 2.0 %subtract_reduce_fusion = (f32[8,4096]{1,0:T(8,128)S(1)}, f32[8,4096]{1,0:T(8,128)S(1)}, f32[8,4096]{1,0:T(8,128)S(1)}, f32[8,4096]{1,0:T(8,128)S(1)}) fusion(f32[8,16,2,4096]{3,1,2,0:T(8,128)S(1)} %fusion.41, f32[16,4096]{1,0:T(8,128)S(1)} %copy-done.23, f32[16,4096]{1,0:T(8,128)S(1)} %copy-done.21, f32[8,16,2,4096]{3,1,2,0:T(8,128)S(1)} %fusion.43, ...), kind=kLoop, calls=%fused_computation.8 | loop fusion | flops 8257536 | bytes 9961472 | tf_op jit(solution)/shard_map/reduce_sum | solution.py:115
  131.2 0.7 fusion.12
  131.9 56.2 %reduce-scatter.2.cloned.1.call-done = f32[256,16]{0,1:T(8,128)} async-done(((f32[4096,16]{0,1:T(8,128)}), f32[256,16]{0,1:T(8,128)}) %reduce-scatter.2.cloned.1.call-update) | async-done | bytes 16400 | tf_op jit(solution)/shard_map/reduce_scatter | solution.py:147
  (133 shorter events, 1.3 us)
Async XLA Ops:
  7.2 180.9 %reduce-scatter.2.cloned.1.call-start = ((), (), s32[]{:S(2)}) async-start(), calls=%async_computation.1 | async-start | bytes 278528 | tf_op jit(solution)/shard_map/reduce_scatter | solution.py:147
  8.3 47.8 %collective-permute-start = (f32[3,8,16]{2,1,0:T(8,128)S(1)}, f32[3,8,16]{2,1,0:T(8,128)S(1)}, u32[]{:S(2)}, u32[]{:S(2)}) collective-permute-start(f32[3,8,16]{2,1,0:T(8,128)S(1)} %bitcast.247), channel_id=1, source_target_pairs={{1,0},{2,1},{3,2},{5,4},{6,5},{7,6},{9,8},{10,9},{11,10},{13,12},{... | collective-permute-start | bytes 4616 | tf_op jit(solution)/shard_map/ppermute | solution.py:20
  10.6 46.4 %collective-permute-start.1 = (f32[3,8,256]{2,1,0:T(8,128)S(1)}, f32[3,8,256]{2,1,0:T(8,128)S(1)}, u32[]{:S(2)}, u32[]{:S(2)}) collective-permute-start(f32[3,8,256]{2,1,0:T(8,128)S(1)} %bitcast.244), channel_id=1, source_target_pairs={{4,0},{8,4},{12,8},{5,1},{9,5},{13,9},{6,2},{10,6},{14,10},{7,3},{... | collective-permute-start | bytes 73736 | tf_op jit(solution)/shard_map/ppermute | solution.py:20
  29.8 25.9 %copy-start = (f32[3,8,16,256]{3,2,1,0:T(8,128)S(1)}, f32[3,8,16,256]{3,2,1,0:T(8,128)}, u32[]{:S(2)}) copy-start(f32[3,8,16,256]{3,2,1,0:T(8,128)} %param.9) | copy-start | bytes 1179652
  33.7 23.3 %slice-start = ((f32[3,8,16,256]{3,2,1,0:T(8,128)}), f32[3,7,16,256]{3,2,1,0:T(8,128)S(1)}, s32[]{:S(2)}) async-start(f32[3,8,16,256]{3,2,1,0:T(8,128)} %param.9), calls=%async_computation.2 | async-start | bytes 688128 | tf_op jit(solution)/shard_map/slice | solution.py:45
  33.7 24.4 %copy-start.3 = (f32[3,8,16,256]{3,2,1,0:T(8,128)S(1)}, f32[3,8,16,256]{3,2,1,0:T(8,128)}, u32[]{:S(2)}) copy-start(f32[3,8,16,256]{3,2,1,0:T(8,128)} %param.10) | copy-start | bytes 1179652
  44.3 11.5 %copy-start.26 = (pred[8,16,256]{2,1,0:T(8,128)(4,1)}, pred[8,16,256]{2,1,0:T(8,128)(4,1)S(1)}, u32[]{:S(2)}) copy-start(pred[8,16,256]{2,1,0:T(8,128)(4,1)S(1)} %get-tuple-element.8) | copy-start | bytes 98308
  44.3 11.5 %copy-start.27 = (pred[8,16,256]{2,1,0:T(8,128)(4,1)}, pred[8,16,256]{2,1,0:T(8,128)(4,1)S(1)}, u32[]{:S(2)}) copy-start(pred[8,16,256]{2,1,0:T(8,128)(4,1)S(1)} %get-tuple-element.9) | copy-start | bytes 98308
  44.3 11.5 %copy-start.28 = (pred[8,16,256]{2,1,0:T(8,128)(4,1)}, pred[8,16,256]{2,1,0:T(8,128)(4,1)S(1)}, u32[]{:S(2)}) copy-start(pred[8,16,256]{2,1,0:T(8,128)(4,1)S(1)} %get-tuple-element.10) | copy-start | bytes 98308
  44.3 11.5 %copy-start.29 = (pred[8,16,256]{2,1,0:T(8,128)(4,1)}, pred[8,16,256]{2,1,0:T(8,128)(4,1)S(1)}, u32[]{:S(2)}) copy-start(pred[8,16,256]{2,1,0:T(8,128)(4,1)S(1)} %get-tuple-element.11) | copy-start | bytes 98308
  44.4 11.5 %copy-start.30 = (pred[8,16,256]{2,1,0:T(8,128)(4,1)}, pred[8,16,256]{2,1,0:T(8,128)(4,1)S(1)}, u32[]{:S(2)}) copy-start(pred[8,16,256]{2,1,0:T(8,128)(4,1)S(1)} %get-tuple-element.12) | copy-start | bytes 98308
  44.4 11.5 %copy-start.31 = (pred[8,16,256]{2,1,0:T(8,128)(4,1)}, pred[8,16,256]{2,1,0:T(8,128)(4,1)S(1)}, u32[]{:S(2)}) copy-start(pred[8,16,256]{2,1,0:T(8,128)(4,1)S(1)} %get-tuple-element.13) | copy-start | bytes 98308
  44.4 11.5 %copy-start.32 = (pred[8,16,256]{2,1,0:T(8,128)(4,1)}, pred[8,16,256]{2,1,0:T(8,128)(4,1)S(1)}, u32[]{:S(2)}) copy-start(pred[8,16,256]{2,1,0:T(8,128)(4,1)S(1)} %get-tuple-element.14) | copy-start | bytes 98308
  44.4 11.5 %copy-start.33 = (pred[8,16,256]{2,1,0:T(8,128)(4,1)}, pred[8,16,256]{2,1,0:T(8,128)(4,1)S(1)}, u32[]{:S(2)}) copy-start(pred[8,16,256]{2,1,0:T(8,128)(4,1)S(1)} %get-tuple-element.15) | copy-start | bytes 98308
  44.4 11.5 %copy-start.34 = (pred[8,16,256]{2,1,0:T(8,128)(4,1)}, pred[8,16,256]{2,1,0:T(8,128)(4,1)S(1)}, u32[]{:S(2)}) copy-start(pred[8,16,256]{2,1,0:T(8,128)(4,1)S(1)} %get-tuple-element.16) | copy-start | bytes 98308
  44.4 11.5 %copy-start.35 = (pred[8,16,256]{2,1,0:T(8,128)(4,1)}, pred[8,16,256]{2,1,0:T(8,128)(4,1)S(1)}, u32[]{:S(2)}) copy-start(pred[8,16,256]{2,1,0:T(8,128)(4,1)S(1)} %get-tuple-element.17) | copy-start | bytes 98308
  44.4 11.5 %copy-start.36 = (pred[8,16,256]{2,1,0:T(8,128)(4,1)}, pred[8,16,256]{2,1,0:T(8,128)(4,1)S(1)}, u32[]{:S(2)}) copy-start(pred[8,16,256]{2,1,0:T(8,128)(4,1)S(1)} %get-tuple-element.18) | copy-start | bytes 98308
  44.4 11.5 %copy-start.37 = (pred[8,16,256]{2,1,0:T(8,128)(4,1)}, pred[8,16,256]{2,1,0:T(8,128)(4,1)S(1)}, u32[]{:S(2)}) copy-start(pred[8,16,256]{2,1,0:T(8,128)(4,1)S(1)} %get-tuple-element.19) | copy-start | bytes 98308
  44.4 11.5 %copy-start.38 = (pred[8,16,256]{2,1,0:T(8,128)(4,1)}, pred[8,16,256]{2,1,0:T(8,128)(4,1)S(1)}, u32[]{:S(2)}) copy-start(pred[8,16,256]{2,1,0:T(8,128)(4,1)S(1)} %get-tuple-element.20) | copy-start | bytes 98308
  44.4 11.5 %copy-start.39 = (pred[8,16,256]{2,1,0:T(8,128)(4,1)}, pred[8,16,256]{2,1,0:T(8,128)(4,1)S(1)}, u32[]{:S(2)}) copy-start(pred[8,16,256]{2,1,0:T(8,128)(4,1)S(1)} %get-tuple-element.21) | copy-start | bytes 98308
  44.5 11.5 %copy-start.40 = (pred[8,16,256]{2,1,0:T(8,128)(4,1)}, pred[8,16,256]{2,1,0:T(8,128)(4,1)S(1)}, u32[]{:S(2)}) copy-start(pred[8,16,256]{2,1,0:T(8,128)(4,1)S(1)} %get-tuple-element.22) | copy-start | bytes 98308
  44.5 11.5 %copy-start.41 = (pred[8,16,256]{2,1,0:T(8,128)(4,1)}, pred[8,16,256]{2,1,0:T(8,128)(4,1)S(1)}, u32[]{:S(2)}) copy-start(pred[8,16,256]{2,1,0:T(8,128)(4,1)S(1)} %get-tuple-element.23) | copy-start | bytes 98308
  44.5 34.3 %copy-start.6 = (f32[8,16,256]{2,1,0:T(8,128)}, f32[8,16,256]{2,1,0:T(8,128)S(1)}, u32[]{:S(2)}) copy-start(f32[8,16,256]{2,1,0:T(8,128)S(1)} %get-tuple-element.7) | copy-start | bytes 393220
  55.0 23.8 %copy-start.17 = (f32[8,16,256]{2,1,0:T(8,128)}, f32[8,16,256]{2,1,0:T(8,128)S(1)}, u32[]{:S(2)}) copy-start(f32[8,16,256]{2,1,0:T(8,128)S(1)} %select_select_fusion.1) | copy-start | bytes 393220
  56.1 22.7 %copy-start.4 = (f32[3,8,16,256]{3,2,1,0:T(8,128)S(1)}, f32[3,8,16,256]{3,2,1,0:T(8,128)}, u32[]{:S(2)}) copy-start(f32[3,8,16,256]{3,2,1,0:T(8,128)} %param.11) | copy-start | bytes 1179652
  56.1 22.7 %copy-start.5 = (f32[3,8,16,256]{3,2,1,0:T(8,128)S(1)}, f32[3,8,16,256]{3,2,1,0:T(8,128)}, u32[]{:S(2)}) copy-start(f32[3,8,16,256]{3,2,1,0:T(8,128)} %param.12) | copy-start | bytes 1179652
  58.0 20.2 %copy-start.8 = (f32[1,8,16,256]{3,2,1,0:T(8,128)}, f32[1,8,16,256]{3,2,1,0:T(8,128)S(1)}, u32[]{:S(2)}) copy-start(f32[1,8,16,256]{3,2,1,0:T(8,128)S(1)} %get-tuple-element.33) | copy-start | bytes 393220
  58.1 20.2 %copy-start.9 = (f32[1,8,16,256]{3,2,1,0:T(8,128)}, f32[1,8,16,256]{3,2,1,0:T(8,128)S(1)}, u32[]{:S(2)}) copy-start(f32[1,8,16,256]{3,2,1,0:T(8,128)S(1)} %get-tuple-element.34) | copy-start | bytes 393220
  58.1 20.2 %copy-start.10 = (f32[1,8,16,256]{3,2,1,0:T(8,128)}, f32[1,8,16,256]{3,2,1,0:T(8,128)S(1)}, u32[]{:S(2)}) copy-start(f32[1,8,16,256]{3,2,1,0:T(8,128)S(1)} %get-tuple-element.35) | copy-start | bytes 393220
  58.4 19.9 %collective-permute-start.2 = (f32[3,8,16]{2,1,0:T(8,128)S(1)}, f32[3,8,16]{2,1,0:T(8,128)S(1)}, u32[]{:S(2)}, u32[]{:S(2)}) collective-permute-start(f32[3,8,16]{2,1,0:T(8,128)S(1)} %slice_reduce_fusion.2), channel_id=1, source_target_pairs={{0,1},{1,2},{2,3},{4,5},{5,6},{6,7},{8,9},{9,10},{10,11},{12,13},{... | collective-permute-start | bytes 4616 | tf_op jit(solution)/shard_map/ppermute | solution.py:20
  61.5 17.0 %collective-permute-start.3 = (f32[3,8,256]{2,1,0:T(8,128)S(1)}, f32[3,8,256]{2,1,0:T(8,128)S(1)}, u32[]{:S(2)}, u32[]{:S(2)}) collective-permute-start(f32[3,8,256]{2,1,0:T(8,128)S(1)} %bitcast.245), channel_id=1, source_target_pairs={{0,4},{4,8},{8,12},{1,5},{5,9},{9,13},{2,6},{6,10},{10,14},{3,7},{... | collective-permute-start | bytes 73736 | tf_op jit(solution)/shard_map/ppermute | solution.py:20
  80.2 4.2 %collective-permute-start.4 = (f32[3,8,16]{2,1,0:T(8,128)S(1)}, f32[3,8,16]{2,1,0:T(8,128)S(1)}, u32[]{:S(2)}, u32[]{:S(2)}) collective-permute-start(f32[3,8,16]{2,1,0:T(8,128)S(1)} %slice_reduce_fusion.1), channel_id=1, source_target_pairs={{1,0},{2,1},{3,2},{5,4},{6,5},{7,6},{9,8},{10,9},{11,10},{13,12},{... | collective-permute-start | bytes 4616 | tf_op jit(solution)/shard_map/ppermute | solution.py:20
  82.3 6.0 %collective-permute-start.5 = (f32[3,8,256]{2,1,0:T(8,128)}, f32[3,8,256]{2,1,0:T(8,128)}, u32[]{:S(2)}, u32[]{:S(2)}) collective-permute-start(f32[3,8,256]{2,1,0:T(8,128)} %bitcast.223), channel_id=1, source_target_pairs={{4,0},{8,4},{12,8},{5,1},{9,5},{13,9},{6,2},{10,6},{14,10},{7,3},{... | collective-permute-start | bytes 73736 | tf_op jit(solution)/shard_map/ppermute | solution.py:20
  90.1 16.6 %copy-start.7 = (f32[8,16,256]{2,1,0:T(8,128)S(1)}, f32[8,16,256]{2,1,0:T(8,128)}, u32[]{:S(2)}) copy-start(f32[8,16,256]{2,1,0:T(8,128)} %copy-done.6) | copy-start | bytes 393220
  90.1 16.6 %copy-start.12 = (f32[1,8,16,256]{3,2,1,0:T(8,128)S(1)}, f32[1,8,16,256]{3,2,1,0:T(8,128)}, u32[]{:S(2)}) copy-start(f32[1,8,16,256]{3,2,1,0:T(8,128)} %copy-done.11) | copy-start | bytes 393220
  90.1 16.6 %copy-start.14 = (f32[1,8,16,256]{3,2,1,0:T(8,128)S(1)}, f32[1,8,16,256]{3,2,1,0:T(8,128)}, u32[]{:S(2)}) copy-start(f32[1,8,16,256]{3,2,1,0:T(8,128)} %copy-done.13) | copy-start | bytes 393220
  90.1 17.9 %copy-start.2 = (s32[2,16,256]{2,1,0:T(8,128)S(1)}, s32[2,16,256]{2,1,0:T(8,128)}, u32[]{:S(2)}) copy-start(s32[2,16,256]{2,1,0:T(8,128)} %param.15) | copy-start | bytes 98308
  91.3 28.8 %copy-start.1 = (f32[3,8,16,256]{3,2,1,0:T(8,128)}, f32[3,8,16,256]{3,2,1,0:T(8,128)S(1)}, u32[]{:S(2)}) copy-start(f32[3,8,16,256]{3,2,1,0:T(8,128)S(1)} %fusion.4) | copy-start | bytes 1179652
  91.3 15.4 %copy-start.16 = (f32[1,8,16,256]{3,2,1,0:T(8,128)S(1)}, f32[1,8,16,256]{3,2,1,0:T(8,128)}, u32[]{:S(2)}) copy-start(f32[1,8,16,256]{3,2,1,0:T(8,128)} %copy-done.15) | copy-start | bytes 393220
  91.4 15.4 %copy-start.18 = (f32[8,16,256]{2,1,0:T(8,128)S(1)}, f32[8,16,256]{2,1,0:T(8,128)}, u32[]{:S(2)}) copy-start(f32[8,16,256]{2,1,0:T(8,128)} %copy-done.17) | copy-start | bytes 393220
  91.4 15.4 %copy-start.20 = (f32[8,16,256]{2,1,0:T(8,128)S(1)}, f32[8,16,256]{2,1,0:T(8,128)}, u32[]{:S(2)}) copy-start(f32[8,16,256]{2,1,0:T(8,128)} %copy-done.19) | copy-start | bytes 393220
  91.6 11.1 %collective-permute-start.6 = (f32[3,8,16]{2,1,0:T(8,128)S(1)}, f32[3,8,16]{2,1,0:T(8,128)S(1)}, u32[]{:S(2)}, u32[]{:S(2)}) collective-permute-start(f32[3,8,16]{2,1,0:T(8,128)S(1)} %slice_reduce_fusion), channel_id=1, source_target_pairs={{0,1},{1,2},{2,3},{4,5},{5,6},{6,7},{8,9},{9,10},{10,11},{12,13},{... | collective-permute-start | bytes 4616 | tf_op jit(solution)/shard_map/ppermute | solution.py:20
  95.0 9.9 %collective-permute-start.7 = (f32[3,8,256]{2,1,0:T(8,128)}, f32[3,8,256]{2,1,0:T(8,128)}, u32[]{:S(2)}, u32[]{:S(2)}) collective-permute-start(f32[3,8,256]{2,1,0:T(8,128)} %bitcast.222), channel_id=1, source_target_pairs={{0,4},{4,8},{8,12},{1,5},{5,9},{9,13},{2,6},{6,10},{10,14},{3,7},{... | collective-permute-start | bytes 73736 | tf_op jit(solution)/shard_map/ppermute | solution.py:20
  108.1 12.1 %slice-start.1 = ((s8[8388608]{0:T(1024)(128)(4,1)}), s8[4194304]{0:T(1024)(128)(4,1)S(1)}, s32[]{:S(2)}) async-start(s8[8388608]{0:T(1024)(128)(4,1)} %bitcast.235), calls=%async_computation.3 | async-start | bytes 8388608
  108.8 11.4 %slice-start.2 = ((s8[8388608]{0:T(1024)(128)(4,1)}), s8[4194304]{0:T(1024)(128)(4,1)S(1)}, s32[]{:S(2)}) async-start(s8[8388608]{0:T(1024)(128)(4,1)} %bitcast.235), calls=%async_computation.4 | async-start | bytes 8388608
  120.2 9.0 %copy-start.21 = (f32[16,4096]{1,0:T(8,128)S(1)}, f32[16,4096]{1,0:T(8,128)}, u32[]{:S(2)}) copy-start(f32[16,4096]{1,0:T(8,128)} %get-tuple-element.48) | copy-start | bytes 786436
  120.2 9.0 %copy-start.22 = (f32[16,4096]{1,0:T(8,128)S(1)}, f32[16,4096]{1,0:T(8,128)}, u32[]{:S(2)}) copy-start(f32[16,4096]{1,0:T(8,128)} %get-tuple-element.49) | copy-start | bytes 786436
  120.2 9.0 %copy-start.23 = (f32[16,4096]{1,0:T(8,128)S(1)}, f32[16,4096]{1,0:T(8,128)}, u32[]{:S(2)}) copy-start(f32[16,4096]{1,0:T(8,128)} %get-tuple-element.50) | copy-start | bytes 786436
  (9 other events, 35.4 us)
Sparse Core Ops, SparseCore 0:
  132.1 56.0 reduce-scatter.1
where the time goes:
time: 196 us; the launch traced here: 195 us
  other arithmetic  66.2 us (34%)
  waiting for transfers between devices  57.9 us (30%)
  starting transfers between devices  21 us (11%)
  matrix products  20.3 us (10%)
  between operations  15.2 us (8%)
  local copies, waits for them, and re-layouts  14.3 us (7%)
    reduce_scatter x1, waiting for transfers between devices, local(): lax.psum_scatter(terms(jnp.int32(0), lax.axis_size(('gx', 'gy')) * owned)...  56.2 us
    ppermute x8, starting transfers between devices, from_behind(): return lax.ppermute(array, axis, pairs)  21 us
    dot_general x2, matrix products, project(): lax.dot_general(plane.reshape(8 * width_x, width_y), table_y, (((1,), (1,...  20.3 us
    cos x1, other arithmetic, project(): table_y = jnp.concatenate([jnp.cos(angle_y), jnp.sin(angle_y)], axis=0)  14.7 us
    select_n x1, other arithmetic, pole_table(): coef_c = jnp.where(selected, table_c[number], coef_c)  11.2 us
    select_n x1, other arithmetic, pole_table(): coef_a = jnp.where(selected, table_a[number], coef_a)  10.6 us
    select_n x1, other arithmetic, pole_table(): coef_b = jnp.where(selected, table_b[number], coef_b)  10.5 us
  transfers between devices with their start and end apart: 9, of which 2 were waited for; matrix products, arithmetic and copies ran while one was open for 34% of the time, Pallas kernels for 0%

commit v1 on v0

v1 whole, which is shorter than its diff:
```python
from functools import partial
import math

import jax
import jax.numpy as jnp
from jax import lax
from jax.experimental import pallas as pl
from jax.experimental.pallas import tpu as pltpu
from jax.sharding import PartitionSpec as P

COURANT = 0.5
WAVE = 0.3
OMEGA = 0.25
LANES = 128
ITEMS = 10
VMEM = pltpu.CompilerParams(vmem_limit_bytes=24 * 1024 * 1024)


def lane_index(shape):
    return lax.broadcasted_iota(jnp.int32, shape, len(shape) - 1)


def row_index(shape):
    return lax.broadcasted_iota(jnp.int32, shape, 0)


def sincos(angle):
    turns = jnp.round(angle * (0.5 / math.pi))
    rest = angle - turns * 6.28125
    rest = rest - turns * 0.0019350051879882812
    rest = rest - turns * 3.0199159819567e-07
    half = 0.5 * rest
    sq = half * half
    sin_half = 1.0 / 6227020800.0
    for term in (-1.0 / 39916800.0, 1.0 / 362880.0, -1.0 / 5040.0, 1.0 / 120.0, -1.0 / 6.0, 1.0):
        sin_half = sin_half * sq + term
    sin_half = sin_half * half
    cos_half = -1.0 / 87178291200.0
    for term in (1.0 / 479001600.0, -1.0 / 3628800.0, 1.0 / 40320.0, -1.0 / 720.0, 1.0 / 24.0, -0.5, 1.0):
        cos_half = cos_half * sq + term
    return 2.0 * sin_half * cos_half, 1.0 - 2.0 * sin_half * sin_half


def prepare_body(e_ref, h_ref, p_ref, q_ref, eps_ref, mat_ref, poles_ref, one_ref, two_ref, d_ref, g_ref, k_ref, table_ref):
    levels, rows, width = eps_ref.shape
    last = width - LANES
    table_ref[0:3, 0 : poles_ref.shape[1]] = poles_ref[...]
    omega_dt, gamma_dt, strength = (table_ref[i : i + 1, :] for i in range(3))
    denominator = 1.0 + 0.5 * gamma_dt
    tile = (rows, LANES)
    table_a = jnp.broadcast_to((2.0 - omega_dt * omega_dt) / denominator, tile)
    table_b = jnp.broadcast_to(-(1.0 - 0.5 * gamma_dt) / denominator, tile)
    table_c = jnp.broadcast_to(strength * omega_dt * omega_dt / denominator, tile)
    lane = lane_index(tile)
    even = lax.rem(lax.axis_index("gy"), 2) == 0
    for z in range(levels):
        up = jnp.zeros(tile, jnp.float32)
        down = jnp.zeros(tile, jnp.float32)
        for start in range(0, width, LANES):
            cut = slice(start, start + LANES)
            number = mat_ref[z, :, cut]
            a = jnp.take_along_axis(table_a, number, axis=1)
            b = jnp.take_along_axis(table_b, number, axis=1)
            c = jnp.take_along_axis(table_c, number, axis=1)
            inv = 1.0 / eps_ref[z, :, cut]
            half = COURANT * inv
            k_ref[0, z, :, cut] = half
            k_ref[1, z, :, cut] = 1.0 - c * inv
            items = [e_ref[i, z, :, cut] for i in range(3)] + [h_ref[i, z, :, cut] for i in range(3)]
            for i in range(3):
                now, old = p_ref[i, z, :, cut], q_ref[i, z, :, cut]
                new = a * now + b * old + c * items[i]
                local = items[i] - (new - now) * inv
                d_ref[i, z, :, cut] = local
                g_ref[i, z, :, cut] = ((a * new - new) + b * now) * inv
                items.append(local)
            items.append(half)
            for k, item in enumerate(items):
                if start == 0:
                    moved = pltpu.roll(item, 2 * k, 1) if k else item
                    down = jnp.where((lane >= 2 * k) & (lane < 2 * k + 2), moved, down)
                if start == last:
                    moved = pltpu.roll(item, LANES - 2 * k, 1) if k else item
                    up = jnp.where((lane >= LANES - 2 - 2 * k) & (lane < LANES - 2 * k), moved, up)
        one_ref[z] = jnp.where(even, up, down)
        two_ref[z] = jnp.where(even, down, up)


def prepare(e_field, h_field, pol_now, pol_old, eps_inf, materials, poles):
    levels, rows, width = eps_inf.shape
    message = jax.ShapeDtypeStruct((levels, rows, LANES), jnp.float32)
    field = jax.ShapeDtypeStruct(e_field.shape, jnp.float32)
    pair = jax.ShapeDtypeStruct((2, levels, rows, width), jnp.float32)
    return pl.pallas_call(
        prepare_body,
        out_shape=(message, message, field, field, pair),
        scratch_shapes=[pltpu.VMEM((8, LANES), jnp.float32)],
        compiler_params=VMEM,
        name="prepare",
    )(e_field, h_field, pol_now, pol_old, eps_inf, materials, poles)


def read_wide(own_ref, index, z, messages, item):
    before, after = messages
    lane = lane_index(before[z].shape)
    shift = 2 * item
    late = pltpu.roll(after[z], LANES - shift, 1) if item else after[z]
    early = pltpu.roll(before[z], shift, 1) if item else before[z]
    halo = jnp.where(lane < 2, late, jnp.where(lane >= LANES - 2, early, 0.0))
    return jnp.concatenate([own_ref[index, z], halo], axis=1)


def y_messages(one_ref, two_ref):
    place = lax.axis_index("gy")
    count = lax.axis_size("gy")
    even = lax.rem(place, 2) == 0
    before, after = [], []
    for z in range(one_ref.shape[0]):
        one, two = one_ref[z], two_ref[z]
        before.append(jnp.where(place > 0, jnp.where(even, two, one), 0.0))
        after.append(jnp.where(place < count - 1, jnp.where(even, one, two), 0.0))
    return before, after


def ahead_y(v):
    return pltpu.roll(v, v.shape[1] - 1, 1)


def behind_y(v):
    return pltpu.roll(v, 1, 1)


def ahead_x(v, row):
    at = row_index(v.shape)
    return jnp.where(at == v.shape[0] - 1, row, pltpu.roll(v, v.shape[0] - 1, 0))


def behind_x(v, row):
    at = row_index(v.shape)
    return jnp.where(at == 0, row, pltpu.roll(v, 1, 0))


def magnetic(e_here, e_above, h_here, row_y, row_z, keep):
    ex, ey, ez = e_here
    hx, hy, hz = h_here
    up_x, up_y = e_above
    hx = hx - COURANT * ((ahead_y(ez) - ez) - (up_y - ey))
    hy = hy - COURANT * ((up_x - ex) - (ahead_x(ez, row_z) - ez))
    hz = hz - COURANT * ((ahead_x(ey, row_y) - ey) - (ahead_y(ex) - ex))
    return [jnp.where(keep, v, 0.0) for v in (hx, hy, hz)]


def curl_back(h_here, h_below, row_y, row_z):
    hx, hy, hz = h_here
    low_x, low_y = h_below
    return (
        (hz - behind_y(hz)) - (hy - low_y),
        (hx - low_x) - (hz - behind_x(hz, row_z)),
        (hy - behind_x(hy, row_y)) - (hx - behind_y(hx)),
    )


def kept_lanes(shape, width):
    return (lane_index(shape) < width + LANES // 2) | (lax.axis_index("gy") > 0)


def first_body(e_ref, h_ref, d_ref, k_ref, one_ref, two_ref, out_one_ref, out_two_ref, h1_ref, e1_ref, e0_ref):
    levels, rows, width = one_ref.shape[0], one_ref.shape[1], e_ref.shape[3]
    wide = (rows, width + LANES)
    messages = y_messages(one_ref, two_ref)
    keep = kept_lanes(wide, width)
    zero_row = jnp.zeros((1, wide[1]), jnp.float32)
    zero = jnp.zeros(wide, jnp.float32)
    for z in range(levels):
        for i in range(3):
            e0_ref[i, z] = read_wide(e_ref, i, z, messages, i)
    for z in range(levels):
        above = [e0_ref[i, z + 1] for i in range(2)] if z + 1 < levels else [zero, zero]
        h_here = [read_wide(h_ref, i, z, messages, 3 + i) for i in range(3)]
        new = magnetic([e0_ref[i, z] for i in range(3)], above, h_here, zero_row, zero_row, keep)
        for i in range(3):
            h1_ref[i, z] = new[i]
    inv = []
    for z in range(levels):
        below = [h1_ref[i, z - 1] for i in range(2)] if z else [zero, zero]
        curl = curl_back([h1_ref[i, z] for i in range(3)], below, zero_row, zero_row)
        inv.append(read_wide(k_ref, 0, z, messages, 9))
        for i in range(3):
            e1_ref[i, z] = read_wide(d_ref, i, z, messages, 6 + i) + inv[z] * curl[i]
    even = lax.rem(lax.axis_index("gx"), 2) == 0
    keep_row = kept_lanes((1, wide[1]), width)
    end = slice(rows - 1, rows)
    for z in range(levels):
        hy, hz = h1_ref[1, z, end], h1_ref[2, z, end]
        ex, ey, ez = (e1_ref[i, z, end] for i in range(3))
        up_x = e1_ref[0, z + 1, end] if z + 1 < levels else zero_row
        second_y = hy - COURANT * ((up_x - ex) + ez)
        second_z = hz - COURANT * (-ey - (ahead_y(ex) - ex))
        up = [hy, hz, jnp.where(keep_row, second_y, 0.0), jnp.where(keep_row, second_z, 0.0), inv[z][end]]
        down = [e0_ref[1, z, 0:1], e0_ref[2, z, 0:1], e1_ref[1, z, 0:1], e1_ref[2, z, 0:1], inv[z][0:1]]
        for k in range(5):
            out_one_ref[k, z : z + 1] = jnp.where(even, up[k], down[k])
            out_two_ref[k, z : z + 1] = jnp.where(even, down[k], up[k])


def first_step(e_field, h_field, local, factors, one, two):
    _, levels, rows, width = e_field.shape
    message = jax.ShapeDtypeStruct((5, levels, width + LANES), jnp.float32)
    store = pltpu.VMEM((3, levels, rows, width + LANES), jnp.float32)
    return pl.pallas_call(
        first_body,
        out_shape=(message, message),
        scratch_shapes=[store, store, store],
        compiler_params=VMEM,
        name="first_step",
    )(e_field, h_field, local, factors, one, two)


def both_body(e_ref, h_ref, d_ref, g_ref, k_ref, surface_ref, one_ref, two_ref, x_one_ref, x_two_ref,
              e_out, h_out, ev_ref, ev_low_ref, od_ref, od_low_ref, e0_ref, h1_ref, e1_ref, h2_ref, plane_ref):
    levels, rows, width = one_ref.shape[0], one_ref.shape[1], e_ref.shape[3]
    wide = (rows, width + LANES)
    messages = y_messages(one_ref, two_ref)
    keep = kept_lanes(wide, width)
    keep_row = kept_lanes((1, wide[1]), width)
    zero_row = jnp.zeros((1, wide[1]), jnp.float32)
    zero = jnp.zeros(wide, jnp.float32)
    place, count = lax.axis_index("gx"), lax.axis_size("gx")
    even = lax.rem(place, 2) == 0
    has_before, has_after = place > 0, place < count - 1

    def from_before(k, z):
        got = jnp.where(even, x_two_ref[k, z : z + 1], x_one_ref[k, z : z + 1])
        return jnp.where(has_before, got, 0.0)

    def from_after(k, z):
        got = jnp.where(even, x_one_ref[k, z : z + 1], x_two_ref[k, z : z + 1])
        return jnp.where(has_after, got, 0.0)

    def store_plane(number, layer, part, value):
        at = ((number * 2 + layer) * 4 + part) * rows
        weighted = value[:, :width] * surface_ref[layer].astype(jnp.float32)
        plane_ref[0, at : at + rows] = weighted[:, : width // 2]
        plane_ref[1, at : at + rows] = weighted[:, width // 2 :]

    def layer_of(z):
        return {0: 0, levels - 1: 1}.get(z)

    for z in range(levels):
        for i in range(3):
            e0_ref[i, z] = read_wide(e_ref, i, z, messages, i)
    for z in range(levels):
        above = [e0_ref[i, z + 1] for i in range(2)] if z + 1 < levels else [zero, zero]
        h_here = [read_wide(h_ref, i, z, messages, 3 + i) for i in range(3)]
        new = magnetic(
            [e0_ref[i, z] for i in range(3)], above, h_here, from_after(0, z), from_after(1, z), keep
        )
        for i in range(3):
            h1_ref[i, z] = new[i]
        if layer_of(z) is not None:
            for i in range(2):
                store_plane(0, layer_of(z), 2 + i, new[i])

    first = slice(0, 1)
    end = slice(rows - 1, rows)
    diff_y = [jnp.where(has_before, COURANT * e0_ref[2, z, first], 0.0) for z in range(levels)]
    diff_z = [jnp.where(has_before, -COURANT * e0_ref[1, z, first], 0.0) for z in range(levels)]
    for z in range(levels):
        below = [h1_ref[i, z - 1] for i in range(2)] if z else [zero, zero]
        row_y = from_before(0, z) + diff_y[z]
        row_z = from_before(1, z) + diff_z[z]
        curl = curl_back([h1_ref[i, z] for i in range(3)], below, row_y, row_z)
        inv = read_wide(k_ref, 0, z, messages, 9)
        for i in range(3):
            new = read_wide(d_ref, i, z, messages, 6 + i) + inv * curl[i]
            e1_ref[i, z] = new
            if i < 2 and layer_of(z) is not None:
                store_plane(0, layer_of(z), i, new)

    for z in range(levels):
        above = [e1_ref[i, z + 1] for i in range(2)] if z + 1 < levels else [zero, zero]
        inv = from_after(4, z)
        row_y = from_after(2, z) + inv * h1_ref[2, z, end]
        row_z = from_after(3, z) - inv * h1_ref[1, z, end]
        new = magnetic(
            [e1_ref[i, z] for i in range(3)], above, [h1_ref[i, z] for i in range(3)], row_y, row_z, keep
        )
        for i in range(3):
            h2_ref[i, z] = new[i]
            h_out[i, z] = new[i][:, :width]
        if layer_of(z) is not None:
            for i in range(2):
                store_plane(1, layer_of(z), 2 + i, new[i])

    inv_before = [from_before(4, z) for z in range(levels)]
    diff_ex = []
    for z in range(levels):
        low = diff_y[z - 1] if z else zero_row
        diff_ex.append(inv_before[z] * ((diff_z[z] - behind_y(diff_z[z])) - (diff_y[z] - low)))
    for z in range(levels):
        below = [h2_ref[i, z - 1] for i in range(2)] if z else [zero, zero]
        up = diff_ex[z + 1] if z + 1 < levels else zero_row
        diff_ey = -inv_before[z] * diff_z[z]
        diff_ez = inv_before[z] * diff_y[z]
        row_y = from_before(2, z) + diff_y[z] - COURANT * ((up - diff_ex[z]) - (e1_ref[2, z, first] - diff_ez))
        row_z = from_before(3, z) + diff_z[z] - COURANT * (
            (e1_ref[1, z, first] - diff_ey) - (ahead_y(diff_ex[z]) - diff_ex[z])
        )
        open_row = keep_row & has_before
        row_y = jnp.where(open_row, row_y, 0.0)
        row_z = jnp.where(open_row, row_z, 0.0)
        curl = curl_back([h2_ref[i, z] for i in range(3)], below, row_y, row_z)
        for i in range(3):
            new = k_ref[1, z] * e1_ref[i, z, :, :width] + k_ref[0, z] * curl[i][:, :width] - g_ref[i, z]
            e_out[i, z] = new
            if i < 2 and layer_of(z) is not None:
                store_plane(1, layer_of(z), i, new)

    kinds = 16
    half = width // 2
    back = half - 1 - lane_index((kinds, half))
    for v in range(rows // 2):
        high = [plane_ref[side, pl.ds(rows // 2 + v, kinds, stride=rows), :] for side in range(2)]
        low = [plane_ref[side, pl.ds(rows // 2 - 1 - v, kinds, stride=rows), :] for side in range(2)]
        for parity in range(2):
            left, right = (b - a if parity else b + a for a, b in zip(low, high))
            left = jnp.take_along_axis(left, back, axis=1)
            at = slice((2 * v + parity) * kinds, (2 * v + parity + 1) * kinds)
            for value, ref, low_ref in ((right + left, ev_ref, ev_low_ref), (right - left, od_ref, od_low_ref)):
                top = value.astype(jnp.bfloat16)
                ref[at, :half] = top
                ref[at, half:] = top
                low_ref[at] = (value - top.astype(jnp.float32)).astype(jnp.bfloat16)


def both_steps(e_field, h_field, local, late, factors, surface, one, two, x_one, x_two):
    _, levels, rows, width = e_field.shape
    field = jax.ShapeDtypeStruct(e_field.shape, jnp.float32)
    full = jax.ShapeDtypeStruct((16 * rows, width), jnp.bfloat16)
    part = jax.ShapeDtypeStruct((16 * rows, width // 2), jnp.bfloat16)
    store = pltpu.VMEM((3, levels, rows, width + LANES), jnp.float32)
    return pl.pallas_call(
        both_body,
        out_shape=(field, field, full, part, full, part),
        scratch_shapes=[store, store, store, store, pltpu.VMEM((2, 16 * rows, width // 2), jnp.float32)],
        compiler_params=VMEM,
        name="both_steps",
    )(e_field, h_field, local, late, factors, surface, one, two, x_one, x_two)


def table_body(waves_ref, cos_ref, sin_ref, phase_ref, *, rows, width, scale):
    count = waves_ref.shape[1]
    half = width // 2
    wave_x, wave_y = WAVE * waves_ref[0:1, :], WAVE * waves_ref[1:2, :]
    step = (row_index((8, count)).astype(jnp.float32)) + 0.5
    sin_x, cos_x = sincos(wave_x * step)
    phase_ref[0:8] = cos_x
    phase_ref[8:16] = sin_x
    centre_x = (lax.axis_index("gx") * rows).astype(jnp.float32) + 0.5 * (rows - 1)
    centre_y = (lax.axis_index("gy") * width).astype(jnp.float32) + 0.5 * (width - 1)
    sin_c, cos_c = sincos(wave_x * centre_x + wave_y * centre_y)
    phase_ref[16:24] = jnp.broadcast_to(scale * cos_c, (8, count))
    phase_ref[24:32] = jnp.broadcast_to(scale * sin_c, (8, count))
    sin_y, cos_y = sincos(wave_y * step)
    sin_w, cos_w = sincos(wave_y * 8.0)
    cos_y = jnp.concatenate([cos_y, cos_y * cos_w - sin_y * sin_w], axis=0)
    sin_y = jnp.concatenate([sin_y, sin_y * cos_w + cos_y[0:8] * sin_w], axis=0)
    sin_w, cos_w = 2.0 * sin_w * cos_w, 1.0 - 2.0 * sin_w * sin_w
    for start in range(0, half, 16):
        if start:
            cos_y, sin_y = cos_y * cos_w - sin_y * sin_w, sin_y * cos_w + cos_y * sin_w
        for value, ref in ((cos_y, cos_ref), (sin_y, sin_ref)):
            top = value.astype(jnp.bfloat16)
            ref[start : start + 16] = top
            ref[half + start : half + start + 16] = (value - top.astype(jnp.float32)).astype(jnp.bfloat16)


def tables(waves, rows, width, scale):
    count = waves.shape[1]
    chunk = 256
    table = jax.ShapeDtypeStruct((width, count), jnp.bfloat16)
    block = pl.BlockSpec((width, chunk), lambda i: (0, i))
    return pl.pallas_call(
        partial(table_body, rows=rows, width=width, scale=scale),
        grid=(count // chunk,),
        out_shape=(table, table, jax.ShapeDtypeStruct((32, count), jnp.float32)),
        in_specs=[pl.BlockSpec((2, chunk), lambda i: (0, i))],
        out_specs=(block, block, pl.BlockSpec((32, chunk), lambda i: (0, i))),
        compiler_params=VMEM,
        cost_estimate=pl.CostEstimate(flops=40 * width * count, bytes_accessed=4 * width * count, transcendentals=0),
        name="tables",
    )(waves)


def project_body(ev_ref, ev_low_ref, od_ref, od_low_ref, cos_ref, sin_ref, phase_ref, out_ref):
    half = ev_low_ref.shape[1]
    dot = partial(jnp.dot, preferred_element_type=jnp.float32)
    part_c = dot(ev_ref[...], cos_ref[...]) + dot(ev_low_ref[...], cos_ref[:half])
    part_s = dot(od_ref[...], sin_ref[...]) + dot(od_low_ref[...], sin_ref[:half])
    real = [0.0, 0.0]
    imag = [0.0, 0.0]
    for v in range(8):
        cos_x = phase_ref[v : v + 1]
        sin_x = phase_ref[8 + v : 9 + v]
        for n in range(2):
            same = slice((v * 4 + n) * 8, (v * 4 + n) * 8 + 8)
            flip = slice((v * 4 + 2 + n) * 8, (v * 4 + 2 + n) * 8 + 8)
            real[n] = real[n] + (cos_x * part_c[same] - sin_x * part_s[flip])
            imag[n] = imag[n] + (cos_x * part_s[same] + sin_x * part_c[flip])
    sum_real = 0.0
    sum_imag = 0.0
    for n in range(2):
        cos_n, sin_n = math.cos(OMEGA * (n + 1)), math.sin(OMEGA * (n + 1))
        sum_real = sum_real + (cos_n * real[n] + sin_n * imag[n])
        sum_imag = sum_imag + (cos_n * imag[n] - sin_n * real[n])
    cos_c, sin_c = phase_ref[16:24], phase_ref[24:32]
    out_ref[0:8] = sum_real * cos_c - sum_imag * sin_c
    out_ref[8:16] = sum_real * sin_c + sum_imag * cos_c


def project(planes, cos_y, sin_y, phases, start, count):
    chunk = 512
    ev, ev_low, od, od_low = planes
    width = cos_y.shape[0]
    offset = start // chunk
    whole = lambda a: pl.BlockSpec(a.shape, lambda i: (0, 0))
    table = pl.BlockSpec((width, chunk), lambda i: (0, i + offset))
    return pl.pallas_call(
        project_body,
        grid=(count // chunk,),
        out_shape=jax.ShapeDtypeStruct((16, count), jnp.float32),
        in_specs=[whole(ev), whole(ev_low), whole(od), whole(od_low), table, table,
                  pl.BlockSpec((32, chunk), lambda i: (0, i + offset))],
        out_specs=pl.BlockSpec((16, chunk), lambda i: (0, i)),
        compiler_params=VMEM,
        cost_estimate=pl.CostEstimate(
            flops=8 * ev.shape[0] * width * count, bytes_accessed=4 * width * count, transcendentals=0
        ),
        name="project",
    )(ev, ev_low, od, od_low, cos_y, sin_y, phases)


def swap(array, axis, mask):
    return lax.ppermute(array, axis, [(i, i ^ mask) for i in range(lax.axis_size(axis))])


def swap_other(array, axis):
    count = lax.axis_size(axis)
    return lax.ppermute(array, axis, [(i, (((i + 1) ^ 1) - 1) % count) for i in range(count)])


def bits_of(axis):
    return lax.axis_size(axis).bit_length() - 1


def own_first(directions):
    bits_x, bits_y = bits_of("gx"), bits_of("gy")
    owned = directions.shape[0] // (1 << (bits_x + bits_y))
    waves = directions.T.reshape((2,) + (2,) * (bits_x + bits_y) + (owned,))
    for bit in range(bits_x):
        turn = (lax.axis_index("gx") >> (bits_x - 1 - bit)) & 1
        waves = jnp.where(turn == 1, jnp.flip(waves, 1 + bit), waves)
    for bit in range(bits_y):
        turn = (lax.axis_index("gy") >> (bits_y - 1 - bit)) & 1
        waves = jnp.where(turn == 1, jnp.flip(waves, 1 + bits_x + bit), waves)
    order = [0] + [1 + bits_x + bit for bit in reversed(range(bits_y))]
    order = order + [1 + bit for bit in range(bits_x)] + [1 + bits_x + bits_y]
    return waves.transpose(order).reshape(2, directions.shape[0])


def local(e_field, h_field, pol_now, pol_old, eps_inf, materials, surface, poles, directions):
    _, _, rows, width = e_field.shape
    scale = 1.0 / math.sqrt(rows * lax.axis_size("gx") * width * lax.axis_size("gy"))
    one, two, near, late, factors = prepare(e_field, h_field, pol_now, pol_old, eps_inf, materials, poles)
    one = swap(one, "gy", 1)
    two = swap_other(two, "gy")
    cos_y, sin_y, phases = tables(own_first(directions), rows, width, scale)
    x_one, x_two = first_step(e_field, h_field, near, factors, one, two)
    x_one = swap(x_one, "gx", 1)
    x_two = swap_other(x_two, "gx")
    e_new, h_new, *planes = both_steps(
        e_field, h_field, near, late, factors, surface, one, two, x_one, x_two
    )
    half = directions.shape[0] // 2
    far = project(planes, cos_y, sin_y, phases, half, half)
    arrived = swap(far, "gy", 1)
    far = project(planes, cos_y, sin_y, phases, 0, half) + arrived
    for axis, masks in (("gy", [1 << b for b in range(1, bits_of("gy"))]),
                        ("gx", [1 << b for b in reversed(range(bits_of("gx")))])):
        for mask in masks:
            half = half // 2
            far = far[:, :half] + swap(far[:, half:], axis, mask)
    return e_new, h_new, far.T


def solution(mesh):
    field = P("design", None, "gx", "gy")
    cell = P("design", "gx", "gy")
    return jax.shard_map(
        local,
        mesh=mesh,
        in_specs=(field, field, field, field, cell, cell, cell, P(), P()),
        out_specs=(field, field, P(("gx", "gy"), "design")),
        check_vma=False,
    )
```

time: 196 us -> 42.8 us (0.22)
  other arithmetic: 66.2 us -> 0.71 us
  waiting for transfers between devices: 57.9 us -> 12.1 us
  matrix products: 20.3 us -> 0 us
  between operations: 15.2 us -> 0.81 us
  Pallas kernels: 0 us -> 9.99 us
  starting transfers between devices: 21 us -> 11.2 us
  local copies, waits for them, and re-layouts: 14.3 us -> 7.5 us
    reduce_scatter x1 -> x0, waiting for transfers between devices: 56.2 us -> none  [local(): lax.psum_scatter(terms(jnp.int32(0), lax.axis_size(('gx', 'gy')) * owned)...]
    select_n x3, other arithmetic: 32.3 us -> 0.06 us  [the longest x2 0.04 us: own_first(): waves = jnp.where(turn == 1, jnp.flip(waves, 1 + bit), waves)]
    dot_general x2 -> x0, matrix products: 20.3 us -> none  [project(): lax.dot_general(plane.reshape(8 * width_x, width_y), table_y, (((1,), (1,...]
    cos x2 -> x0, other arithmetic: 18.1 us -> none  [the longest x1 14.7 us: project(): table_y = jnp.concatenate([jnp.cos(angle_y), jnp.sin(angle_y)], axis=0)]
    ppermute x8, waiting for transfers between devices: 1.76 us -> 12.1 us  [the longest x6 9.6 us: swap(): lax.ppermute(array, axis, [(i, i ^ mask) for i in range(lax.axis_size(axi...]
    pallas_call x0 -> x6, Pallas kernels: none -> 9.99 us  [the longest x2 4.04 us: project(): pl.pallas_call(project_body, grid=(count // chunk,), out_shape=jax.ShapeD...]
    ppermute x8, starting transfers between devices: 21 us -> 11.2 us  [the longest x6 6.15 us: swap(): lax.ppermute(array, axis, [(i, i ^ mask) for i in range(lax.axis_size(axi...]
    broadcast_in_dim x8 -> x0, local copies, waits for them, and re-layouts: 5.85 us -> none  [the longest x2 2.48 us: curl_e(): next_y[:, :, :, None]]
  transfers between devices with their start and end apart: 9 -> 8, of which waited for: 2 -> 5; matrix products, arithmetic and copies ran while one was open for 34% -> 3% of each run, Pallas kernels for 0% -> 10%
where the time goes in v1:
time: 42.8 us; the launch traced here: 42.4 us
  waiting for transfers between devices  12.1 us (28%)
  starting transfers between devices  11.2 us (26%)
  Pallas kernels  9.99 us (23%)
  local copies, waits for them, and re-layouts  7.5 us (18%)
  between operations  0.81 us (2%)
  other arithmetic  0.71 us (2%)
    ppermute x6, waiting for transfers between devices, swap(): lax.ppermute(array, axis, [(i, i ^ mask) for i in range(lax.axis_size(axi...  9.6 us
    unnamed x20, local copies, waits for them, and re-layouts  6.47 us
    ppermute x6, starting transfers between devices, swap(): lax.ppermute(array, axis, [(i, i ^ mask) for i in range(lax.axis_size(axi...  6.15 us
    ppermute x2, starting transfers between devices, swap_other(): lax.ppermute(array, axis, [(i, ((i + 1 ^ 1) - 1) % count) for i in range(...  5.09 us
    pallas_call x2, Pallas kernels, project(): pl.pallas_call(project_body, grid=(count // chunk,), out_shape=jax.ShapeD...  4.04 us
    ppermute x2, waiting for transfers between devices, swap_other(): lax.ppermute(array, axis, [(i, ((i + 1 ^ 1) - 1) % count) for i in range(...  2.54 us
    pallas_call x1, Pallas kernels, tables(): pl.pallas_call(partial(table_body, rows=rows, width=width, scale=scale),...  2.3 us
    pallas_call x1, Pallas kernels, both_steps(): pl.pallas_call(both_body, out_shape=(field, field, full, part, full, part...  1.8 us
  transfers between devices with their start and end apart: 8, of which 5 were waited for; matrix products, arithmetic and copies ran while one was open for 3% of the time, Pallas kernels for 10%

profile of v1, /device:TPU:0, one launch (start us, length us, event | category | flops | bytes accessed | tf_op | source)
XLA Modules:
  0.0 42.4 jit_solution(16402644882629031883)
XLA Ops:
  0.6 0.0 copy-start
  0.6 1.0 %copy-done = f32[3,8,16,256]{3,2,1,0:T(8,128)S(1)} copy-done((f32[3,8,16,256]{3,2,1,0:T(8,128)S(1)}, f32[3,8,16,256]{3,2,1,0:T(8,128)}, u32[]{:S(2)}) %copy-start) | copy-done | bytes 393240
  1.6 0.0 copy-start.2
  1.6 1.0 %copy-done.2 = f32[3,8,16,256]{3,2,1,0:T(8,128)S(1)} copy-done((f32[3,8,16,256]{3,2,1,0:T(8,128)S(1)}, f32[3,8,16,256]{3,2,1,0:T(8,128)}, u32[]{:S(2)}) %copy-start.2) | copy-done | bytes 393240
  2.6 0.0 copy-start.4
  2.6 1.0 %copy-done.4 = f32[3,8,16,256]{3,2,1,0:T(8,128)S(1)} copy-done((f32[3,8,16,256]{3,2,1,0:T(8,128)S(1)}, f32[3,8,16,256]{3,2,1,0:T(8,128)}, u32[]{:S(2)}) %copy-start.4) | copy-done | bytes 393240
  3.6 0.0 copy-start.5
  3.6 1.0 %copy-done.5 = f32[3,8,16,256]{3,2,1,0:T(8,128)S(1)} copy-done((f32[3,8,16,256]{3,2,1,0:T(8,128)S(1)}, f32[3,8,16,256]{3,2,1,0:T(8,128)}, u32[]{:S(2)}) %copy-start.5) | copy-done | bytes 393240
  4.6 0.0 copy-start.6
  4.6 0.9 %copy-done.6 = f32[8,16,256]{2,1,0:T(8,128)S(1)} copy-done((f32[8,16,256]{2,1,0:T(8,128)S(1)}, f32[8,16,256]{2,1,0:T(8,128)}, u32[]{:S(2)}) %copy-start.6) | copy-done | bytes 131096
  5.5 0.0 copy-start.7
  5.5 0.9 %copy-done.7 = s32[8,16,256]{2,1,0:T(8,128)S(1)} copy-done((s32[8,16,256]{2,1,0:T(8,128)S(1)}, s32[8,16,256]{2,1,0:T(8,128)}, u32[]{:S(2)}) %copy-start.7) | copy-done | bytes 131096
  6.4 0.0 copy-start.9
  6.4 0.7 %copy-done.9 = f32[3,16]{1,0:T(4,128)S(1)} copy-done((f32[3,16]{1,0:T(4,128)S(1)}, f32[3,16]{1,0:T(4,128)}, u32[]{:S(2)}) %copy-start.9) | copy-done | bytes 216
  7.1 0.0 copy-start.1
  7.1 0.0 copy-start.3
  7.1 0.0 copy-start.8
  7.1 1.2 %prepare.1 = (f32[8,16,128]{2,1,0:T(8,128)S(1)}, f32[8,16,128]{2,1,0:T(8,128)S(1)}, f32[3,8,16,256]{3,2,1,0:T(8,128)S(1)}, f32[3,8,16,256]{3,2,1,0:T(8,128)S(1)}, f32[2,8,16,256]{3,2,1,0:T(8,128)S(1)}) custom-call(f32[3,8,16,256]{3,2,1,0:T(8,128)S(1)} %copy-done, f32[3,8,16,256]{3,2,1,0:T(8,128)S(1)} %copy-done.2, f32[3,8,16,256]{3,2,1,0:T(8,128)S(1)} %copy-done.4, ...), custom_call_target="tpu_custom_call" | custom-call | tf_op jit(solution)/shard_map/prepare/pallas_call | solution.py:94
  8.3 0.5 %collective-permute-start = (f32[8,16,128]{2,1,0:T(8,128)S(1)}, f32[8,16,128]{2,1,0:T(8,128)S(1)}, u32[]{:S(2)}, u32[]{:S(2)}) collective-permute-start(f32[8,16,128]{2,1,0:T(8,128)S(1)} %get-tuple-element.22), channel_id=1, source_target_pairs={{0,1},{1,0},{2,3},{3,2},{4,5},{5,4},{6,7},{7,6},{8,9},{9,8},{10,11... | collective-permute-start | bytes 196616 | tf_op jit(solution)/shard_map/ppermute | solution.py:444
  8.8 2.6 %collective-permute-start.1 = (f32[8,16,128]{2,1,0:T(8,128)S(1)}, f32[8,16,128]{2,1,0:T(8,128)S(1)}, u32[]{:S(2)}, u32[]{:S(2)}) collective-permute-start(f32[8,16,128]{2,1,0:T(8,128)S(1)} %get-tuple-element.23), channel_id=1, source_target_pairs={{0,3},{1,2},{2,1},{3,0},{4,7},{5,6},{6,5},{7,4},{8,11},{9,10},{10,... | collective-permute-start | bytes 196616 | tf_op jit(solution)/shard_map/ppermute | solution.py:449
  11.4 0.8 %reshape.12 = f32[2,2,2,2,2,256]{5,4,3,2,1,0:T(2,128)S(1)} reshape(f32[2,4096]{1,0:T(2,128)} %bitcast.5) | data formatting | bytes 65536 | tf_op jit(solution)/shard_map/reshape | solution.py:459
  12.3 0.2 rev.17
  12.5 0.0 collective-permute-done.one_ref
  12.5 1.3 %collective-permute-done.1.two_ref = f32[8,16,128]{2,1,0:T(8,128)S(1)} collective-permute-done((f32[8,16,128]{2,1,0:T(8,128)S(1)}, f32[8,16,128]{2,1,0:T(8,128)S(1)}, u32[]{:S(2)}, u32[]{:S(2)}) %collective-permute-start.1) | collective-permute-done | bytes 65568 | tf_op jit(solution)/shard_map/ppermute | solution.py:449
  13.8 0.0 copy-done.1
  13.8 0.0 copy-done.3
  13.8 0.7 %first_step.1 = (f32[5,8,384]{2,1,0:T(8,128)S(1)}, f32[5,8,384]{2,1,0:T(8,128)S(1)}) custom-call(f32[3,8,16,256]{3,2,1,0:T(8,128)S(1)} %copy-done.1, f32[3,8,16,256]{3,2,1,0:T(8,128)S(1)} %copy-done.3, f32[3,8,16,256]{3,2,1,0:T(8,128)S(1)} %get-tuple-element.19.d_ref, f32[2,8,16,256]{3,2,1,0:T(8,128)S(1)} %get-tuple-element.21.k_ref, ...), custom_call_target="tpu_custom_call" | custom-call | tf_op jit(solution)/shard_map/first_step/pallas_call | solution.py:210
  14.5 1.6 %collective-permute-start.2 = (f32[5,8,384]{2,1,0:T(8,128)S(1)}, f32[5,8,384]{2,1,0:T(8,128)S(1)}, u32[]{:S(2)}, u32[]{:S(2)}) collective-permute-start(f32[5,8,384]{2,1,0:T(8,128)S(1)} %get-tuple-element.24), channel_id=1, source_target_pairs={{0,4},{4,0},{8,12},{12,8},{1,5},{5,1},{9,13},{13,9},{2,6},{6,2},{1... | collective-permute-start | bytes 184328 | tf_op jit(solution)/shard_map/ppermute | solution.py:444
  16.1 2.5 %collective-permute-start.3 = (f32[5,8,384]{2,1,0:T(8,128)S(1)}, f32[5,8,384]{2,1,0:T(8,128)S(1)}, u32[]{:S(2)}, u32[]{:S(2)}) collective-permute-start(f32[5,8,384]{2,1,0:T(8,128)S(1)} %get-tuple-element.25), channel_id=1, source_target_pairs={{0,12},{4,8},{8,4},{12,0},{1,13},{5,9},{9,5},{13,1},{2,14},{6,10},... | collective-permute-start | bytes 184328 | tf_op jit(solution)/shard_map/ppermute | solution.py:449
  18.6 2.3 %tables.1 = (bf16[256,4096]{1,0:T(8,128)(2,1)S(1)}, bf16[256,4096]{1,0:T(8,128)(2,1)S(1)}, f32[32,4096]{1,0:T(8,128)S(1)}) custom-call(f32[2,4096]{1,0:T(2,128)S(1)} %reshape.13.waves_ref), custom_call_target="tpu_custom_call" | custom-call | flops 41943040 | bytes 4194304 | tf_op jit(solution)/shard_map/tables/pallas_call | solution.py:383
  20.9 0.0 collective-permute-done.2.x_one_ref
  20.9 1.2 %collective-permute-done.3.x_two_ref = f32[5,8,384]{2,1,0:T(8,128)S(1)} collective-permute-done((f32[5,8,384]{2,1,0:T(8,128)S(1)}, f32[5,8,384]{2,1,0:T(8,128)S(1)}, u32[]{:S(2)}, u32[]{:S(2)}) %collective-permute-start.3) | collective-permute-done | bytes 61472 | tf_op jit(solution)/shard_map/ppermute | solution.py:449
  22.2 0.0 copy-done.8
  22.2 1.8 %both_steps.1 = (f32[3,8,16,256]{3,2,1,0:T(8,128)}, f32[3,8,16,256]{3,2,1,0:T(8,128)}, bf16[256,256]{1,0:T(8,128)(2,1)S(1)}, bf16[256,128]{1,0:T(8,128)(2,1)S(1)...) custom-call(f32[3,8,16,256]{3,2,1,0:T(8,128)S(1)} %copy-done.1, f32[3,8,16,256]{3,2,1,0:T(8,128)S(1)} %copy-done.3, ...), custom_call_target="tpu_custom_call" | custom-call | tf_op jit(solution)/shard_map/both_steps/pallas_call | solution.py:342
  24.0 2.0 %project.3 = f32[16,2048]{1,0:T(8,128)S(1)} custom-call(bf16[256,256]{1,0:T(8,128)(2,1)S(1)} %get-tuple-element.28.ev_ref, bf16[256,128]{1,0:T(8,128)(2,1)S(1)} %get-tuple-element.29.ev_low_ref, bf16[256,256]{1,0:T(8,128)(2,1)S(1)} %get-tuple-element.30.od_ref, bf16[256,128]{1,0:T(8,128)(2,1)S(1)} %get-tuple-element.31.od_low_ref, ...), custom_call_target="tpu_custom_call" | custom-call | flops 1073741824 | bytes 2097152 | tf_op jit(solution)/shard_map/project/pallas_call | solution.py:428
  26.0 0.1 collective-permute-start.4
  26.1 2.0 %project.2 = f32[16,2048]{1,0:T(8,128)S(1)} custom-call(bf16[256,256]{1,0:T(8,128)(2,1)S(1)} %get-tuple-element.28.ev_ref, bf16[256,128]{1,0:T(8,128)(2,1)S(1)} %get-tuple-element.29.ev_low_ref, bf16[256,256]{1,0:T(8,128)(2,1)S(1)} %get-tuple-element.30.od_ref, bf16[256,128]{1,0:T(8,128)(2,1)S(1)} %get-tuple-element.31.od_low_ref, ...), custom_call_target="tpu_custom_call" | custom-call | flops 1073741824 | bytes 2097152 | tf_op jit(solution)/shard_map/project/pallas_call | solution.py:428
  28.1 0.0 collective-permute-done.4
  28.2 1.6 %collective-permute-start.5 = (f32[16,1024]{1,0:T(8,128)S(1)}, f32[16,1024]{1,0:T(8,128)S(1)}, u32[]{:S(2)}, u32[]{:S(2)}) collective-permute-start(f32[16,1024]{1,0:T(8,128)S(1)} %slice.25), channel_id=1, source_target_pairs={{0,2},{1,3},{2,0},{3,1},{4,6},{5,7},{6,4},{7,5},{8,10},{9,11},{10,... | collective-permute-start | bytes 196616 | tf_op jit(solution)/shard_map/ppermute | solution.py:444
  29.7 3.0 %collective-permute-done.5 = f32[16,1024]{1,0:T(8,128)S(1)} collective-permute-done((f32[16,1024]{1,0:T(8,128)S(1)}, f32[16,1024]{1,0:T(8,128)S(1)}, u32[]{:S(2)}, u32[]{:S(2)}) %collective-permute-start.5) | collective-permute-done | bytes 65568 | tf_op jit(solution)/shard_map/ppermute | solution.py:444
  32.7 2.0 %collective-permute-start.6 = (f32[16,512]{1,0:T(8,128)S(1)}, f32[16,512]{1,0:T(8,128)S(1)}, u32[]{:S(2)}, u32[]{:S(2)}) collective-permute-start(f32[16,512]{1,0:T(8,128)S(1)} %slice.27), channel_id=1, source_target_pairs={{0,8},{4,12},{8,0},{12,4},{1,9},{5,13},{9,1},{13,5},{2,10},{6,14},... | collective-permute-start | bytes 98312 | tf_op jit(solution)/shard_map/ppermute | solution.py:444
  34.7 3.2 %collective-permute-done.6 = f32[16,512]{1,0:T(8,128)S(1)} collective-permute-done((f32[16,512]{1,0:T(8,128)S(1)}, f32[16,512]{1,0:T(8,128)S(1)}, u32[]{:S(2)}, u32[]{:S(2)}) %collective-permute-start.6) | collective-permute-done | bytes 32800 | tf_op jit(solution)/shard_map/ppermute | solution.py:444
  38.0 0.4 %collective-permute-start.7 = (f32[16,256]{1,0:T(8,128)S(1)}, f32[16,256]{1,0:T(8,128)S(1)}, u32[]{:S(2)}, u32[]{:S(2)}) collective-permute-start(f32[16,256]{1,0:T(8,128)S(1)} %slice.29), channel_id=1, source_target_pairs={{0,4},{4,0},{8,12},{12,8},{1,5},{5,1},{9,13},{13,9},{2,6},{6,2},{1... | collective-permute-start | bytes 49160 | tf_op jit(solution)/shard_map/ppermute | solution.py:444
  38.4 3.4 %collective-permute-done.7 = f32[16,256]{1,0:T(8,128)S(1)} collective-permute-done((f32[16,256]{1,0:T(8,128)S(1)}, f32[16,256]{1,0:T(8,128)S(1)}, u32[]{:S(2)}, u32[]{:S(2)}) %collective-permute-start.7) | collective-permute-done | bytes 16416 | tf_op jit(solution)/shard_map/ppermute | solution.py:444
  41.8 0.6 %fusion.1 = f32[256,16]{0,1:T(8,128)} fusion(f32[16,256]{1,0:T(8,128)S(1)} %collective-permute-done.7, f32[16,512]{1,0:T(8,128)S(1)} %slice_add_fusion.1), kind=kLoop, calls=%fused_computation.8 | loop fusion | flops 4096 | bytes 49152 | tf_op jit(solution)/shard_map/transpose | solution.py:493
  (12 shorter events, 0.2 us)
Async XLA Ops:
  0.6 1.0 %copy-start = (f32[3,8,16,256]{3,2,1,0:T(8,128)S(1)}, f32[3,8,16,256]{3,2,1,0:T(8,128)}, u32[]{:S(2)}) copy-start(f32[3,8,16,256]{3,2,1,0:T(8,128)} %e_ref.5) | copy-start | bytes 1179652
  1.6 1.0 %copy-start.2 = (f32[3,8,16,256]{3,2,1,0:T(8,128)S(1)}, f32[3,8,16,256]{3,2,1,0:T(8,128)}, u32[]{:S(2)}) copy-start(f32[3,8,16,256]{3,2,1,0:T(8,128)} %h_ref.5) | copy-start | bytes 1179652
  2.6 1.0 %copy-start.4 = (f32[3,8,16,256]{3,2,1,0:T(8,128)S(1)}, f32[3,8,16,256]{3,2,1,0:T(8,128)}, u32[]{:S(2)}) copy-start(f32[3,8,16,256]{3,2,1,0:T(8,128)} %p_ref.1) | copy-start | bytes 1179652
  3.6 1.0 %copy-start.5 = (f32[3,8,16,256]{3,2,1,0:T(8,128)S(1)}, f32[3,8,16,256]{3,2,1,0:T(8,128)}, u32[]{:S(2)}) copy-start(f32[3,8,16,256]{3,2,1,0:T(8,128)} %q_ref.1) | copy-start | bytes 1179652
  4.6 0.9 %copy-start.6 = (f32[8,16,256]{2,1,0:T(8,128)S(1)}, f32[8,16,256]{2,1,0:T(8,128)}, u32[]{:S(2)}) copy-start(f32[8,16,256]{2,1,0:T(8,128)} %eps_ref.1) | copy-start | bytes 393220
  5.5 0.9 %copy-start.7 = (s32[8,16,256]{2,1,0:T(8,128)S(1)}, s32[8,16,256]{2,1,0:T(8,128)}, u32[]{:S(2)}) copy-start(s32[8,16,256]{2,1,0:T(8,128)} %mat_ref.1) | copy-start | bytes 393220
  6.4 0.7 %copy-start.9 = (f32[3,16]{1,0:T(4,128)S(1)}, f32[3,16]{1,0:T(4,128)}, u32[]{:S(2)}) copy-start(f32[3,16]{1,0:T(4,128)} %poles_ref.1) | copy-start | bytes 580
  7.1 6.7 %copy-start.1 = (f32[3,8,16,256]{3,2,1,0:T(8,128)S(1)}, f32[3,8,16,256]{3,2,1,0:T(8,128)}, u32[]{:S(2)}) copy-start(f32[3,8,16,256]{3,2,1,0:T(8,128)} %e_ref.5) | copy-start | bytes 1179652
  7.1 6.7 %copy-start.3 = (f32[3,8,16,256]{3,2,1,0:T(8,128)S(1)}, f32[3,8,16,256]{3,2,1,0:T(8,128)}, u32[]{:S(2)}) copy-start(f32[3,8,16,256]{3,2,1,0:T(8,128)} %h_ref.5) | copy-start | bytes 1179652
  7.1 15.1 %copy-start.8 = (s32[2,16,256]{2,1,0:T(8,128)S(1)}, s32[2,16,256]{2,1,0:T(8,128)}, u32[]{:S(2)}) copy-start(s32[2,16,256]{2,1,0:T(8,128)} %surface_ref.1) | copy-start | bytes 98308
  8.3 4.2 %collective-permute-start = (f32[8,16,128]{2,1,0:T(8,128)S(1)}, f32[8,16,128]{2,1,0:T(8,128)S(1)}, u32[]{:S(2)}, u32[]{:S(2)}) collective-permute-start(f32[8,16,128]{2,1,0:T(8,128)S(1)} %get-tuple-element.22), channel_id=1, source_target_pairs={{0,1},{1,0},{2,3},{3,2},{4,5},{5,4},{6,7},{7,6},{8,9},{9,8},{10,11... | collective-permute-start | bytes 196616 | tf_op jit(solution)/shard_map/ppermute | solution.py:444
  8.8 5.0 %collective-permute-start.1 = (f32[8,16,128]{2,1,0:T(8,128)S(1)}, f32[8,16,128]{2,1,0:T(8,128)S(1)}, u32[]{:S(2)}, u32[]{:S(2)}) collective-permute-start(f32[8,16,128]{2,1,0:T(8,128)S(1)} %get-tuple-element.23), channel_id=1, source_target_pairs={{0,3},{1,2},{2,1},{3,0},{4,7},{5,6},{6,5},{7,4},{8,11},{9,10},{10,... | collective-permute-start | bytes 196616 | tf_op jit(solution)/shard_map/ppermute | solution.py:449
  14.5 6.4 %collective-permute-start.2 = (f32[5,8,384]{2,1,0:T(8,128)S(1)}, f32[5,8,384]{2,1,0:T(8,128)S(1)}, u32[]{:S(2)}, u32[]{:S(2)}) collective-permute-start(f32[5,8,384]{2,1,0:T(8,128)S(1)} %get-tuple-element.24), channel_id=1, source_target_pairs={{0,4},{4,0},{8,12},{12,8},{1,5},{5,1},{9,13},{13,9},{2,6},{6,2},{1... | collective-permute-start | bytes 184328 | tf_op jit(solution)/shard_map/ppermute | solution.py:444
  16.1 6.1 %collective-permute-start.3 = (f32[5,8,384]{2,1,0:T(8,128)S(1)}, f32[5,8,384]{2,1,0:T(8,128)S(1)}, u32[]{:S(2)}, u32[]{:S(2)}) collective-permute-start(f32[5,8,384]{2,1,0:T(8,128)S(1)} %get-tuple-element.25), channel_id=1, source_target_pairs={{0,12},{4,8},{8,4},{12,0},{1,13},{5,9},{9,5},{13,1},{2,14},{6,10},... | collective-permute-start | bytes 184328 | tf_op jit(solution)/shard_map/ppermute | solution.py:449
  26.0 2.1 %collective-permute-start.4 = (f32[16,2048]{1,0:T(8,128)S(1)}, f32[16,2048]{1,0:T(8,128)S(1)}, u32[]{:S(2)}, u32[]{:S(2)}) collective-permute-start(f32[16,2048]{1,0:T(8,128)S(1)} %project.3), channel_id=1, source_target_pairs={{0,1},{1,0},{2,3},{3,2},{4,5},{5,4},{6,7},{7,6},{8,9},{9,8},{10,11... | collective-permute-start | bytes 393224 | tf_op jit(solution)/shard_map/ppermute | solution.py:444
  28.2 4.5 %collective-permute-start.5 = (f32[16,1024]{1,0:T(8,128)S(1)}, f32[16,1024]{1,0:T(8,128)S(1)}, u32[]{:S(2)}, u32[]{:S(2)}) collective-permute-start(f32[16,1024]{1,0:T(8,128)S(1)} %slice.25), channel_id=1, source_target_pairs={{0,2},{1,3},{2,0},{3,1},{4,6},{5,7},{6,4},{7,5},{8,10},{9,11},{10,... | collective-permute-start | bytes 196616 | tf_op jit(solution)/shard_map/ppermute | solution.py:444
  32.7 5.2 %collective-permute-start.6 = (f32[16,512]{1,0:T(8,128)S(1)}, f32[16,512]{1,0:T(8,128)S(1)}, u32[]{:S(2)}, u32[]{:S(2)}) collective-permute-start(f32[16,512]{1,0:T(8,128)S(1)} %slice.27), channel_id=1, source_target_pairs={{0,8},{4,12},{8,0},{12,4},{1,9},{5,13},{9,1},{13,5},{2,10},{6,14},... | collective-permute-start | bytes 98312 | tf_op jit(solution)/shard_map/ppermute | solution.py:444
  38.0 3.8 %collective-permute-start.7 = (f32[16,256]{1,0:T(8,128)S(1)}, f32[16,256]{1,0:T(8,128)S(1)}, u32[]{:S(2)}, u32[]{:S(2)}) collective-permute-start(f32[16,256]{1,0:T(8,128)S(1)} %slice.29), channel_id=1, source_target_pairs={{0,4},{4,0},{8,12},{12,8},{1,5},{5,1},{9,13},{13,9},{2,6},{6,2},{1... | collective-permute-start | bytes 49160 | tf_op jit(solution)/shard_map/ppermute | solution.py:444

commit v2 on v1

--- a/solution.py
+++ b/solution.py
@@ -12,7 +12,7 @@
 WAVE = 0.3
 OMEGA = 0.25
 LANES = 128
-ITEMS = 10
+GROUPS = 4
 VMEM = pltpu.CompilerParams(vmem_limit_bytes=24 * 1024 * 1024)
 
 
@@ -41,9 +41,23 @@
     return 2.0 * sin_half * cos_half, 1.0 - 2.0 * sin_half * sin_half
 
 
-def prepare_body(e_ref, h_ref, p_ref, q_ref, eps_ref, mat_ref, poles_ref, one_ref, two_ref, d_ref, g_ref, k_ref, table_ref):
+def prepare_body(e_in, h_in, p_in, q_in, eps_in, mat_in, poles_in, one_ref, two_ref, d_ref, g_ref, k_ref, e_ref, h_ref,
+                 p_ref, q_ref, eps_ref, mat_ref, poles_ref, table_ref, sems, poles_sem):
     levels, rows, width = eps_ref.shape
     last = width - LANES
+    pairs = ((e_in, e_ref), (h_in, h_ref), (p_in, p_ref), (q_in, q_ref), (eps_in, eps_ref), (mat_in, mat_ref))
+    group = levels // GROUPS
+    poles_copy = pltpu.make_async_copy(poles_in, poles_ref, poles_sem)
+    poles_copy.start()
+    copies = []
+    for part in range(GROUPS):
+        cut = pl.ds(part * group, group)
+        for k, (source, target) in enumerate(pairs):
+            at = (slice(None), cut) if len(source.shape) == 4 else (cut,)
+            copy = pltpu.make_async_copy(source.at[at], target.at[at], sems.at[part, k])
+            copy.start()
+            copies.append(copy)
+    poles_copy.wait()
     table_ref[0:3, 0 : poles_ref.shape[1]] = poles_ref[...]
     omega_dt, gamma_dt, strength = (table_ref[i : i + 1, :] for i in range(3))
     denominator = 1.0 + 0.5 * gamma_dt
@@ -54,6 +68,9 @@
     lane = lane_index(tile)
     even = lax.rem(lax.axis_index("gy"), 2) == 0
     for z in range(levels):
+        if z % group == 0:
+            for copy in copies[z // group * 6 : z // group * 6 + 6]:
+                copy.wait()
         up = jnp.zeros(tile, jnp.float32)
         down = jnp.zeros(tile, jnp.float32)
         for start in range(0, width, LANES):
@@ -91,13 +108,24 @@
     message = jax.ShapeDtypeStruct((levels, rows, LANES), jnp.float32)
     field = jax.ShapeDtypeStruct(e_field.shape, jnp.float32)
     pair = jax.ShapeDtypeStruct((2, levels, rows, width), jnp.float32)
+    arrays = (e_field, h_field, pol_now, pol_old, eps_inf, materials, poles)
     return pl.pallas_call(
         prepare_body,
-        out_shape=(message, message, field, field, pair),
-        scratch_shapes=[pltpu.VMEM((8, LANES), jnp.float32)],
+        out_shape=(message, message, field, field, pair, field, field),
+        in_specs=[pl.BlockSpec(memory_space=pltpu.HBM)] * 7,
+        scratch_shapes=[
+            pltpu.VMEM(e_field.shape, jnp.float32),
+            pltpu.VMEM(e_field.shape, jnp.float32),
+            pltpu.VMEM(eps_inf.shape, jnp.float32),
+            pltpu.VMEM(eps_inf.shape, jnp.int32),
+            pltpu.VMEM(poles.shape, jnp.float32),
+            pltpu.VMEM((8, LANES), jnp.float32),
+            pltpu.SemaphoreType.DMA((GROUPS, 6)),
+            pltpu.SemaphoreType.DMA,
+        ],
         compiler_params=VMEM,
         name="prepare",
-    )(e_field, h_field, pol_now, pol_old, eps_inf, materials, poles)
+    )(*(pltpu.with_memory_space_constraint(array, pltpu.HBM) for array in arrays))
 
 
 def read_wide(own_ref, index, z, messages, item):
@@ -349,89 +377,83 @@
 
 
 def table_body(waves_ref, cos_ref, sin_ref, phase_ref, *, rows, width, scale):
-    count = waves_ref.shape[1]
     half = width // 2
-    wave_x, wave_y = WAVE * waves_ref[0:1, :], WAVE * waves_ref[1:2, :]
-    step = (row_index((8, count)).astype(jnp.float32)) + 0.5
-    sin_x, cos_x = sincos(wave_x * step)
-    phase_ref[0:8] = cos_x
-    phase_ref[8:16] = sin_x
+    chunk = 256
+    step = (row_index((8, chunk)).astype(jnp.float32)) + 0.5
     centre_x = (lax.axis_index("gx") * rows).astype(jnp.float32) + 0.5 * (rows - 1)
     centre_y = (lax.axis_index("gy") * width).astype(jnp.float32) + 0.5 * (width - 1)
-    sin_c, cos_c = sincos(wave_x * centre_x + wave_y * centre_y)
-    phase_ref[16:24] = jnp.broadcast_to(scale * cos_c, (8, count))
-    phase_ref[24:32] = jnp.broadcast_to(scale * sin_c, (8, count))
-    sin_y, cos_y = sincos(wave_y * step)
-    sin_w, cos_w = sincos(wave_y * 8.0)
-    cos_y = jnp.concatenate([cos_y, cos_y * cos_w - sin_y * sin_w], axis=0)
-    sin_y = jnp.concatenate([sin_y, sin_y * cos_w + cos_y[0:8] * sin_w], axis=0)
-    sin_w, cos_w = 2.0 * sin_w * cos_w, 1.0 - 2.0 * sin_w * sin_w
-    for start in range(0, half, 16):
-        if start:
-            cos_y, sin_y = cos_y * cos_w - sin_y * sin_w, sin_y * cos_w + cos_y * sin_w
-        for value, ref in ((cos_y, cos_ref), (sin_y, sin_ref)):
-            top = value.astype(jnp.bfloat16)
-            ref[start : start + 16] = top
-            ref[half + start : half + start + 16] = (value - top.astype(jnp.float32)).astype(jnp.bfloat16)
+
+    @pl.loop(0, waves_ref.shape[1] // chunk)
+    def _(turn):
+        cut = pl.ds(pl.multiple_of(turn * chunk, chunk), chunk)
+        wave_x, wave_y = WAVE * waves_ref[0:1, cut], WAVE * waves_ref[1:2, cut]
+        sin_x, cos_x = sincos(wave_x * step)
+        phase_ref[0:8, cut] = cos_x
+        phase_ref[8:16, cut] = sin_x
+        sin_c, cos_c = sincos(wave_x * centre_x + wave_y * centre_y)
+        phase_ref[16:24, cut] = jnp.broadcast_to(scale * cos_c, step.shape)
+        phase_ref[24:32, cut] = jnp.broadcast_to(scale * sin_c, step.shape)
+        sin_y, cos_y = sincos(wave_y * step)
+        sin_w, cos_w = sincos(wave_y * 8.0)
+        cos_y = jnp.concatenate([cos_y, cos_y * cos_w - sin_y * sin_w], axis=0)
+        sin_y = jnp.concatenate([sin_y, sin_y * cos_w + cos_y[0:8] * sin_w], axis=0)
+        sin_w, cos_w = 2.0 * sin_w * cos_w, 1.0 - 2.0 * sin_w * sin_w
+        for start in range(0, half, 16):
+            if start:
+                cos_y, sin_y = cos_y * cos_w - sin_y * sin_w, sin_y * cos_w + cos_y * sin_w
+            for value, ref in ((cos_y, cos_ref), (sin_y, sin_ref)):
+                top = value.astype(jnp.bfloat16)
+                ref[start : start + 16, cut] = top
+                ref[half + start : half + start + 16, cut] = (value - top.astype(jnp.float32)).astype(jnp.bfloat16)
 
 
 def tables(waves, rows, width, scale):
     count = waves.shape[1]
-    chunk = 256
     table = jax.ShapeDtypeStruct((width, count), jnp.bfloat16)
-    block = pl.BlockSpec((width, chunk), lambda i: (0, i))
     return pl.pallas_call(
         partial(table_body, rows=rows, width=width, scale=scale),
-        grid=(count // chunk,),
         out_shape=(table, table, jax.ShapeDtypeStruct((32, count), jnp.float32)),
-        in_specs=[pl.BlockSpec((2, chunk), lambda i: (0, i))],
-        out_specs=(block, block, pl.BlockSpec((32, chunk), lambda i: (0, i))),
         compiler_params=VMEM,
         cost_estimate=pl.CostEstimate(flops=40 * width * count, bytes_accessed=4 * width * count, transcendentals=0),
         name="tables",
     )(waves)
 
 
-def project_body(ev_ref, ev_low_ref, od_ref, od_low_ref, cos_ref, sin_ref, phase_ref, out_ref):
+def project_body(ev_ref, ev_low_ref, od_ref, od_low_ref, cos_ref, sin_ref, phase_ref, out_ref, *, start):
     half = ev_low_ref.shape[1]
+    chunk = 256
     dot = partial(jnp.dot, preferred_element_type=jnp.float32)
-    part_c = dot(ev_ref[...], cos_ref[...]) + dot(ev_low_ref[...], cos_ref[:half])
-    part_s = dot(od_ref[...], sin_ref[...]) + dot(od_low_ref[...], sin_ref[:half])
-    real = [0.0, 0.0]
-    imag = [0.0, 0.0]
-    for v in range(8):
-        cos_x = phase_ref[v : v + 1]
-        sin_x = phase_ref[8 + v : 9 + v]
+    for at in range(0, out_ref.shape[1], chunk):
+        cut = slice(start + at, start + at + chunk)
+        part_c = dot(ev_ref[...], cos_ref[:, cut]) + dot(ev_low_ref[...], cos_ref[:half, cut])
+        part_s = dot(od_ref[...], sin_ref[:, cut]) + dot(od_low_ref[...], sin_ref[:half, cut])
+        real = [0.0, 0.0]
+        imag = [0.0, 0.0]
+        for v in range(8):
+            cos_x = phase_ref[v : v + 1, cut]
+            sin_x = phase_ref[8 + v : 9 + v, cut]
+            for n in range(2):
+                same = slice((v * 4 + n) * 8, (v * 4 + n) * 8 + 8)
+                flip = slice((v * 4 + 2 + n) * 8, (v * 4 + 2 + n) * 8 + 8)
+                real[n] = real[n] + (cos_x * part_c[same] - sin_x * part_s[flip])
+                imag[n] = imag[n] + (cos_x * part_s[same] + sin_x * part_c[flip])
+        sum_real = 0.0
+        sum_imag = 0.0
         for n in range(2):
-            same = slice((v * 4 + n) * 8, (v * 4 + n) * 8 + 8)
-            flip = slice((v * 4 + 2 + n) * 8, (v * 4 + 2 + n) * 8 + 8)
-            real[n] = real[n] + (cos_x * part_c[same] - sin_x * part_s[flip])
-            imag[n] = imag[n] + (cos_x * part_s[same] + sin_x * part_c[flip])
-    sum_real = 0.0
-    sum_imag = 0.0
-    for n in range(2):
-        cos_n, sin_n = math.cos(OMEGA * (n + 1)), math.sin(OMEGA * (n + 1))
-        sum_real = sum_real + (cos_n * real[n] + sin_n * imag[n])
-        sum_imag = sum_imag + (cos_n * imag[n] - sin_n * real[n])
-    cos_c, sin_c = phase_ref[16:24], phase_ref[24:32]
-    out_ref[0:8] = sum_real * cos_c - sum_imag * sin_c
-    out_ref[8:16] = sum_real * sin_c + sum_imag * cos_c
+            cos_n, sin_n = math.cos(OMEGA * (n + 1)), math.sin(OMEGA * (n + 1))
+            sum_real = sum_real + (cos_n * real[n] + sin_n * imag[n])
+            sum_imag = sum_imag + (cos_n * imag[n] - sin_n * real[n])
+        cos_c, sin_c = phase_ref[16:24, cut], phase_ref[24:32, cut]
+        out_ref[0:8, at : at + chunk] = sum_real * cos_c - sum_imag * sin_c
+        out_ref[8:16, at : at + chunk] = sum_real * sin_c + sum_imag * cos_c
 
 
 def project(planes, cos_y, sin_y, phases, start, count):
-    chunk = 512
     ev, ev_low, od, od_low = planes
     width = cos_y.shape[0]
-    offset = start // chunk
-    whole = lambda a: pl.BlockSpec(a.shape, lambda i: (0, 0))
-    table = pl.BlockSpec((width, chunk), lambda i: (0, i + offset))
     return pl.pallas_call(
-        project_body,
-        grid=(count // chunk,),
+        partial(project_body, start=start),
         out_shape=jax.ShapeDtypeStruct((16, count), jnp.float32),
-        in_specs=[whole(ev), whole(ev_low), whole(od), whole(od_low), table, table,
-                  pl.BlockSpec((32, chunk), lambda i: (0, i + offset))],
-        out_specs=pl.BlockSpec((16, chunk), lambda i: (0, i)),
         compiler_params=VMEM,
         cost_estimate=pl.CostEstimate(
             flops=8 * ev.shape[0] * width * count, bytes_accessed=4 * width * count, transcendentals=0
@@ -445,8 +467,8 @@
 
 
 def swap_other(array, axis):
-    count = lax.axis_size(axis)
-    return lax.ppermute(array, axis, [(i, (((i + 1) ^ 1) - 1) % count) for i in range(count)])
+    pairs = [(i, ((i + 1) ^ 1) - 1) for i in range(1, lax.axis_size(axis) - 1)]
+    return lax.ppermute(array, axis, pairs)
 
 
 def bits_of(axis):
@@ -471,7 +493,7 @@
 def local(e_field, h_field, pol_now, pol_old, eps_inf, materials, surface, poles, directions):
     _, _, rows, width = e_field.shape
     scale = 1.0 / math.sqrt(rows * lax.axis_size("gx") * width * lax.axis_size("gy"))
-    one, two, near, late, factors = prepare(e_field, h_field, pol_now, pol_old, eps_inf, materials, poles)
+    one, two, near, late, factors, e_field, h_field = prepare(e_field, h_field, pol_now, pol_old, eps_inf, materials, poles)
     one = swap(one, "gy", 1)
     two = swap_other(two, "gy")
     cos_y, sin_y, phases = tables(own_first(directions), rows, width, scale)

time: 42.8 us -> 36.8 us (0.86)
  local copies, waits for them, and re-layouts: 7.5 us -> 1.03 us
  starting transfers between devices: 11.2 us -> 17.3 us
  waiting for transfers between devices: 12.1 us -> 7.29 us
  Pallas kernels: 9.99 us -> 9.37 us
    ppermute x6, starting transfers between devices: 6.15 us -> 16 us  [swap(): lax.ppermute(array, axis, [(i, i ^ mask) for i in range(lax.axis_size(axi...]
    unnamed x20 -> x2, local copies, waits for them, and re-layouts: 6.47 us -> 0.01 us
    ppermute x2, starting transfers between devices: 5.09 us -> 1.31 us  [swap_other(): return lax.ppermute(array, axis, pairs)]
    ppermute x2, waiting for transfers between devices: 2.54 us -> 0.01 us  [swap_other(): return lax.ppermute(array, axis, pairs)]
    ppermute x6, waiting for transfers between devices: 9.6 us -> 7.29 us  [swap(): lax.ppermute(array, axis, [(i, i ^ mask) for i in range(lax.axis_size(axi...]
    pallas_call x2, Pallas kernels: 4.04 us -> 2.58 us  [project(): pl.pallas_call(partial(project_body, start=start), out_shape=jax.ShapeDty...]
    pallas_call x1, Pallas kernels: 1.18 us -> 2.56 us  [prepare(): pl.pallas_call(prepare_body, out_shape=(message, message, field, field, p...]
    pallas_call x1, Pallas kernels: 2.3 us -> 1.75 us  [tables(): pl.pallas_call(partial(table_body, rows=rows, width=width, scale=scale),...]
  transfers between devices with their start and end apart: 8 -> 8, of which waited for: 5 -> 3; matrix products, arithmetic and copies ran while one was open for 3% -> 3% of each run, Pallas kernels for 10% -> 8%
where the time goes in v2:
time: 36.8 us; the launch traced here: 36.6 us
  starting transfers between devices  17.3 us (47%)
  Pallas kernels  9.37 us (25%)
  waiting for transfers between devices  7.29 us (20%)
  local copies, waits for them, and re-layouts  1.03 us (3%)
  between operations  0.84 us (2%)
  other arithmetic  0.71 us (2%)
    ppermute x6, starting transfers between devices, swap(): lax.ppermute(array, axis, [(i, i ^ mask) for i in range(lax.axis_size(axi...  16 us
    ppermute x6, waiting for transfers between devices, swap(): lax.ppermute(array, axis, [(i, i ^ mask) for i in range(lax.axis_size(axi...  7.29 us
    pallas_call x2, Pallas kernels, project(): pl.pallas_call(partial(project_body, start=start), out_shape=jax.ShapeDty...  2.58 us
    pallas_call x1, Pallas kernels, prepare(): pl.pallas_call(prepare_body, out_shape=(message, message, field, field, p...  2.56 us
    pallas_call x1, Pallas kernels, both_steps(): pl.pallas_call(both_body, out_shape=(field, field, full, part, full, part...  1.82 us
    pallas_call x1, Pallas kernels, tables(): pl.pallas_call(partial(table_body, rows=rows, width=width, scale=scale),...  1.75 us
    ppermute x2, starting transfers between devices, swap_other(): return lax.ppermute(array, axis, pairs)  1.31 us
    reshape x2, local copies, waits for them, and re-layouts, own_first(): waves = directions.T.reshape((2,) + (2,) * (bits_x + bits_y) + (owned,))  0.82 us
  transfers between devices with their start and end apart: 8, of which 3 were waited for; matrix products, arithmetic and copies ran while one was open for 3% of the time, Pallas kernels for 8%

profile of v2, /device:TPU:0, one launch (start us, length us, event | category | flops | bytes accessed | tf_op | source)
XLA Modules:
  0.0 36.6 jit_solution(2762293950898584779)
XLA Ops:
  0.6 0.0 copy-start
  0.6 2.6 %prepare.1 = (f32[8,16,128]{2,1,0:T(8,128)S(1)}, f32[8,16,128]{2,1,0:T(8,128)S(1)}, f32[3,8,16,256]{3,2,1,0:T(8,128)S(1)}, f32[3,8,16,256]{3,2,1,0:T(8,128)S(1)}...) custom-call(f32[3,8,16,256]{3,2,1,0:T(8,128)} %e_in.1, ...), custom_call_target="tpu_custom_call" | custom-call | tf_op jit(solution)/shard_map/prepare/pallas_call | solution.py:112
  3.2 0.5 %collective-permute-start = (f32[8,16,128]{2,1,0:T(8,128)S(1)}, f32[8,16,128]{2,1,0:T(8,128)S(1)}, u32[]{:S(2)}, u32[]{:S(2)}) collective-permute-start(f32[8,16,128]{2,1,0:T(8,128)S(1)} %get-tuple-element.26), channel_id=1, source_target_pairs={{0,1},{1,0},{2,3},{3,2},{4,5},{5,4},{6,7},{7,6},{8,9},{9,8},{10,11... | collective-permute-start | bytes 196616 | tf_op jit(solution)/shard_map/ppermute | solution.py:466
  3.7 0.7 %collective-permute-start.1 = (f32[8,16,128]{2,1,0:T(8,128)S(1)}, f32[8,16,128]{2,1,0:T(8,128)S(1)}, u32[]{:S(2)}, u32[]{:S(2)}) collective-permute-start(f32[8,16,128]{2,1,0:T(8,128)S(1)} %get-tuple-element.27), channel_id=1, source_target_pairs={{1,2},{2,1},{5,6},{6,5},{9,10},{10,9},{13,14},{14,13},{17,18},{18,... | collective-permute-start | bytes 196616 | tf_op jit(solution)/shard_map/ppermute | solution.py:471
  4.4 0.8 %reshape.12 = f32[2,2,2,2,2,256]{5,4,3,2,1,0:T(2,128)S(1)} reshape(f32[2,4096]{1,0:T(2,128)} %bitcast.5) | data formatting | bytes 65536 | tf_op jit(solution)/shard_map/reshape | solution.py:481
  5.3 0.2 rev.17
  5.5 0.0 collective-permute-done.one_ref
  5.5 0.0 collective-permute-done.1.two_ref
  5.5 0.7 %first_step.1 = (f32[5,8,384]{2,1,0:T(8,128)S(1)}, f32[5,8,384]{2,1,0:T(8,128)S(1)}) custom-call(f32[3,8,16,256]{3,2,1,0:T(8,128)S(1)} %get-tuple-element.21.e_ref, f32[3,8,16,256]{3,2,1,0:T(8,128)S(1)} %get-tuple-element.22.h_ref, f32[3,8,16,256]{3,2,1,0:T(8,128)S(1)} %get-tuple-element.23.d_ref, f32[2,8,16,256]{3,2,1,0:T(8,128)S(1)} %get-tuple-element.25.k_ref, ...), custom_call_target="tpu_custom_call" | custom-call | tf_op jit(solution)/shard_map/first_step/pallas_call | solution.py:238
  6.2 2.7 %collective-permute-start.2 = (f32[5,8,384]{2,1,0:T(8,128)S(1)}, f32[5,8,384]{2,1,0:T(8,128)S(1)}, u32[]{:S(2)}, u32[]{:S(2)}) collective-permute-start(f32[5,8,384]{2,1,0:T(8,128)S(1)} %get-tuple-element.28), channel_id=1, source_target_pairs={{0,4},{4,0},{8,12},{12,8},{1,5},{5,1},{9,13},{13,9},{2,6},{6,2},{1... | collective-permute-start | bytes 184328 | tf_op jit(solution)/shard_map/ppermute | solution.py:466
  8.8 0.7 %collective-permute-start.3 = (f32[5,8,384]{2,1,0:T(8,128)S(1)}, f32[5,8,384]{2,1,0:T(8,128)S(1)}, u32[]{:S(2)}, u32[]{:S(2)}) collective-permute-start(f32[5,8,384]{2,1,0:T(8,128)S(1)} %get-tuple-element.29), channel_id=1, source_target_pairs={{4,8},{8,4},{5,9},{9,5},{6,10},{10,6},{7,11},{11,7},{20,24},{24,20... | collective-permute-start | bytes 184328 | tf_op jit(solution)/shard_map/ppermute | solution.py:471
  9.6 1.7 %tables.1 = (bf16[256,4096]{1,0:T(8,128)(2,1)S(1)}, bf16[256,4096]{1,0:T(8,128)(2,1)S(1)}, f32[32,4096]{1,0:T(8,128)S(1)}) custom-call(f32[2,4096]{1,0:T(2,128)S(1)} %reshape.13.waves_ref), custom_call_target="tpu_custom_call" | custom-call | flops 41943040 | bytes 4194304 | tf_op jit(solution)/shard_map/tables/pallas_call | solution.py:413
  11.3 0.0 collective-permute-done.2.x_one_ref
  11.3 0.0 collective-permute-done.3.x_two_ref
  11.3 0.0 copy-done
  11.4 1.8 %both_steps.1 = (f32[3,8,16,256]{3,2,1,0:T(8,128)}, f32[3,8,16,256]{3,2,1,0:T(8,128)}, bf16[256,256]{1,0:T(8,128)(2,1)S(1)}, bf16[256,128]{1,0:T(8,128)(2,1)S(1)...) custom-call(f32[3,8,16,256]{3,2,1,0:T(8,128)S(1)} %get-tuple-element.21.e_ref, ...), custom_call_target="tpu_custom_call" | custom-call | tf_op jit(solution)/shard_map/both_steps/pallas_call | solution.py:370
  13.2 1.3 %project.3 = f32[16,2048]{1,0:T(8,128)S(1)} custom-call(bf16[256,256]{1,0:T(8,128)(2,1)S(1)} %get-tuple-element.32.ev_ref, bf16[256,128]{1,0:T(8,128)(2,1)S(1)} %get-tuple-element.33.ev_low_ref, bf16[256,256]{1,0:T(8,128)(2,1)S(1)} %get-tuple-element.34.od_ref, bf16[256,128]{1,0:T(8,128)(2,1)S(1)} %get-tuple-element.35.od_low_ref, ...), custom_call_target="tpu_custom_call" | custom-call | flops 1073741824 | bytes 2097152 | tf_op jit(solution)/shard_map/project/pallas_call | solution.py:454
  14.5 4.4 %collective-permute-start.4 = (f32[16,2048]{1,0:T(8,128)S(1)}, f32[16,2048]{1,0:T(8,128)S(1)}, u32[]{:S(2)}, u32[]{:S(2)}) collective-permute-start(f32[16,2048]{1,0:T(8,128)S(1)} %project.3), channel_id=1, source_target_pairs={{0,1},{1,0},{2,3},{3,2},{4,5},{5,4},{6,7},{7,6},{8,9},{9,8},{10,11... | collective-permute-start | bytes 393224 | tf_op jit(solution)/shard_map/ppermute | solution.py:466
  18.8 1.3 %project.2 = f32[16,2048]{1,0:T(8,128)S(1)} custom-call(bf16[256,256]{1,0:T(8,128)(2,1)S(1)} %get-tuple-element.32.ev_ref, bf16[256,128]{1,0:T(8,128)(2,1)S(1)} %get-tuple-element.33.ev_low_ref, bf16[256,256]{1,0:T(8,128)(2,1)S(1)} %get-tuple-element.34.od_ref, bf16[256,128]{1,0:T(8,128)(2,1)S(1)} %get-tuple-element.35.od_low_ref, ...), custom_call_target="tpu_custom_call" | custom-call | flops 1073741824 | bytes 2097152 | tf_op jit(solution)/shard_map/project/pallas_call | solution.py:454
  20.1 0.0 collective-permute-done.4
  20.2 1.2 %collective-permute-start.5 = (f32[16,1024]{1,0:T(8,128)S(1)}, f32[16,1024]{1,0:T(8,128)S(1)}, u32[]{:S(2)}, u32[]{:S(2)}) collective-permute-start(f32[16,1024]{1,0:T(8,128)S(1)} %slice.25), channel_id=1, source_target_pairs={{0,2},{1,3},{2,0},{3,1},{4,6},{5,7},{6,4},{7,5},{8,10},{9,11},{10,... | collective-permute-start | bytes 196616 | tf_op jit(solution)/shard_map/ppermute | solution.py:466
  21.4 3.1 %collective-permute-done.5 = f32[16,1024]{1,0:T(8,128)S(1)} collective-permute-done((f32[16,1024]{1,0:T(8,128)S(1)}, f32[16,1024]{1,0:T(8,128)S(1)}, u32[]{:S(2)}, u32[]{:S(2)}) %collective-permute-start.5) | collective-permute-done | bytes 65568 | tf_op jit(solution)/shard_map/ppermute | solution.py:466
  24.5 5.7 %collective-permute-start.6 = (f32[16,512]{1,0:T(8,128)S(1)}, f32[16,512]{1,0:T(8,128)S(1)}, u32[]{:S(2)}, u32[]{:S(2)}) collective-permute-start(f32[16,512]{1,0:T(8,128)S(1)} %slice.27), channel_id=1, source_target_pairs={{0,8},{4,12},{8,0},{12,4},{1,9},{5,13},{9,1},{13,5},{2,10},{6,14},... | collective-permute-start | bytes 98312 | tf_op jit(solution)/shard_map/ppermute | solution.py:466
  30.3 1.9 %collective-permute-done.6 = f32[16,512]{1,0:T(8,128)S(1)} collective-permute-done((f32[16,512]{1,0:T(8,128)S(1)}, f32[16,512]{1,0:T(8,128)S(1)}, u32[]{:S(2)}, u32[]{:S(2)}) %collective-permute-start.6) | collective-permute-done | bytes 32800 | tf_op jit(solution)/shard_map/ppermute | solution.py:466
  32.2 1.5 %collective-permute-start.7 = (f32[16,256]{1,0:T(8,128)S(1)}, f32[16,256]{1,0:T(8,128)S(1)}, u32[]{:S(2)}, u32[]{:S(2)}) collective-permute-start(f32[16,256]{1,0:T(8,128)S(1)} %slice.29), channel_id=1, source_target_pairs={{0,4},{4,0},{8,12},{12,8},{1,5},{5,1},{9,13},{13,9},{2,6},{6,2},{1... | collective-permute-start | bytes 49160 | tf_op jit(solution)/shard_map/ppermute | solution.py:466
  33.7 2.3 %collective-permute-done.7 = f32[16,256]{1,0:T(8,128)S(1)} collective-permute-done((f32[16,256]{1,0:T(8,128)S(1)}, f32[16,256]{1,0:T(8,128)S(1)}, u32[]{:S(2)}, u32[]{:S(2)}) %collective-permute-start.7) | collective-permute-done | bytes 16416 | tf_op jit(solution)/shard_map/ppermute | solution.py:466
  36.0 0.6 %fusion.1 = f32[256,16]{0,1:T(8,128)} fusion(f32[16,256]{1,0:T(8,128)S(1)} %collective-permute-done.7, f32[16,512]{1,0:T(8,128)S(1)} %slice_add_fusion.1), kind=kLoop, calls=%fused_computation.8 | loop fusion | flops 4096 | bytes 49152 | tf_op jit(solution)/shard_map/transpose | solution.py:515
  (12 shorter events, 0.2 us)
Async XLA Ops:
  0.6 10.7 %copy-start = (s32[2,16,256]{2,1,0:T(8,128)S(1)}, s32[2,16,256]{2,1,0:T(8,128)}, u32[]{:S(2)}) copy-start(s32[2,16,256]{2,1,0:T(8,128)} %surface_ref.1) | copy-start | bytes 98308
  3.2 2.3 %collective-permute-start = (f32[8,16,128]{2,1,0:T(8,128)S(1)}, f32[8,16,128]{2,1,0:T(8,128)S(1)}, u32[]{:S(2)}, u32[]{:S(2)}) collective-permute-start(f32[8,16,128]{2,1,0:T(8,128)S(1)} %get-tuple-element.26), channel_id=1, source_target_pairs={{0,1},{1,0},{2,3},{3,2},{4,5},{5,4},{6,7},{7,6},{8,9},{9,8},{10,11... | collective-permute-start | bytes 196616 | tf_op jit(solution)/shard_map/ppermute | solution.py:466
  3.7 1.8 %collective-permute-start.1 = (f32[8,16,128]{2,1,0:T(8,128)S(1)}, f32[8,16,128]{2,1,0:T(8,128)S(1)}, u32[]{:S(2)}, u32[]{:S(2)}) collective-permute-start(f32[8,16,128]{2,1,0:T(8,128)S(1)} %get-tuple-element.27), channel_id=1, source_target_pairs={{1,2},{2,1},{5,6},{6,5},{9,10},{10,9},{13,14},{14,13},{17,18},{18,... | collective-permute-start | bytes 196616 | tf_op jit(solution)/shard_map/ppermute | solution.py:471
  6.2 5.2 %collective-permute-start.2 = (f32[5,8,384]{2,1,0:T(8,128)S(1)}, f32[5,8,384]{2,1,0:T(8,128)S(1)}, u32[]{:S(2)}, u32[]{:S(2)}) collective-permute-start(f32[5,8,384]{2,1,0:T(8,128)S(1)} %get-tuple-element.28), channel_id=1, source_target_pairs={{0,4},{4,0},{8,12},{12,8},{1,5},{5,1},{9,13},{13,9},{2,6},{6,2},{1... | collective-permute-start | bytes 184328 | tf_op jit(solution)/shard_map/ppermute | solution.py:466
  8.8 2.5 %collective-permute-start.3 = (f32[5,8,384]{2,1,0:T(8,128)S(1)}, f32[5,8,384]{2,1,0:T(8,128)S(1)}, u32[]{:S(2)}, u32[]{:S(2)}) collective-permute-start(f32[5,8,384]{2,1,0:T(8,128)S(1)} %get-tuple-element.29), channel_id=1, source_target_pairs={{4,8},{8,4},{5,9},{9,5},{6,10},{10,6},{7,11},{11,7},{20,24},{24,20... | collective-permute-start | bytes 184328 | tf_op jit(solution)/shard_map/ppermute | solution.py:471
  14.5 5.7 %collective-permute-start.4 = (f32[16,2048]{1,0:T(8,128)S(1)}, f32[16,2048]{1,0:T(8,128)S(1)}, u32[]{:S(2)}, u32[]{:S(2)}) collective-permute-start(f32[16,2048]{1,0:T(8,128)S(1)} %project.3), channel_id=1, source_target_pairs={{0,1},{1,0},{2,3},{3,2},{4,5},{5,4},{6,7},{7,6},{8,9},{9,8},{10,11... | collective-permute-start | bytes 393224 | tf_op jit(solution)/shard_map/ppermute | solution.py:466
  20.2 4.3 %collective-permute-start.5 = (f32[16,1024]{1,0:T(8,128)S(1)}, f32[16,1024]{1,0:T(8,128)S(1)}, u32[]{:S(2)}, u32[]{:S(2)}) collective-permute-start(f32[16,1024]{1,0:T(8,128)S(1)} %slice.25), channel_id=1, source_target_pairs={{0,2},{1,3},{2,0},{3,1},{4,6},{5,7},{6,4},{7,5},{8,10},{9,11},{10,... | collective-permute-start | bytes 196616 | tf_op jit(solution)/shard_map/ppermute | solution.py:466
  24.5 7.6 %collective-permute-start.6 = (f32[16,512]{1,0:T(8,128)S(1)}, f32[16,512]{1,0:T(8,128)S(1)}, u32[]{:S(2)}, u32[]{:S(2)}) collective-permute-start(f32[16,512]{1,0:T(8,128)S(1)} %slice.27), channel_id=1, source_target_pairs={{0,8},{4,12},{8,0},{12,4},{1,9},{5,13},{9,1},{13,5},{2,10},{6,14},... | collective-permute-start | bytes 98312 | tf_op jit(solution)/shard_map/ppermute | solution.py:466
  32.2 3.8 %collective-permute-start.7 = (f32[16,256]{1,0:T(8,128)S(1)}, f32[16,256]{1,0:T(8,128)S(1)}, u32[]{:S(2)}, u32[]{:S(2)}) collective-permute-start(f32[16,256]{1,0:T(8,128)S(1)} %slice.29), channel_id=1, source_target_pairs={{0,4},{4,0},{8,12},{12,8},{1,5},{5,1},{9,13},{13,9},{2,6},{6,2},{1... | collective-permute-start | bytes 49160 | tf_op jit(solution)/shard_map/ppermute | solution.py:466

commit v3 on v2

v3 whole, which is shorter than its diff:
```python
from functools import partial
import math

import jax
import jax.numpy as jnp
from jax import lax
from jax.experimental import pallas as pl
from jax.experimental.pallas import tpu as pltpu
from jax.sharding import PartitionSpec as P

COURANT = 0.5
WAVE = 0.3
OMEGA = 0.25
LANES = 128
GROUPS = 4
SLOTS = 24
VMEM = pltpu.CompilerParams(vmem_limit_bytes=24 * 1024 * 1024)


def lane_index(shape):
    return lax.broadcasted_iota(jnp.int32, shape, len(shape) - 1)


def row_index(shape):
    return lax.broadcasted_iota(jnp.int32, shape, 0)


def sincos(angle):
    turns = jnp.round(angle * (0.5 / math.pi))
    rest = angle - turns * 6.28125
    rest = rest - turns * 0.0019350051879882812
    rest = rest - turns * 3.0199159819567e-07
    half = 0.5 * rest
    sq = half * half
    sin_half = 1.0 / 6227020800.0
    for term in (-1.0 / 39916800.0, 1.0 / 362880.0, -1.0 / 5040.0, 1.0 / 120.0, -1.0 / 6.0, 1.0):
        sin_half = sin_half * sq + term
    sin_half = sin_half * half
    cos_half = -1.0 / 87178291200.0
    for term in (1.0 / 479001600.0, -1.0 / 3628800.0, 1.0 / 40320.0, -1.0 / 720.0, 1.0 / 24.0, -0.5, 1.0):
        cos_half = cos_half * sq + term
    return 2.0 * sin_half * cos_half, 1.0 - 2.0 * sin_half * sin_half


def prepare_body(e_in, h_in, p_in, q_in, eps_in, mat_in, poles_in, one_ref, two_ref, d_ref, g_ref, k_ref, e_ref, h_ref,
                 p_ref, q_ref, eps_ref, mat_ref, poles_ref, table_ref, up_ref, down_ref, sems, poles_sem):
    levels, rows, width = eps_ref.shape
    last = width - LANES
    pairs = ((e_in, e_ref), (h_in, h_ref), (p_in, p_ref), (q_in, q_ref), (eps_in, eps_ref), (mat_in, mat_ref))
    group = levels // GROUPS
    poles_copy = pltpu.make_async_copy(poles_in, poles_ref, poles_sem)
    poles_copy.start()
    copies = []
    for part in range(GROUPS):
        cut = pl.ds(part * group, group)
        for k, (source, target) in enumerate(pairs):
            at = (slice(None), cut) if len(source.shape) == 4 else (cut,)
            copy = pltpu.make_async_copy(source.at[at], target.at[at], sems.at[part, k])
            copy.start()
            copies.append(copy)
    poles_copy.wait()
    table_ref[0:3, 0 : poles_ref.shape[1]] = poles_ref[...]
    omega_dt, gamma_dt, strength = (table_ref[i : i + 1, :] for i in range(3))
    denominator = 1.0 + 0.5 * gamma_dt
    tile = (rows, LANES)
    table_a = jnp.broadcast_to((2.0 - omega_dt * omega_dt) / denominator, tile)
    table_b = jnp.broadcast_to(-(1.0 - 0.5 * gamma_dt) / denominator, tile)
    table_c = jnp.broadcast_to(strength * omega_dt * omega_dt / denominator, tile)
    lane = lane_index(tile)
    even = lax.rem(lax.axis_index("gy"), 2) == 0
    for z in range(levels):
        if z % group == 0:
            for copy in copies[z // group * 6 : z // group * 6 + 6]:
                copy.wait()
        up = jnp.zeros(tile, jnp.float32)
        down = jnp.zeros(tile, jnp.float32)
        for start in range(0, width, LANES):
            cut = slice(start, start + LANES)
            number = mat_ref[z, :, cut]
            a = jnp.take_along_axis(table_a, number, axis=1)
            b = jnp.take_along_axis(table_b, number, axis=1)
            c = jnp.take_along_axis(table_c, number, axis=1)
            inv = 1.0 / eps_ref[z, :, cut]
            half = COURANT * inv
            k_ref[0, z, :, cut] = half
            k_ref[1, z, :, cut] = 1.0 - c * inv
            items = [e_ref[i, z, :, cut] for i in range(3)] + [h_ref[i, z, :, cut] for i in range(3)]
            for i in range(3):
                now, old = p_ref[i, z, :, cut], q_ref[i, z, :, cut]
                new = a * now + b * old + c * items[i]
                local = items[i] - (new - now) * inv
                d_ref[i, z, :, cut] = local
                g_ref[i, z, :, cut] = ((a * new - new) + b * now) * inv
                items.append(local)
            items.append(half)
            for k, item in enumerate(items):
                if start == 0:
                    moved = pltpu.roll(item, 2 * k, 1) if k else item
                    down = jnp.where((lane >= 2 * k) & (lane < 2 * k + 2), moved, down)
                if start == last:
                    moved = pltpu.roll(item, LANES - 2 * k, 1) if k else item
                    up = jnp.where((lane >= LANES - 2 - 2 * k) & (lane < LANES - 2 * k), moved, up)
        up_ref[z * rows : (z + 1) * rows] = up
        down_ref[z * rows : (z + 1) * rows] = down
    up = up_ref[...].T[LANES - SLOTS :]
    down = down_ref[...].T[:SLOTS]
    one_ref[...] = jnp.where(even, up, down)
    two_ref[...] = jnp.where(even, down, up)


def prepare(e_field, h_field, pol_now, pol_old, eps_inf, materials, poles):
    levels, rows, width = eps_inf.shape
    message = jax.ShapeDtypeStruct((SLOTS, levels * rows), jnp.float32)
    field = jax.ShapeDtypeStruct(e_field.shape, jnp.float32)
    pair = jax.ShapeDtypeStruct((2, levels, rows, width), jnp.float32)
    arrays = (e_field, h_field, pol_now, pol_old, eps_inf, materials, poles)
    return pl.pallas_call(
        prepare_body,
        out_shape=(message, message, field, field, pair, field, field),
        in_specs=[pl.BlockSpec(memory_space=pltpu.HBM)] * 7,
        scratch_shapes=[
            pltpu.VMEM(e_field.shape, jnp.float32),
            pltpu.VMEM(e_field.shape, jnp.float32),
            pltpu.VMEM(eps_inf.shape, jnp.float32),
            pltpu.VMEM(eps_inf.shape, jnp.int32),
            pltpu.VMEM(poles.shape, jnp.float32),
            pltpu.VMEM((8, LANES), jnp.float32),
            pltpu.VMEM((levels * rows, LANES), jnp.float32),
            pltpu.VMEM((levels * rows, LANES), jnp.float32),
            pltpu.SemaphoreType.DMA((GROUPS, 6)),
            pltpu.SemaphoreType.DMA,
        ],
        compiler_params=VMEM,
        name="prepare",
    )(*(pltpu.with_memory_space_constraint(array, pltpu.HBM) for array in arrays))


def read_wide(own_ref, index, z, halo_ref, item):
    both = halo_ref[z]
    lane = lane_index(both.shape)
    shift = 2 * item
    late = pltpu.roll(both, LANES - shift, 1) if item else both
    early = pltpu.roll(both, shift, 1) if item else both
    halo = jnp.where(lane < 2, late, jnp.where(lane >= LANES - 2, early, 0.0))
    return jnp.concatenate([own_ref[index, z], halo], axis=1)


def read_y_messages(one_ref, two_ref, halo_ref):
    place = lax.axis_index("gy")
    even = lax.rem(place, 2) == 0
    one, two = one_ref[...], two_ref[...]
    before = jnp.where(place > 0, jnp.where(even, two, one), 0.0)
    after = jnp.where(place < lax.axis_size("gy") - 1, jnp.where(even, one, two), 0.0)
    blank = jnp.zeros((LANES - 2 * SLOTS, one.shape[1]), jnp.float32)
    halo_ref[...] = jnp.concatenate([after, blank, before], axis=0).T.reshape(halo_ref.shape)


def ahead_y(v):
    return pltpu.roll(v, v.shape[1] - 1, 1)


def behind_y(v):
    return pltpu.roll(v, 1, 1)


def ahead_x(v, row):
    at = row_index(v.shape)
    return jnp.where(at == v.shape[0] - 1, row, pltpu.roll(v, v.shape[0] - 1, 0))


def behind_x(v, row):
    at = row_index(v.shape)
    return jnp.where(at == 0, row, pltpu.roll(v, 1, 0))


def magnetic(e_here, e_above, h_here, row_y, row_z, keep):
    ex, ey, ez = e_here
    hx, hy, hz = h_here
    up_x, up_y = e_above
    hx = hx - COURANT * ((ahead_y(ez) - ez) - (up_y - ey))
    hy = hy - COURANT * ((up_x - ex) - (ahead_x(ez, row_z) - ez))
    hz = hz - COURANT * ((ahead_x(ey, row_y) - ey) - (ahead_y(ex) - ex))
    return [jnp.where(keep, v, 0.0) for v in (hx, hy, hz)]


def curl_back(h_here, h_below, row_y, row_z):
    hx, hy, hz = h_here
    low_x, low_y = h_below
    return (
        (hz - behind_y(hz)) - (hy - low_y),
        (hx - low_x) - (hz - behind_x(hz, row_z)),
        (hy - behind_x(hy, row_y)) - (hx - behind_y(hx)),
    )


def kept_lanes(shape, width):
    return (lane_index(shape) < width + LANES // 2) | (lax.axis_index("gy") > 0)


def first_body(e_ref, h_ref, d_ref, k_ref, one_ref, two_ref, tie_ref, out_one_ref, out_two_ref, h1_ref, e1_ref, e0_ref, halo_ref):
    del tie_ref
    _, levels, rows, width = e_ref.shape
    wide = (rows, width + LANES)
    read_y_messages(one_ref, two_ref, halo_ref)
    keep = kept_lanes(wide, width)
    zero_row = jnp.zeros((1, wide[1]), jnp.float32)
    zero = jnp.zeros(wide, jnp.float32)
    for z in range(levels):
        for i in range(3):
            e0_ref[i, z] = read_wide(e_ref, i, z, halo_ref, i)
    for z in range(levels):
        above = [e0_ref[i, z + 1] for i in range(2)] if z + 1 < levels else [zero, zero]
        h_here = [read_wide(h_ref, i, z, halo_ref, 3 + i) for i in range(3)]
        new = magnetic([e0_ref[i, z] for i in range(3)], above, h_here, zero_row, zero_row, keep)
        for i in range(3):
            h1_ref[i, z] = new[i]
    inv = []
    for z in range(levels):
        below = [h1_ref[i, z - 1] for i in range(2)] if z else [zero, zero]
        curl = curl_back([h1_ref[i, z] for i in range(3)], below, zero_row, zero_row)
        inv.append(read_wide(k_ref, 0, z, halo_ref, 9))
        for i in range(3):
            e1_ref[i, z] = read_wide(d_ref, i, z, halo_ref, 6 + i) + inv[z] * curl[i]
    even = lax.rem(lax.axis_index("gx"), 2) == 0
    keep_row = kept_lanes((1, wide[1]), width)
    end = slice(rows - 1, rows)
    for z in range(levels):
        hy, hz = h1_ref[1, z, end], h1_ref[2, z, end]
        ex, ey, ez = (e1_ref[i, z, end] for i in range(3))
        up_x = e1_ref[0, z + 1, end] if z + 1 < levels else zero_row
        second_y = hy - COURANT * ((up_x - ex) + ez)
        second_z = hz - COURANT * (-ey - (ahead_y(ex) - ex))
        up = [hy, hz, jnp.where(keep_row, second_y, 0.0), jnp.where(keep_row, second_z, 0.0), inv[z][end]]
        down = [e0_ref[1, z, 0:1], e0_ref[2, z, 0:1], e1_ref[1, z, 0:1], e1_ref[2, z, 0:1], inv[z][0:1]]
        for k in range(5):
            out_one_ref[k, z : z + 1] = jnp.where(even, up[k], down[k])
            out_two_ref[k, z : z + 1] = jnp.where(even, down[k], up[k])


def first_step(e_field, h_field, local, factors, one, two, tie):
    _, levels, rows, width = e_field.shape
    message = jax.ShapeDtypeStruct((5, levels, width + LANES), jnp.float32)
    store = (3, levels, rows, width + LANES)
    field = jax.ShapeDtypeStruct(store, jnp.float32)
    vmem = pl.BlockSpec(memory_space=pltpu.VMEM)
    return pl.pallas_call(
        first_body,
        out_shape=(message, message, field, field),
        in_specs=[vmem] * 6 + [pl.BlockSpec(memory_space=pl.ANY)],
        scratch_shapes=[pltpu.VMEM(store, jnp.float32), pltpu.VMEM((levels, rows, LANES), jnp.float32)],
        compiler_params=VMEM,
        name="first_step",
    )(e_field, h_field, local, factors, one, two, tie)


def store_plane(plane_ref, surface_ref, number, layer, part, value):
    rows, half = value.shape[0], plane_ref.shape[2]
    at = ((number * 2 + layer) * 4 + part) * rows
    weighted = value[:, : 2 * half] * surface_ref[layer].astype(jnp.float32)
    plane_ref[0, at : at + rows] = weighted[:, :half]
    plane_ref[1, at : at + rows] = weighted[:, half:]


def split_planes(plane_ref, split_refs, rows, pairs):
    ev_ref, ev_low_ref, od_ref, od_low_ref = split_refs
    kinds = 16
    half = plane_ref.shape[2]
    back = half - 1 - lane_index((kinds, half))
    for turn, v in enumerate(pairs):
        high = [plane_ref[side, pl.ds(rows // 2 + v, kinds, stride=rows), :] for side in range(2)]
        low = [plane_ref[side, pl.ds(rows // 2 - 1 - v, kinds, stride=rows), :] for side in range(2)]
        for parity in range(2):
            left, right = (b - a if parity else b + a for a, b in zip(low, high))
            left = jnp.take_along_axis(left, back, axis=1)
            at = slice((2 * turn + parity) * kinds, (2 * turn + parity + 1) * kinds)
            for value, ref, low_ref in ((right + left, ev_ref, ev_low_ref), (right - left, od_ref, od_low_ref)):
                top = value.astype(jnp.bfloat16)
                ref[at, :half] = top
                ref[at, half:] = top
                low_ref[at] = (value - top.astype(jnp.float32)).astype(jnp.bfloat16)


def project_chunk(split_refs, cos_ref, sin_ref, phase_ref, cut, pairs):
    ev_ref, ev_low_ref, od_ref, od_low_ref = split_refs
    half = ev_low_ref.shape[1]
    dot = partial(jnp.dot, preferred_element_type=jnp.float32)
    part_c = dot(ev_ref[...], cos_ref[:, cut]) + dot(ev_low_ref[...], cos_ref[:half, cut])
    part_s = dot(od_ref[...], sin_ref[:, cut]) + dot(od_low_ref[...], sin_ref[:half, cut])
    real = [0.0, 0.0]
    imag = [0.0, 0.0]
    for turn, v in enumerate(pairs):
        cos_x = phase_ref[v : v + 1, cut]
        sin_x = phase_ref[8 + v : 9 + v, cut]
        for n in range(2):
            same = slice((turn * 4 + n) * 8, (turn * 4 + n) * 8 + 8)
            flip = slice((turn * 4 + 2 + n) * 8, (turn * 4 + 2 + n) * 8 + 8)
            real[n] = real[n] + (cos_x * part_c[same] - sin_x * part_s[flip])
            imag[n] = imag[n] + (cos_x * part_s[same] + sin_x * part_c[flip])
    sum_real = 0.0
    sum_imag = 0.0
    for n in range(2):
        cos_n, sin_n = math.cos(OMEGA * (n + 1)), math.sin(OMEGA * (n + 1))
        sum_real = sum_real + (cos_n * real[n] + sin_n * imag[n])
        sum_imag = sum_imag + (cos_n * imag[n] - sin_n * real[n])
    cos_c, sin_c = phase_ref[16:24, cut], phase_ref[24:32, cut]
    return sum_real * cos_c - sum_imag * sin_c, sum_real * sin_c + sum_imag * cos_c


def split_shapes(pairs, width):
    count = 32 * len(pairs)
    return [(count, width), (count, width // 2)] * 2


def inside_body(h1_ref, e1_ref, g_ref, k_ref, surface_ref, cos_ref, sin_ref, phase_ref, out_ref, plane_ref, *split_refs, pairs):
    _, levels, rows, _ = h1_ref.shape
    width = g_ref.shape[3]
    wide = (rows, h1_ref.shape[3])
    keep = kept_lanes(wide, width)
    zero_row = jnp.zeros((1, wide[1]), jnp.float32)
    zero = jnp.zeros(wide, jnp.float32)

    def second(z):
        above = [e1_ref[i, z + 1] for i in range(2)] if z + 1 < levels else [zero, zero]
        here = [e1_ref[i, z] for i in range(3)]
        return magnetic(here, above, [h1_ref[i, z] for i in range(3)], zero_row, zero_row, keep)

    for layer, z in enumerate((0, levels - 1)):
        h2 = second(z)
        below = second(z - 1)[:2] if z else [zero, zero]
        curl = curl_back(h2, below, zero_row, zero_row)
        for i in range(2):
            store_plane(plane_ref, surface_ref, 0, layer, i, e1_ref[i, z])
            store_plane(plane_ref, surface_ref, 0, layer, 2 + i, h1_ref[i, z])
            new = k_ref[1, z] * e1_ref[i, z, :, :width] + k_ref[0, z] * curl[i][:, :width] - g_ref[i, z]
            store_plane(plane_ref, surface_ref, 1, layer, i, new)
            store_plane(plane_ref, surface_ref, 1, layer, 2 + i, h2[i])
    split_planes(plane_ref, split_refs, rows, pairs)
    chunk = 256
    for at in range(0, out_ref.shape[1], chunk):
        cut = slice(at, at + chunk)
        out_ref[0:8, cut], out_ref[8:16, cut] = project_chunk(split_refs, cos_ref, sin_ref, phase_ref, cut, pairs)


def inside(h1, e1, late, factors, surface, cos_y, sin_y, phases):
    _, _, rows, width = late.shape
    pairs = range(rows // 2 - 2)
    count = cos_y.shape[1]
    return pl.pallas_call(
        partial(inside_body, pairs=pairs),
        out_shape=jax.ShapeDtypeStruct((16, count), jnp.float32),
        scratch_shapes=[pltpu.VMEM((2, 16 * rows, width // 2), jnp.float32)]
        + [pltpu.VMEM(shape, jnp.bfloat16) for shape in split_shapes(pairs, width)],
        compiler_params=VMEM,
        cost_estimate=pl.CostEstimate(
            flops=8 * 32 * len(pairs) * width * count, bytes_accessed=4 * width * count, transcendentals=0
        ),
        name="inside",
    )(h1, e1, late, factors, surface, cos_y, sin_y, phases)


def second_body(h1_in, e1_in, g_ref, k_ref, surface_ref, own_one_ref, own_two_ref, x_one_ref, x_two_ref, e_out, h_out,
                ev_ref, ev_low_ref, od_ref, od_low_ref, h1_ref, e1_ref, h2_ref, plane_ref, *, pairs):
    _, levels, rows, _ = h1_in.shape
    width = g_ref.shape[3]
    wide = (rows, h1_in.shape[3])
    keep = kept_lanes(wide, width)
    keep_row = kept_lanes((1, wide[1]), width)
    zero_row = jnp.zeros((1, wide[1]), jnp.float32)
    zero = jnp.zeros(wide, jnp.float32)
    at_row = row_index(wide)
    place, count = lax.axis_index("gx"), lax.axis_size("gx")
    even = lax.rem(place, 2) == 0
    has_before, has_after = place > 0, place < count - 1
    first, end = slice(0, 1), slice(rows - 1, rows)
    layers = {0: 0, levels - 1: 1}

    def from_before(k, z):
        got = jnp.where(even, x_two_ref[k, z : z + 1], x_one_ref[k, z : z + 1])
        return jnp.where(has_before, got, 0.0)

    def from_after(k, z):
        got = jnp.where(even, x_one_ref[k, z : z + 1], x_two_ref[k, z : z + 1])
        return jnp.where(has_after, got, 0.0)

    def own_up(k, z):
        return jnp.where(even, own_one_ref[k, z : z + 1], own_two_ref[k, z : z + 1])

    def own_down(k, z):
        return jnp.where(even, own_two_ref[k, z : z + 1], own_one_ref[k, z : z + 1])

    def patched(value, start, stop):
        if start is not None:
            value = jnp.where(at_row == 0, value + start, value)
        return jnp.where(at_row == rows - 1, value + stop, value)

    diff_y = [jnp.where(has_before, COURANT * own_down(1, z), 0.0) for z in range(levels)]
    diff_z = [jnp.where(has_before, -COURANT * own_down(0, z), 0.0) for z in range(levels)]
    last_y = [COURANT * from_after(1, z) for z in range(levels)]
    last_z = [-COURANT * from_after(0, z) for z in range(levels)]
    for z in range(levels):
        h1 = [h1_in[0, z], patched(h1_in[1, z], None, last_y[z]), patched(h1_in[2, z], None, last_z[z])]
        low = last_y[z - 1] if z else zero_row
        inv, inv_first = own_up(4, z), own_down(4, z)
        stop_x = inv * ((last_z[z] - behind_y(last_z[z])) - (last_y[z] - low))
        start_y = inv_first * (from_before(1, z) + diff_z[z])
        start_z = -inv_first * (from_before(0, z) + diff_y[z])
        e1 = [
            patched(e1_in[0, z], None, stop_x),
            patched(e1_in[1, z], start_y, -inv * last_z[z]),
            patched(e1_in[2, z], start_z, inv * last_y[z]),
        ]
        for i in range(3):
            h1_ref[i, z] = h1[i]
            e1_ref[i, z] = e1[i]
        if z in layers:
            for i in range(2):
                store_plane(plane_ref, surface_ref, 0, layers[z], i, e1[i])
                store_plane(plane_ref, surface_ref, 0, layers[z], 2 + i, h1[i])

    for z in range(levels):
        above = [e1_ref[i, z + 1] for i in range(2)] if z + 1 < levels else [zero, zero]
        inv = from_after(4, z)
        row_y = from_after(2, z) + inv * h1_ref[2, z, end]
        row_z = from_after(3, z) - inv * h1_ref[1, z, end]
        new = magnetic(
            [e1_ref[i, z] for i in range(3)], above, [h1_ref[i, z] for i in range(3)], row_y, row_z, keep
        )
        for i in range(3):
            h2_ref[i, z] = new[i]
            h_out[i, z] = new[i][:, :width]
        if z in layers:
            for i in range(2):
                store_plane(plane_ref, surface_ref, 1, layers[z], 2 + i, new[i])

    inv_before = [from_before(4, z) for z in range(levels)]
    diff_ex = []
    for z in range(levels):
        low = diff_y[z - 1] if z else zero_row
        diff_ex.append(inv_before[z] * ((diff_z[z] - behind_y(diff_z[z])) - (diff_y[z] - low)))
    for z in range(levels):
        below = [h2_ref[i, z - 1] for i in range(2)] if z else [zero, zero]
        up = diff_ex[z + 1] if z + 1 < levels else zero_row
        diff_ey = -inv_before[z] * diff_z[z]
        diff_ez = inv_before[z] * diff_y[z]
        row_y = from_before(2, z) + diff_y[z] - COURANT * ((up - diff_ex[z]) - (e1_ref[2, z, first] - diff_ez))
        row_z = from_before(3, z) + diff_z[z] - COURANT * (
            (e1_ref[1, z, first] - diff_ey) - (ahead_y(diff_ex[z]) - diff_ex[z])
        )
        open_row = keep_row & has_before
        row_y = jnp.where(open_row, row_y, 0.0)
        row_z = jnp.where(open_row, row_z, 0.0)
        curl = curl_back([h2_ref[i, z] for i in range(3)], below, row_y, row_z)
        for i in range(3):
            new = k_ref[1, z] * e1_ref[i, z, :, :width] + k_ref[0, z] * curl[i][:, :width] - g_ref[i, z]
            e_out[i, z] = new
            if i < 2 and z in layers:
                store_plane(plane_ref, surface_ref, 1, layers[z], i, new)
    split_planes(plane_ref, (ev_ref, ev_low_ref, od_ref, od_low_ref), rows, pairs)


def edge_pairs(rows):
    return range(rows // 2 - 2, rows // 2)


def second_step(h1, e1, late, factors, surface, own_one, own_two, x_one, x_two):
    _, _, rows, width = late.shape
    pairs = edge_pairs(rows)
    field = jax.ShapeDtypeStruct(late.shape, jnp.float32)
    store = pltpu.VMEM(h1.shape, jnp.float32)
    return pl.pallas_call(
        partial(second_body, pairs=pairs),
        out_shape=(field, field)
        + tuple(jax.ShapeDtypeStruct(shape, jnp.bfloat16) for shape in split_shapes(pairs, width)),
        scratch_shapes=[store, store, store, pltpu.VMEM((2, 16 * rows, width // 2), jnp.float32)],
        compiler_params=VMEM,
        name="second_step",
    )(h1, e1, late, factors, surface, own_one, own_two, x_one, x_two)


def table_body(waves_ref, tie_ref, cos_ref, sin_ref, phase_ref, *, rows, width, scale):
    del tie_ref
    half = width // 2
    chunk = 256
    step = (row_index((8, chunk)).astype(jnp.float32)) + 0.5
    centre_x = (lax.axis_index("gx") * rows).astype(jnp.float32) + 0.5 * (rows - 1)
    centre_y = (lax.axis_index("gy") * width).astype(jnp.float32) + 0.5 * (width - 1)

    @pl.loop(0, waves_ref.shape[1] // chunk)
    def _(turn):
        cut = pl.ds(pl.multiple_of(turn * chunk, chunk), chunk)
        wave_x, wave_y = WAVE * waves_ref[0:1, cut], WAVE * waves_ref[1:2, cut]
        sin_x, cos_x = sincos(wave_x * step)
        phase_ref[0:8, cut] = cos_x
        phase_ref[8:16, cut] = sin_x
        sin_c, cos_c = sincos(wave_x * centre_x + wave_y * centre_y)
        phase_ref[16:24, cut] = jnp.broadcast_to(scale * cos_c, step.shape)
        phase_ref[24:32, cut] = jnp.broadcast_to(scale * sin_c, step.shape)
        sin_y, cos_y = sincos(wave_y * step)
        sin_w, cos_w = sincos(wave_y * 8.0)
        cos_y = jnp.concatenate([cos_y, cos_y * cos_w - sin_y * sin_w], axis=0)
        sin_y = jnp.concatenate([sin_y, sin_y * cos_w + cos_y[0:8] * sin_w], axis=0)
        sin_w, cos_w = 2.0 * sin_w * cos_w, 1.0 - 2.0 * sin_w * sin_w
        for start in range(0, half, 16):
            if start:
                cos_y, sin_y = cos_y * cos_w - sin_y * sin_w, sin_y * cos_w + cos_y * sin_w
            for value, ref in ((cos_y, cos_ref), (sin_y, sin_ref)):
                top = value.astype(jnp.bfloat16)
                ref[start : start + 16, cut] = top
                ref[half + start : half + start + 16, cut] = (value - top.astype(jnp.float32)).astype(jnp.bfloat16)


def tables(waves, tie, rows, width, scale):
    count = waves.shape[1]
    table = jax.ShapeDtypeStruct((width, count), jnp.bfloat16)
    return pl.pallas_call(
        partial(table_body, rows=rows, width=width, scale=scale),
        out_shape=(table, table, jax.ShapeDtypeStruct((32, count), jnp.float32)),
        in_specs=[pl.BlockSpec(memory_space=pltpu.VMEM), pl.BlockSpec(memory_space=pl.ANY)],
        compiler_params=VMEM,
        cost_estimate=pl.CostEstimate(flops=40 * width * count, bytes_accessed=4 * width * count, transcendentals=0),
        name="tables",
    )(waves, tie)


def project_body(ev_ref, ev_low_ref, od_ref, od_low_ref, cos_ref, sin_ref, phase_ref, inner_ref, out_ref, *, start, pairs):
    chunk = 256
    for at in range(0, out_ref.shape[1], chunk):
        cut, to = slice(start + at, start + at + chunk), slice(at, at + chunk)
        real, imag = project_chunk(
            (ev_ref, ev_low_ref, od_ref, od_low_ref), cos_ref, sin_ref, phase_ref, cut, pairs
        )
        out_ref[0:8, to] = real + inner_ref[0:8, cut]
        out_ref[8:16, to] = imag + inner_ref[8:16, cut]


def project(planes, cos_y, sin_y, phases, inner, rows, start, count):
    width = cos_y.shape[0]
    return pl.pallas_call(
        partial(project_body, start=start, pairs=edge_pairs(rows)),
        out_shape=jax.ShapeDtypeStruct((16, count), jnp.float32),
        compiler_params=VMEM,
        cost_estimate=pl.CostEstimate(
            flops=8 * planes[0].shape[0] * width * count, bytes_accessed=4 * width * count, transcendentals=0
        ),
        name="project",
    )(*planes, cos_y, sin_y, phases, inner)


def swap(array, axis, mask):
    return lax.ppermute(array, axis, [(i, i ^ mask) for i in range(lax.axis_size(axis))])


def swap_other(array, axis):
    pairs = [(i, ((i + 1) ^ 1) - 1) for i in range(1, lax.axis_size(axis) - 1)]
    return lax.ppermute(array, axis, pairs)


def group_of(axis):
    return min(lax.axis_size(axis), 4)


def own_first(directions):
    count_x, count_y = lax.axis_size("gx"), lax.axis_size("gy")
    group = group_of("gx")
    waves = directions.T.reshape(2, count_x // group, group, count_y // 2, 2, -1)
    place_x, place_y = lax.axis_index("gx"), lax.axis_index("gy")
    waves = jnp.where(place_y % 2 == 1, jnp.flip(waves, 4), waves)
    waves = lax.dynamic_slice_in_dim(jnp.concatenate([waves, waves], axis=2), place_x % group, group, axis=2)
    waves = exclusive(waves, 1, place_x // group)
    waves = exclusive(waves, 3, place_y // 2)
    return waves.transpose(0, 4, 1, 2, 3, 5).reshape(2, directions.shape[0])


def exclusive(array, axis, place):
    size = array.shape[axis]
    bit = 1
    while bit < size:
        pieces = jnp.split(array, size // bit, axis)
        turned = jnp.concatenate([pieces[i ^ 1] for i in range(len(pieces))], axis)
        array = jnp.where(place & bit, turned, array)
        bit = 2 * bit
    return array


def halve(far, axis, mask):
    half = far.shape[1] // 2
    return far[:, :half] + swap(far[:, half:], axis, mask)


def halve_all(far, axis, low, size):
    mask = size // 2
    while mask >= 1:
        far = halve(far, axis, mask * low)
        mask = mask // 2
    return far


def scatter_group(far, axis):
    count, group = lax.axis_size(axis), group_of(axis)
    part = far.shape[1] // group
    total = far[:, :part]
    got = []
    for step in sorted(range(1, group), key=lambda step: (step != group // 2, step)):
        pairs = [(i, i // group * group + (i + step) % group) for i in range(count)]
        got.append(lax.ppermute(far[:, step * part : (step + 1) * part], axis, pairs))
    for array in got:
        total = total + array
    return total


def local(e_field, h_field, pol_now, pol_old, eps_inf, materials, surface, poles, directions):
    _, _, rows, width = e_field.shape
    scale = 1.0 / math.sqrt(rows * lax.axis_size("gx") * width * lax.axis_size("gy"))
    one, two, near, late, factors, e_field, h_field = prepare(e_field, h_field, pol_now, pol_old, eps_inf, materials, poles)
    tie = factors
    one = swap(one, "gy", 1)
    two = swap_other(two, "gy")
    cos_y, sin_y, phases = tables(own_first(directions), tie, rows, width, scale)
    own_one, own_two, h1, e1 = first_step(e_field, h_field, near, factors, one, two, phases)
    x_one = swap(own_one, "gx", 1)
    x_two = swap_other(own_two, "gx")
    inner = inside(h1, e1, late, factors, surface, cos_y, sin_y, phases)
    e_new, h_new, *planes = second_step(h1, e1, late, factors, surface, own_one, own_two, x_one, x_two)
    half = directions.shape[0] // 2
    far = project(planes, cos_y, sin_y, phases, inner, rows, half, half)
    arrived = swap(far, "gy", 1)
    far = project(planes, cos_y, sin_y, phases, inner, rows, 0, half) + arrived
    far = halve_all(far, "gx", group_of("gx"), lax.axis_size("gx") // group_of("gx"))
    far = scatter_group(far, "gx")
    far = halve_all(far, "gy", 2, lax.axis_size("gy") // 2)
    return e_new, h_new, far.T


def solution(mesh):
    field = P("design", None, "gx", "gy")
    cell = P("design", "gx", "gy")
    return jax.shard_map(
        local,
        mesh=mesh,
        in_specs=(field, field, field, field, cell, cell, cell, P(), P()),
        out_specs=(field, field, P(("gx", "gy"), "design")),
        check_vma=False,
    )
```

time: 36.8 us -> 33.4 us (0.908)
  waiting for transfers between devices: 7.29 us -> 4.56 us
  starting transfers between devices: 17.3 us -> 16.2 us
  Pallas kernels: 9.37 us -> 9.88 us
    ppermute x6 -> x4, starting transfers between devices: 16 us -> 8.03 us  [swap(): lax.ppermute(array, axis, [(i, i ^ mask) for i in range(lax.axis_size(axi...]
    ppermute x0 -> x3, starting transfers between devices: none -> 6.89 us  [scatter_group(): got.append(lax.ppermute(far[:, step * part:(step + 1) * part], axis, pairs))]
    ppermute x6 -> x4, waiting for transfers between devices: 7.29 us -> 2.02 us  [swap(): lax.ppermute(array, axis, [(i, i ^ mask) for i in range(lax.axis_size(axi...]
    ppermute x0 -> x3, waiting for transfers between devices: none -> 2.53 us  [scatter_group(): got.append(lax.ppermute(far[:, step * part:(step + 1) * part], axis, pairs))]
    pallas_call x4 -> x5, Pallas kernels: 5.07 us -> 5.54 us  [the longest x1 2.04 us: inside(): pl.pallas_call(partial(inside_body, pairs=pairs), out_shape=jax.ShapeDtyp...]
  transfers between devices with their start and end apart: 8 -> 9, of which waited for: 3 -> 4; matrix products, arithmetic and copies ran while one was open for 3% -> 3% of each run, Pallas kernels for 8% -> 13%
where the time goes in v3:
time: 33.4 us; the launch traced here: 33.2 us
  starting transfers between devices  16.2 us (49%)
  Pallas kernels  9.88 us (30%)
  waiting for transfers between devices  4.56 us (14%)
  local copies, waits for them, and re-layouts  0.9 us (3%)
  between operations  0.88 us (3%)
  other arithmetic  0.75 us (2%)
    ppermute x4, starting transfers between devices, swap(): lax.ppermute(array, axis, [(i, i ^ mask) for i in range(lax.axis_size(axi...  8.03 us
    ppermute x3, starting transfers between devices, scatter_group(): got.append(lax.ppermute(far[:, step * part:(step + 1) * part], axis, pairs))  6.89 us
    pallas_call x1, Pallas kernels, prepare(): pl.pallas_call(prepare_body, out_shape=(message, message, field, field, p...  2.59 us
    ppermute x3, waiting for transfers between devices, scatter_group(): got.append(lax.ppermute(far[:, step * part:(step + 1) * part], axis, pairs))  2.53 us
    pallas_call x1, Pallas kernels, inside(): pl.pallas_call(partial(inside_body, pairs=pairs), out_shape=jax.ShapeDtyp...  2.04 us
    ppermute x4, waiting for transfers between devices, swap(): lax.ppermute(array, axis, [(i, i ^ mask) for i in range(lax.axis_size(axi...  2.02 us
    pallas_call x1, Pallas kernels, tables(): pl.pallas_call(partial(table_body, rows=rows, width=width, scale=scale),...  1.75 us
    pallas_call x2, Pallas kernels, project(): pl.pallas_call(partial(project_body, start=start, pairs=edge_pairs(rows))...  1.36 us
  transfers between devices with their start and end apart: 9, of which 4 were waited for; matrix products, arithmetic and copies ran while one was open for 3% of the time, Pallas kernels for 13%

profile of v3, /device:TPU:0, one launch (start us, length us, event | category | flops | bytes accessed | tf_op | source)
XLA Modules:
  0.0 33.2 jit_solution(8977666503473134998)
XLA Ops:
  0.6 0.0 copy-start
  0.6 2.6 %prepare.1 = (f32[24,128]{1,0:T(8,128)S(1)}, f32[24,128]{1,0:T(8,128)S(1)}, f32[3,8,16,256]{3,2,1,0:T(8,128)S(1)}, f32[3,8,16,256]{3,2,1,0:T(8,128)S(1)}, f32[2,...) custom-call(f32[3,8,16,256]{3,2,1,0:T(8,128)} %e_in.1, ...), custom_call_target="tpu_custom_call" | custom-call | tf_op jit(solution)/shard_map/prepare/pallas_call | solution.py:117
  3.2 0.5 %collective-permute-start = (f32[24,128]{1,0:T(8,128)S(1)}, f32[24,128]{1,0:T(8,128)S(1)}, u32[]{:S(2)}, u32[]{:S(2)}) collective-permute-start(f32[24,128]{1,0:T(8,128)S(1)} %get-tuple-element.27), channel_id=1, source_target_pairs={{0,1},{1,0},{2,3},{3,2},{4,5},{5,4},{6,7},{7,6},{8,9},{9,8},{10,11... | collective-permute-start | bytes 36872 | tf_op jit(solution)/shard_map/ppermute | solution.py:550
  3.8 0.7 %collective-permute-start.1 = (f32[24,128]{1,0:T(8,128)S(1)}, f32[24,128]{1,0:T(8,128)S(1)}, u32[]{:S(2)}, u32[]{:S(2)}) collective-permute-start(f32[24,128]{1,0:T(8,128)S(1)} %get-tuple-element.28), channel_id=1, source_target_pairs={{1,2},{2,1},{5,6},{6,5},{9,10},{10,9},{13,14},{14,13},{17,18},{18,... | collective-permute-start | bytes 36872 | tf_op jit(solution)/shard_map/ppermute | solution.py:555
  4.4 0.8 %reshape.12 = f32[2,1,4,2,2,256]{5,4,3,2,0,1:T(2,128)S(1)} reshape(f32[2,4096]{1,0:T(2,128)} %bitcast.7) | data formatting | bytes 65536 | tf_op jit(solution)/shard_map/reshape | solution.py:565
  5.4 0.1 fusion.3
  5.5 1.7 %tables.1 = (bf16[256,4096]{1,0:T(8,128)(2,1)S(1)}, bf16[256,4096]{1,0:T(8,128)(2,1)S(1)}, f32[32,4096]{1,0:T(8,128)S(1)}) custom-call(f32[2,4096]{1,0:T(2,128)S(1)} %reshape.13.waves_ref, f32[2,8,16,256]{3,2,1,0:T(8,128)S(1)} %get-tuple-element.26.tie_ref.k_ref), custom_call_target="tpu_custom_call" | custom-call | flops 41943040 | bytes 4194304 | tf_op jit(solution)/shard_map/tables/pallas_call | solution.py:515
  7.3 0.0 collective-permute-done.one_ref
  7.3 0.0 collective-permute-done.1.two_ref
  7.3 0.8 %first_step.1 = (f32[5,8,384]{2,1,0:T(8,128)S(1)}, f32[5,8,384]{2,1,0:T(8,128)S(1)}, f32[3,8,16,384]{3,2,1,0:T(8,128)S(1)}, f32[3,8,16,384]{3,2,1,0:T(8,128)S(1)}) custom-call(f32[3,8,16,256]{3,2,1,0:T(8,128)S(1)} %get-tuple-element.23.e_ref, f32[3,8,16,256]{3,2,1,0:T(8,128)S(1)} %get-tuple-element.24.h_ref, f32[3,8,16,256]{3,2,1,0:T(8,128)S(1)} %get-tuple-element.25.d_ref, ...), custom_call_target="tpu_custom_call" | custom-call | tf_op jit(solution)/shard_map/first_step/pallas_call | solution.py:246
  8.1 2.7 %collective-permute-start.2 = (f32[5,8,384]{2,1,0:T(8,128)S(1)}, f32[5,8,384]{2,1,0:T(8,128)S(1)}, u32[]{:S(2)}, u32[]{:S(2)}) collective-permute-start(f32[5,8,384]{2,1,0:T(8,128)S(1)} %get-tuple-element.33.own_one_ref), channel_id=1, source_target_pairs={{0,4},{4,0},{8,12},{12,8},{1,5},{5,1},{9,13},{13,9},{2,6},{6,2},{1... | collective-permute-start | bytes 184328 | tf_op jit(solution)/shard_map/ppermute | solution.py:550
  10.8 0.7 %collective-permute-start.3 = (f32[5,8,384]{2,1,0:T(8,128)S(1)}, f32[5,8,384]{2,1,0:T(8,128)S(1)}, u32[]{:S(2)}, u32[]{:S(2)}) collective-permute-start(f32[5,8,384]{2,1,0:T(8,128)S(1)} %get-tuple-element.34.own_two_ref), channel_id=1, source_target_pairs={{4,8},{8,4},{5,9},{9,5},{6,10},{10,6},{7,11},{11,7},{20,24},{24,20... | collective-permute-start | bytes 184328 | tf_op jit(solution)/shard_map/ppermute | solution.py:555
  11.4 0.0 copy-done
  11.4 2.0 %inside.1.inner_ref = f32[16,4096]{1,0:T(8,128)S(1)} custom-call(f32[3,8,16,384]{3,2,1,0:T(8,128)S(1)} %get-tuple-element.30.h1_in.h1_ref, f32[3,8,16,384]{3,2,1,0:T(8,128)S(1)} %get-tuple-element.31.e1_in.e1_ref, f32[3,8,16,256]{3,2,1,0:T(8,128)S(1)} %get-tuple-element.32.g_ref, f32[2,8,16,256]{3,2,1,0:T(8,128)S(1)} %get-tuple-element.26.tie_ref.k_ref, ...), custom_call_target="tpu_custom_call" | custom-call | flops 1610612736 | bytes 4194304 | tf_op jit(solution)/shard_map/inside/pallas_call | solution.py:348
  13.5 0.0 collective-permute-done.2.x_one_ref
  13.5 0.0 collective-permute-done.3.x_two_ref
  13.5 1.3 %second_step.1 = (f32[3,8,16,256]{3,2,1,0:T(8,128)}, f32[3,8,16,256]{3,2,1,0:T(8,128)}, bf16[64,256]{1,0:T(8,128)(2,1)S(1)}, bf16[64,128]{1,0:T(8,128)(2,1)S(1)}...) custom-call(f32[3,8,16,384]{3,2,1,0:T(8,128)S(1)} %get-tuple-element.30.h1_in.h1_ref, ...), custom_call_target="tpu_custom_call" | custom-call | tf_op jit(solution)/shard_map/second_step/pallas_call | solution.py:470
  14.9 0.7 %project.3 = f32[16,2048]{1,0:T(8,128)S(1)} custom-call(bf16[64,256]{1,0:T(8,128)(2,1)S(1)} %get-tuple-element.37.ev_ref, bf16[64,128]{1,0:T(8,128)(2,1)S(1)} %get-tuple-element.38.ev_low_ref, bf16[64,256]{1,0:T(8,128)(2,1)S(1)} %get-tuple-element.39.od_ref, bf16[64,128]{1,0:T(8,128)(2,1)S(1)} %get-tuple-element.40.od_low_ref, ...), custom_call_target="tpu_custom_call" | custom-call | flops 268435456 | bytes 2097152 | tf_op jit(solution)/shard_map/project/pallas_call | solution.py:538
  15.5 2.6 %collective-permute-start.4 = (f32[16,2048]{1,0:T(8,128)S(1)}, f32[16,2048]{1,0:T(8,128)S(1)}, u32[]{:S(2)}, u32[]{:S(2)}) collective-permute-start(f32[16,2048]{1,0:T(8,128)S(1)} %project.3), channel_id=1, source_target_pairs={{0,1},{1,0},{2,3},{3,2},{4,5},{5,4},{6,7},{7,6},{8,9},{9,8},{10,11... | collective-permute-start | bytes 393224 | tf_op jit(solution)/shard_map/ppermute | solution.py:550
  18.2 0.7 %project.2 = f32[16,2048]{1,0:T(8,128)S(1)} custom-call(bf16[64,256]{1,0:T(8,128)(2,1)S(1)} %get-tuple-element.37.ev_ref, bf16[64,128]{1,0:T(8,128)(2,1)S(1)} %get-tuple-element.38.ev_low_ref, bf16[64,256]{1,0:T(8,128)(2,1)S(1)} %get-tuple-element.39.od_ref, bf16[64,128]{1,0:T(8,128)(2,1)S(1)} %get-tuple-element.40.od_low_ref, ...), custom_call_target="tpu_custom_call" | custom-call | flops 268435456 | bytes 2097152 | tf_op jit(solution)/shard_map/project/pallas_call | solution.py:538
  18.9 0.3 collective-permute-done.4
  19.2 2.7 %collective-permute-start.7 = (f32[16,512]{1,0:T(8,128)S(1)}, f32[16,512]{1,0:T(8,128)S(1)}, u32[]{:S(2)}, u32[]{:S(2)}) collective-permute-start(f32[16,512]{1,0:T(8,128)S(1)} %get-tuple-element.44), channel_id=1, source_target_pairs={{0,12},{4,0},{8,4},{12,8},{1,13},{5,1},{9,5},{13,9},{2,14},{6,2},{... | collective-permute-start | bytes 98312 | tf_op jit(solution)/shard_map/ppermute | solution.py:605
  21.9 1.5 %collective-permute-start.6 = (f32[16,512]{1,0:T(8,128)S(1)}, f32[16,512]{1,0:T(8,128)S(1)}, u32[]{:S(2)}, u32[]{:S(2)}) collective-permute-start(f32[16,512]{1,0:T(8,128)S(1)} %get-tuple-element.45), channel_id=1, source_target_pairs={{0,4},{4,8},{8,12},{12,0},{1,5},{5,9},{9,13},{13,1},{2,6},{6,10},{... | collective-permute-start | bytes 98312 | tf_op jit(solution)/shard_map/ppermute | solution.py:605
  23.5 2.6 %collective-permute-start.5 = (f32[16,512]{1,0:T(8,128)S(1)}, f32[16,512]{1,0:T(8,128)S(1)}, u32[]{:S(2)}, u32[]{:S(2)}) collective-permute-start(f32[16,512]{1,0:T(8,128)S(1)} %get-tuple-element.43), channel_id=1, source_target_pairs={{0,8},{4,12},{8,0},{12,4},{1,9},{5,13},{9,1},{13,5},{2,10},{6,14},... | collective-permute-start | bytes 98312 | tf_op jit(solution)/shard_map/ppermute | solution.py:605
  26.1 0.0 collective-permute-done.7
  26.1 1.8 %collective-permute-done.6 = f32[16,512]{1,0:T(8,128)S(1)} collective-permute-done((f32[16,512]{1,0:T(8,128)S(1)}, f32[16,512]{1,0:T(8,128)S(1)}, u32[]{:S(2)}, u32[]{:S(2)}) %collective-permute-start.6) | collective-permute-done | bytes 32800 | tf_op jit(solution)/shard_map/ppermute | solution.py:605
  27.8 0.8 %collective-permute-done.5 = f32[16,512]{1,0:T(8,128)S(1)} collective-permute-done((f32[16,512]{1,0:T(8,128)S(1)}, f32[16,512]{1,0:T(8,128)S(1)}, u32[]{:S(2)}, u32[]{:S(2)}) %collective-permute-start.5) | collective-permute-done | bytes 32800 | tf_op jit(solution)/shard_map/ppermute | solution.py:605
  28.6 2.2 %collective-permute-start.8 = (f32[16,256]{1,0:T(8,128)S(1)}, f32[16,256]{1,0:T(8,128)S(1)}, u32[]{:S(2)}, u32[]{:S(2)}) collective-permute-start(f32[16,256]{1,0:T(8,128)S(1)} %slice.29), channel_id=1, source_target_pairs={{0,2},{1,3},{2,0},{3,1},{4,6},{5,7},{6,4},{7,5},{8,10},{9,11},{10,... | collective-permute-start | bytes 49160 | tf_op jit(solution)/shard_map/ppermute | solution.py:550
  30.9 1.7 %collective-permute-done.8 = f32[16,256]{1,0:T(8,128)S(1)} collective-permute-done((f32[16,256]{1,0:T(8,128)S(1)}, f32[16,256]{1,0:T(8,128)S(1)}, u32[]{:S(2)}, u32[]{:S(2)}) %collective-permute-start.8) | collective-permute-done | bytes 16416 | tf_op jit(solution)/shard_map/ppermute | solution.py:550
  32.6 0.6 %fusion.4 = f32[256,16]{0,1:T(8,128)} fusion(f32[16,256]{1,0:T(8,128)S(1)} %collective-permute-done.8, f32[16,512]{1,0:T(8,128)S(1)} %fusion.2), kind=kLoop, calls=%fused_computation.10 | loop fusion | flops 4096 | bytes 49152 | tf_op jit(solution)/shard_map/transpose | solution.py:631
  (9 shorter events, 0.2 us)
Async XLA Ops:
  0.6 10.8 %copy-start = (s32[2,16,256]{2,1,0:T(8,128)S(1)}, s32[2,16,256]{2,1,0:T(8,128)}, u32[]{:S(2)}) copy-start(s32[2,16,256]{2,1,0:T(8,128)} %surface_ref.3) | copy-start | bytes 98308
  3.2 4.0 %collective-permute-start = (f32[24,128]{1,0:T(8,128)S(1)}, f32[24,128]{1,0:T(8,128)S(1)}, u32[]{:S(2)}, u32[]{:S(2)}) collective-permute-start(f32[24,128]{1,0:T(8,128)S(1)} %get-tuple-element.27), channel_id=1, source_target_pairs={{0,1},{1,0},{2,3},{3,2},{4,5},{5,4},{6,7},{7,6},{8,9},{9,8},{10,11... | collective-permute-start | bytes 36872 | tf_op jit(solution)/shard_map/ppermute | solution.py:550
  3.8 3.5 %collective-permute-start.1 = (f32[24,128]{1,0:T(8,128)S(1)}, f32[24,128]{1,0:T(8,128)S(1)}, u32[]{:S(2)}, u32[]{:S(2)}) collective-permute-start(f32[24,128]{1,0:T(8,128)S(1)} %get-tuple-element.28), channel_id=1, source_target_pairs={{1,2},{2,1},{5,6},{6,5},{9,10},{10,9},{13,14},{14,13},{17,18},{18,... | collective-permute-start | bytes 36872 | tf_op jit(solution)/shard_map/ppermute | solution.py:555
  8.1 5.4 %collective-permute-start.2 = (f32[5,8,384]{2,1,0:T(8,128)S(1)}, f32[5,8,384]{2,1,0:T(8,128)S(1)}, u32[]{:S(2)}, u32[]{:S(2)}) collective-permute-start(f32[5,8,384]{2,1,0:T(8,128)S(1)} %get-tuple-element.33.own_one_ref), channel_id=1, source_target_pairs={{0,4},{4,0},{8,12},{12,8},{1,5},{5,1},{9,13},{13,9},{2,6},{6,2},{1... | collective-permute-start | bytes 184328 | tf_op jit(solution)/shard_map/ppermute | solution.py:550
  10.8 2.7 %collective-permute-start.3 = (f32[5,8,384]{2,1,0:T(8,128)S(1)}, f32[5,8,384]{2,1,0:T(8,128)S(1)}, u32[]{:S(2)}, u32[]{:S(2)}) collective-permute-start(f32[5,8,384]{2,1,0:T(8,128)S(1)} %get-tuple-element.34.own_two_ref), channel_id=1, source_target_pairs={{4,8},{8,4},{5,9},{9,5},{6,10},{10,6},{7,11},{11,7},{20,24},{24,20... | collective-permute-start | bytes 184328 | tf_op jit(solution)/shard_map/ppermute | solution.py:555
  15.5 3.6 %collective-permute-start.4 = (f32[16,2048]{1,0:T(8,128)S(1)}, f32[16,2048]{1,0:T(8,128)S(1)}, u32[]{:S(2)}, u32[]{:S(2)}) collective-permute-start(f32[16,2048]{1,0:T(8,128)S(1)} %project.3), channel_id=1, source_target_pairs={{0,1},{1,0},{2,3},{3,2},{4,5},{5,4},{6,7},{7,6},{8,9},{9,8},{10,11... | collective-permute-start | bytes 393224 | tf_op jit(solution)/shard_map/ppermute | solution.py:550
  19.2 6.9 %collective-permute-start.7 = (f32[16,512]{1,0:T(8,128)S(1)}, f32[16,512]{1,0:T(8,128)S(1)}, u32[]{:S(2)}, u32[]{:S(2)}) collective-permute-start(f32[16,512]{1,0:T(8,128)S(1)} %get-tuple-element.44), channel_id=1, source_target_pairs={{0,12},{4,0},{8,4},{12,8},{1,13},{5,1},{9,5},{13,9},{2,14},{6,2},{... | collective-permute-start | bytes 98312 | tf_op jit(solution)/shard_map/ppermute | solution.py:605
  21.9 5.9 %collective-permute-start.6 = (f32[16,512]{1,0:T(8,128)S(1)}, f32[16,512]{1,0:T(8,128)S(1)}, u32[]{:S(2)}, u32[]{:S(2)}) collective-permute-start(f32[16,512]{1,0:T(8,128)S(1)} %get-tuple-element.45), channel_id=1, source_target_pairs={{0,4},{4,8},{8,12},{12,0},{1,5},{5,9},{9,13},{13,1},{2,6},{6,10},{... | collective-permute-start | bytes 98312 | tf_op jit(solution)/shard_map/ppermute | solution.py:605
  23.5 5.2 %collective-permute-start.5 = (f32[16,512]{1,0:T(8,128)S(1)}, f32[16,512]{1,0:T(8,128)S(1)}, u32[]{:S(2)}, u32[]{:S(2)}) collective-permute-start(f32[16,512]{1,0:T(8,128)S(1)} %get-tuple-element.43), channel_id=1, source_target_pairs={{0,8},{4,12},{8,0},{12,4},{1,9},{5,13},{9,1},{13,5},{2,10},{6,14},... | collective-permute-start | bytes 98312 | tf_op jit(solution)/shard_map/ppermute | solution.py:605
  28.6 3.9 %collective-permute-start.8 = (f32[16,256]{1,0:T(8,128)S(1)}, f32[16,256]{1,0:T(8,128)S(1)}, u32[]{:S(2)}, u32[]{:S(2)}) collective-permute-start(f32[16,256]{1,0:T(8,128)S(1)} %slice.29), channel_id=1, source_target_pairs={{0,2},{1,3},{2,0},{3,1},{4,6},{5,7},{6,4},{7,5},{8,10},{9,11},{10,... | collective-permute-start | bytes 49160 | tf_op jit(solution)/shard_map/ppermute | solution.py:550

commit v4 on v3

--- a/solution.py
+++ b/solution.py
@@ -12,7 +12,8 @@
 WAVE = 0.3
 OMEGA = 0.25
 LANES = 128
-GROUPS = 4
+GROUPS = 2
+TABLE_CHUNK = 256
 SLOTS = 24
 VMEM = pltpu.CompilerParams(vmem_limit_bytes=24 * 1024 * 1024)
 
@@ -42,13 +43,13 @@
     return 2.0 * sin_half * cos_half, 1.0 - 2.0 * sin_half * sin_half
 
 
-def prepare_body(e_in, h_in, p_in, q_in, eps_in, mat_in, poles_in, one_ref, two_ref, d_ref, g_ref, k_ref, e_ref, h_ref,
-                 p_ref, q_ref, eps_ref, mat_ref, poles_ref, table_ref, up_ref, down_ref, sems, poles_sem):
+def prepare_body(e_in, h_in, p_in, q_in, eps_in, mat_in, poles_in, waves_in, one_ref, two_ref, d_ref, g_ref, k_ref,
+                 e_ref, h_ref, waves_ref, p_ref, q_ref, eps_ref, mat_ref, poles_ref, table_ref, up_ref, down_ref, sems, small_sems):
     levels, rows, width = eps_ref.shape
     last = width - LANES
     pairs = ((e_in, e_ref), (h_in, h_ref), (p_in, p_ref), (q_in, q_ref), (eps_in, eps_ref), (mat_in, mat_ref))
     group = levels // GROUPS
-    poles_copy = pltpu.make_async_copy(poles_in, poles_ref, poles_sem)
+    poles_copy = pltpu.make_async_copy(poles_in, poles_ref, small_sems.at[0])
     poles_copy.start()
     copies = []
     for part in range(GROUPS):
@@ -58,6 +59,8 @@
             copy = pltpu.make_async_copy(source.at[at], target.at[at], sems.at[part, k])
             copy.start()
             copies.append(copy)
+    waves_copy = pltpu.make_async_copy(waves_in, waves_ref, small_sems.at[1])
+    waves_copy.start()
     poles_copy.wait()
     table_ref[0:3, 0 : poles_ref.shape[1]] = poles_ref[...]
     omega_dt, gamma_dt, strength = (table_ref[i : i + 1, :] for i in range(3))
@@ -106,18 +109,19 @@
     down = down_ref[...].T[:SLOTS]
     one_ref[...] = jnp.where(even, up, down)
     two_ref[...] = jnp.where(even, down, up)
-
-
-def prepare(e_field, h_field, pol_now, pol_old, eps_inf, materials, poles):
+    waves_copy.wait()
+
+
+def prepare(e_field, h_field, pol_now, pol_old, eps_inf, materials, poles, waves):
     levels, rows, width = eps_inf.shape
     message = jax.ShapeDtypeStruct((SLOTS, levels * rows), jnp.float32)
     field = jax.ShapeDtypeStruct(e_field.shape, jnp.float32)
     pair = jax.ShapeDtypeStruct((2, levels, rows, width), jnp.float32)
-    arrays = (e_field, h_field, pol_now, pol_old, eps_inf, materials, poles)
+    arrays = (e_field, h_field, pol_now, pol_old, eps_inf, materials, poles, waves)
     return pl.pallas_call(
         prepare_body,
-        out_shape=(message, message, field, field, pair, field, field),
-        in_specs=[pl.BlockSpec(memory_space=pltpu.HBM)] * 7,
+        out_shape=(message, message, field, field, pair, field, field, jax.ShapeDtypeStruct(waves.shape, jnp.float32)),
+        in_specs=[pl.BlockSpec(memory_space=pltpu.HBM)] * 8,
         scratch_shapes=[
             pltpu.VMEM(e_field.shape, jnp.float32),
             pltpu.VMEM(e_field.shape, jnp.float32),
@@ -128,7 +132,7 @@
             pltpu.VMEM((levels * rows, LANES), jnp.float32),
             pltpu.VMEM((levels * rows, LANES), jnp.float32),
             pltpu.SemaphoreType.DMA((GROUPS, 6)),
-            pltpu.SemaphoreType.DMA,
+            pltpu.SemaphoreType.DMA((2,)),
         ],
         compiler_params=VMEM,
         name="prepare",
@@ -262,9 +266,9 @@
 
 
 def split_planes(plane_ref, split_refs, rows, pairs):
-    ev_ref, ev_low_ref, od_ref, od_low_ref = split_refs
     kinds = 16
     half = plane_ref.shape[2]
+    count = split_refs[0].shape[0] // 2
     back = half - 1 - lane_index((kinds, half))
     for turn, v in enumerate(pairs):
         high = [plane_ref[side, pl.ds(rows // 2 + v, kinds, stride=rows), :] for side in range(2)]
@@ -273,19 +277,22 @@
             left, right = (b - a if parity else b + a for a, b in zip(low, high))
             left = jnp.take_along_axis(left, back, axis=1)
             at = slice((2 * turn + parity) * kinds, (2 * turn + parity + 1) * kinds)
-            for value, ref, low_ref in ((right + left, ev_ref, ev_low_ref), (right - left, od_ref, od_low_ref)):
+            below = slice(count + at.start, count + at.stop)
+            for value, ref in zip((right + left, right - left), split_refs):
                 top = value.astype(jnp.bfloat16)
                 ref[at, :half] = top
                 ref[at, half:] = top
-                low_ref[at] = (value - top.astype(jnp.float32)).astype(jnp.bfloat16)
+                ref[below, :half] = (value - top.astype(jnp.float32)).astype(jnp.bfloat16)
+                ref[below, half:] = jnp.zeros_like(top)
 
 
 def project_chunk(split_refs, cos_ref, sin_ref, phase_ref, cut, pairs):
-    ev_ref, ev_low_ref, od_ref, od_low_ref = split_refs
-    half = ev_low_ref.shape[1]
-    dot = partial(jnp.dot, preferred_element_type=jnp.float32)
-    part_c = dot(ev_ref[...], cos_ref[:, cut]) + dot(ev_low_ref[...], cos_ref[:half, cut])
-    part_s = dot(od_ref[...], sin_ref[:, cut]) + dot(od_low_ref[...], sin_ref[:half, cut])
+    even_ref, odd_ref = split_refs
+    count = even_ref.shape[0] // 2
+    part_c = jnp.dot(even_ref[...], cos_ref[:, cut], preferred_element_type=jnp.float32)
+    part_s = jnp.dot(odd_ref[...], sin_ref[:, cut], preferred_element_type=jnp.float32)
+    part_c = part_c[:count] + part_c[count:]
+    part_s = part_s[:count] + part_s[count:]
     real = [0.0, 0.0]
     imag = [0.0, 0.0]
     for turn, v in enumerate(pairs):
@@ -307,8 +314,7 @@
 
 
 def split_shapes(pairs, width):
-    count = 32 * len(pairs)
-    return [(count, width), (count, width // 2)] * 2
+    return [(2 * 32 * len(pairs), width)] * 2
 
 
 def inside_body(h1_ref, e1_ref, g_ref, k_ref, surface_ref, cos_ref, sin_ref, phase_ref, out_ref, plane_ref, *split_refs, pairs):
@@ -359,7 +365,7 @@
 
 
 def second_body(h1_in, e1_in, g_ref, k_ref, surface_ref, own_one_ref, own_two_ref, x_one_ref, x_two_ref, e_out, h_out,
-                ev_ref, ev_low_ref, od_ref, od_low_ref, h1_ref, e1_ref, h2_ref, plane_ref, *, pairs):
+                even_ref, odd_ref, h1_ref, e1_ref, h2_ref, plane_ref, *, pairs):
     _, levels, rows, _ = h1_in.shape
     width = g_ref.shape[3]
     wide = (rows, h1_in.shape[3])
@@ -455,7 +461,7 @@
             e_out[i, z] = new
             if i < 2 and z in layers:
                 store_plane(plane_ref, surface_ref, 1, layers[z], i, new)
-    split_planes(plane_ref, (ev_ref, ev_low_ref, od_ref, od_low_ref), rows, pairs)
+    split_planes(plane_ref, (even_ref, odd_ref), rows, pairs)
 
 
 def edge_pairs(rows):
@@ -469,7 +475,7 @@
     store = pltpu.VMEM(h1.shape, jnp.float32)
     return pl.pallas_call(
         partial(second_body, pairs=pairs),
-        out_shape=(field, field)
+        out_shape=(pltpu.VMEM(late.shape, jnp.float32), pltpu.VMEM(late.shape, jnp.float32))
         + tuple(jax.ShapeDtypeStruct(shape, jnp.bfloat16) for shape in split_shapes(pairs, width)),
         scratch_shapes=[store, store, store, pltpu.VMEM((2, 16 * rows, width // 2), jnp.float32)],
         compiler_params=VMEM,
@@ -477,28 +483,38 @@
     )(h1, e1, late, factors, surface, own_one, own_two, x_one, x_two)
 
 
-def table_body(waves_ref, tie_ref, cos_ref, sin_ref, phase_ref, *, rows, width, scale):
-    del tie_ref
+def table_body(waves_ref, cos_ref, sin_ref, phase_ref, centre_ref, *, rows, width, scale, owned):
     half = width // 2
-    chunk = 256
+    chunk = TABLE_CHUNK
+    chunks = waves_ref.shape[1] // chunk
     step = (row_index((8, chunk)).astype(jnp.float32)) + 0.5
     centre_x = (lax.axis_index("gx") * rows).astype(jnp.float32) + 0.5 * (rows - 1)
     centre_y = (lax.axis_index("gy") * width).astype(jnp.float32) + 0.5 * (width - 1)
-
-    @pl.loop(0, waves_ref.shape[1] // chunk)
+    for k in range(chunks):
+        cut = slice(k * chunk, (k + 1) * chunk)
+        centre_ref[0, k : k + 1] = WAVE * waves_ref[0:1, cut] * centre_x + WAVE * waves_ref[1:2, cut] * centre_y
+    sin_c, cos_c = sincos(centre_ref[0])
+    centre_ref[0] = scale * cos_c
+    centre_ref[1] = scale * sin_c
+
+    @pl.loop(0, chunks, unroll=2)
     def _(turn):
         cut = pl.ds(pl.multiple_of(turn * chunk, chunk), chunk)
-        wave_x, wave_y = WAVE * waves_ref[0:1, cut], WAVE * waves_ref[1:2, cut]
+        source = block_source(turn, owned // chunk) if owned % chunk == 0 else turn
+        at = pl.ds(pl.multiple_of(source * chunk, chunk), chunk)
+        wave_x, wave_y = WAVE * waves_ref[0:1, at], WAVE * waves_ref[1:2, at]
         sin_x, cos_x = sincos(wave_x * step)
         phase_ref[0:8, cut] = cos_x
         phase_ref[8:16, cut] = sin_x
-        sin_c, cos_c = sincos(wave_x * centre_x + wave_y * centre_y)
-        phase_ref[16:24, cut] = jnp.broadcast_to(scale * cos_c, step.shape)
-        phase_ref[24:32, cut] = jnp.broadcast_to(scale * sin_c, step.shape)
+        phase_ref[16:24, cut] = jnp.broadcast_to(centre_ref[0, pl.ds(source, 1)], step.shape)
+        phase_ref[24:32, cut] = jnp.broadcast_to(centre_ref[1, pl.ds(source, 1)], step.shape)
         sin_y, cos_y = sincos(wave_y * step)
-        sin_w, cos_w = sincos(wave_y * 8.0)
-        cos_y = jnp.concatenate([cos_y, cos_y * cos_w - sin_y * sin_w], axis=0)
-        sin_y = jnp.concatenate([sin_y, sin_y * cos_w + cos_y[0:8] * sin_w], axis=0)
+        cos_w = cos_y[7:8] * cos_y[0:1] - sin_y[7:8] * sin_y[0:1]
+        sin_w = sin_y[7:8] * cos_y[0:1] + cos_y[7:8] * sin_y[0:1]
+        next_cos = cos_y * cos_w - sin_y * sin_w
+        next_sin = sin_y * cos_w + cos_y * sin_w
+        cos_y = jnp.concatenate([cos_y, next_cos], axis=0)
+        sin_y = jnp.concatenate([sin_y, next_sin], axis=0)
         sin_w, cos_w = 2.0 * sin_w * cos_w, 1.0 - 2.0 * sin_w * sin_w
         for start in range(0, half, 16):
             if start:
@@ -509,26 +525,38 @@
                 ref[half + start : half + start + 16, cut] = (value - top.astype(jnp.float32)).astype(jnp.bfloat16)
 
 
-def tables(waves, tie, rows, width, scale):
+def block_source(block, each):
+    count_x, count_y = lax.axis_size("gx"), lax.axis_size("gy")
+    group = group_of("gx")
+    place_x, place_y = lax.axis_index("gx"), lax.axis_index("gy")
+    rest, within = block // each, block % each
+    rest, far_y = rest // (count_y // 2), rest % (count_y // 2)
+    rest, near_x = rest // group, rest % group
+    core, far_x = rest // (count_x // group), rest % (count_x // group)
+    owner_x = (far_x ^ (place_x // group)) * group + (place_x + near_x) % group
+    owner_y = (far_y ^ (place_y // 2)) * 2 + (core ^ (place_y % 2))
+    return (owner_x * count_y + owner_y) * each + within
+
+
+def tables(waves, rows, width, scale):
     count = waves.shape[1]
+    owned = count // (lax.axis_size("gx") * lax.axis_size("gy"))
     table = jax.ShapeDtypeStruct((width, count), jnp.bfloat16)
     return pl.pallas_call(
-        partial(table_body, rows=rows, width=width, scale=scale),
+        partial(table_body, rows=rows, width=width, scale=scale, owned=owned),
         out_shape=(table, table, jax.ShapeDtypeStruct((32, count), jnp.float32)),
-        in_specs=[pl.BlockSpec(memory_space=pltpu.VMEM), pl.BlockSpec(memory_space=pl.ANY)],
+        scratch_shapes=[pltpu.VMEM((2, count // TABLE_CHUNK, TABLE_CHUNK), jnp.float32)],
         compiler_params=VMEM,
         cost_estimate=pl.CostEstimate(flops=40 * width * count, bytes_accessed=4 * width * count, transcendentals=0),
         name="tables",
-    )(waves, tie)
-
-
-def project_body(ev_ref, ev_low_ref, od_ref, od_low_ref, cos_ref, sin_ref, phase_ref, inner_ref, out_ref, *, start, pairs):
+    )(waves)
+
+
+def project_body(even_ref, odd_ref, cos_ref, sin_ref, phase_ref, inner_ref, out_ref, *, start, pairs):
     chunk = 256
     for at in range(0, out_ref.shape[1], chunk):
         cut, to = slice(start + at, start + at + chunk), slice(at, at + chunk)
-        real, imag = project_chunk(
-            (ev_ref, ev_low_ref, od_ref, od_low_ref), cos_ref, sin_ref, phase_ref, cut, pairs
-        )
+        real, imag = project_chunk((even_ref, odd_ref), cos_ref, sin_ref, phase_ref, cut, pairs)
         out_ref[0:8, to] = real + inner_ref[0:8, cut]
         out_ref[8:16, to] = imag + inner_ref[8:16, cut]
 
@@ -611,11 +639,14 @@
 def local(e_field, h_field, pol_now, pol_old, eps_inf, materials, surface, poles, directions):
     _, _, rows, width = e_field.shape
     scale = 1.0 / math.sqrt(rows * lax.axis_size("gx") * width * lax.axis_size("gy"))
-    one, two, near, late, factors, e_field, h_field = prepare(e_field, h_field, pol_now, pol_old, eps_inf, materials, poles)
-    tie = factors
+    owned = directions.shape[0] // (lax.axis_size("gx") * lax.axis_size("gy"))
+    waves = directions.T if owned % TABLE_CHUNK == 0 else own_first(directions)
+    one, two, near, late, factors, e_field, h_field, waves = prepare(
+        e_field, h_field, pol_now, pol_old, eps_inf, materials, poles, waves
+    )
     one = swap(one, "gy", 1)
     two = swap_other(two, "gy")
-    cos_y, sin_y, phases = tables(own_first(directions), tie, rows, width, scale)
+    cos_y, sin_y, phases = tables(waves, rows, width, scale)
     own_one, own_two, h1, e1 = first_step(e_field, h_field, near, factors, one, two, phases)
     x_one = swap(own_one, "gx", 1)
     x_two = swap_other(own_two, "gx")

time: 33.4 us -> 32 us (0.958)
  waiting for transfers between devices: 4.56 us -> 3.28 us
  Pallas kernels: 9.88 us -> 8.8 us
  local copies, waits for them, and re-layouts: 0.9 us -> 1.51 us
  starting transfers between devices: 16.2 us -> 16.8 us
    unnamed x2 -> x4, local copies, waits for them, and re-layouts: 0.01 us -> 1.49 us
    ppermute x4, waiting for transfers between devices: 2.02 us -> 0.74 us  [swap(): lax.ppermute(array, axis, [(i, i ^ mask) for i in range(lax.axis_size(axi...]
    reshape x3 -> x0, local copies, waits for them, and re-layouts: 0.86 us -> none  [the longest x2 0.82 us: own_first(): directions.T.reshape(2, count_x // group, group, count_y // 2, 2, -1)]
    pallas_call x2, Pallas kernels: 3.1 us -> 2.45 us  [the longest x1 1.82 us: tables(): pl.pallas_call(partial(table_body, rows=rows, width=width, scale=scale, o...]
    ppermute x4, starting transfers between devices: 8.03 us -> 8.64 us  [swap(): lax.ppermute(array, axis, [(i, i ^ mask) for i in range(lax.axis_size(axi...]
    pallas_call x2, Pallas kernels: 1.36 us -> 0.93 us  [project(): pl.pallas_call(partial(project_body, start=start, pairs=edge_pairs(rows))...]
  transfers between devices with their start and end apart: 9 -> 9, of which waited for: 4 -> 4; matrix products, arithmetic and copies ran while one was open for 3% -> 5% of each run, Pallas kernels for 13% -> 14%
where the time goes in v4:
time: 32 us; the launch traced here: 31.8 us
  starting transfers between devices  16.8 us (52%)
  Pallas kernels  8.8 us (28%)
  waiting for transfers between devices  3.28 us (10%)
  local copies, waits for them, and re-layouts  1.51 us (5%)
  between operations  0.78 us (2%)
  other arithmetic  0.63 us (2%)
    ppermute x4, starting transfers between devices, swap(): lax.ppermute(array, axis, [(i, i ^ mask) for i in range(lax.axis_size(axi...  8.64 us
    ppermute x3, starting transfers between devices, scatter_group(): got.append(lax.ppermute(far[:, step * part:(step + 1) * part], axis, pairs))  6.89 us
    pallas_call x1, Pallas kernels, prepare(): pl.pallas_call(prepare_body, out_shape=(message, message, field, field, p...  2.59 us
    ppermute x3, waiting for transfers between devices, scatter_group(): got.append(lax.ppermute(far[:, step * part:(step + 1) * part], axis, pairs))  2.53 us
    pallas_call x1, Pallas kernels, inside(): pl.pallas_call(partial(inside_body, pairs=pairs), out_shape=jax.ShapeDtyp...  2.04 us
    pallas_call x1, Pallas kernels, tables(): pl.pallas_call(partial(table_body, rows=rows, width=width, scale=scale, o...  1.82 us
    unnamed x4, local copies, waits for them, and re-layouts  1.49 us
    ppermute x2, starting transfers between devices, swap_other(): return lax.ppermute(array, axis, pairs)  1.3 us
  transfers between devices with their start and end apart: 9, of which 4 were waited for; matrix products, arithmetic and copies ran while one was open for 5% of the time, Pallas kernels for 14%

profile of v4, /device:TPU:0, one launch (start us, length us, event | category | flops | bytes accessed | tf_op | source)
XLA Modules:
  0.0 31.8 jit_solution(17164362297724594386)
XLA Ops:
  0.6 0.0 copy-start
  0.6 2.6 %prepare.1 = (f32[24,128]{1,0:T(8,128)S(1)}, f32[24,128]{1,0:T(8,128)S(1)}, f32[3,8,16,256]{3,2,1,0:T(8,128)S(1)}, f32[3,8,16,256]{3,2,1,0:T(8,128)S(1)}, f32[2,...) custom-call(f32[3,8,16,256]{3,2,1,0:T(8,128)} %e_in.1, ...), custom_call_target="tpu_custom_call" | custom-call | tf_op jit(solution)/shard_map/prepare/pallas_call | solution.py:121
  3.2 0.5 %collective-permute-start = (f32[24,128]{1,0:T(8,128)S(1)}, f32[24,128]{1,0:T(8,128)S(1)}, u32[]{:S(2)}, u32[]{:S(2)}) collective-permute-start(f32[24,128]{1,0:T(8,128)S(1)} %get-tuple-element.26), channel_id=1, source_target_pairs={{0,1},{1,0},{2,3},{3,2},{4,5},{5,4},{6,7},{7,6},{8,9},{9,8},{10,11... | collective-permute-start | bytes 36872 | tf_op jit(solution)/shard_map/ppermute | solution.py:578
  3.8 0.7 %collective-permute-start.1 = (f32[24,128]{1,0:T(8,128)S(1)}, f32[24,128]{1,0:T(8,128)S(1)}, u32[]{:S(2)}, u32[]{:S(2)}) collective-permute-start(f32[24,128]{1,0:T(8,128)S(1)} %get-tuple-element.27), channel_id=1, source_target_pairs={{1,2},{2,1},{5,6},{6,5},{9,10},{10,9},{13,14},{14,13},{17,18},{18,... | collective-permute-start | bytes 36872 | tf_op jit(solution)/shard_map/ppermute | solution.py:583
  4.4 1.8 %tables.1 = (bf16[256,4096]{1,0:T(8,128)(2,1)S(1)}, bf16[256,4096]{1,0:T(8,128)(2,1)S(1)}, f32[32,4096]{1,0:T(8,128)S(1)}) custom-call(f32[2,4096]{1,0:T(2,128)S(1)} %get-tuple-element.28.waves_ref), custom_call_target="tpu_custom_call" | custom-call | flops 41943040 | bytes 4194304 | tf_op jit(solution)/shard_map/tables/pallas_call | solution.py:545
  6.2 0.0 collective-permute-done.one_ref
  6.3 0.0 collective-permute-done.1.two_ref
  6.3 0.8 %first_step.1 = (f32[5,8,384]{2,1,0:T(8,128)S(1)}, f32[5,8,384]{2,1,0:T(8,128)S(1)}, f32[3,8,16,384]{3,2,1,0:T(8,128)S(1)}, f32[3,8,16,384]{3,2,1,0:T(8,128)S(1)}) custom-call(f32[3,8,16,256]{3,2,1,0:T(8,128)S(1)} %get-tuple-element.22.e_ref, f32[3,8,16,256]{3,2,1,0:T(8,128)S(1)} %get-tuple-element.23.h_ref, f32[3,8,16,256]{3,2,1,0:T(8,128)S(1)} %get-tuple-element.24.d_ref, ...), custom_call_target="tpu_custom_call" | custom-call | tf_op jit(solution)/shard_map/first_step/pallas_call | solution.py:250
  7.1 2.7 %collective-permute-start.2 = (f32[5,8,384]{2,1,0:T(8,128)S(1)}, f32[5,8,384]{2,1,0:T(8,128)S(1)}, u32[]{:S(2)}, u32[]{:S(2)}) collective-permute-start(f32[5,8,384]{2,1,0:T(8,128)S(1)} %get-tuple-element.33.own_one_ref), channel_id=1, source_target_pairs={{0,4},{4,0},{8,12},{12,8},{1,5},{5,1},{9,13},{13,9},{2,6},{6,2},{1... | collective-permute-start | bytes 184328 | tf_op jit(solution)/shard_map/ppermute | solution.py:578
  9.7 0.7 %collective-permute-start.3 = (f32[5,8,384]{2,1,0:T(8,128)S(1)}, f32[5,8,384]{2,1,0:T(8,128)S(1)}, u32[]{:S(2)}, u32[]{:S(2)}) collective-permute-start(f32[5,8,384]{2,1,0:T(8,128)S(1)} %get-tuple-element.34.own_two_ref), channel_id=1, source_target_pairs={{4,8},{8,4},{5,9},{9,5},{6,10},{10,6},{7,11},{11,7},{20,24},{24,20... | collective-permute-start | bytes 184328 | tf_op jit(solution)/shard_map/ppermute | solution.py:583
  10.4 0.0 copy-done
  10.4 2.0 %inside.1.inner_ref = f32[16,4096]{1,0:T(8,128)S(1)} custom-call(f32[3,8,16,384]{3,2,1,0:T(8,128)S(1)} %get-tuple-element.30.h1_in.h1_ref, f32[3,8,16,384]{3,2,1,0:T(8,128)S(1)} %get-tuple-element.31.e1_in.e1_ref, f32[3,8,16,256]{3,2,1,0:T(8,128)S(1)} %get-tuple-element.32.g_ref, f32[2,8,16,256]{3,2,1,0:T(8,128)S(1)} %get-tuple-element.25.k_ref, ...), custom_call_target="tpu_custom_call" | custom-call | flops 1610612736 | bytes 4194304 | tf_op jit(solution)/shard_map/inside/pallas_call | solution.py:354
  12.4 0.0 collective-permute-done.2.x_one_ref
  12.5 0.0 collective-permute-done.3.x_two_ref
  12.5 0.6 %second_step.1 = (f32[3,8,16,256]{3,2,1,0:T(8,128)S(1)}, f32[3,8,16,256]{3,2,1,0:T(8,128)S(1)}, bf16[128,256]{1,0:T(8,128)(2,1)S(1)}, bf16[128,256]{1,0:T(8,128)(2,1)S(1)}) custom-call(f32[3,8,16,384]{3,2,1,0:T(8,128)S(1)} %get-tuple-element.30.h1_in.h1_ref, f32[3,8,16,384]{3,2,1,0:T(8,128)S(1)} %get-tuple-element.31.e1_in.e1_ref, ...), custom_call_target="tpu_custom_call" | custom-call | tf_op jit(solution)/shard_map/second_step/pallas_call | solution.py:476
  13.1 0.5 %project.3 = f32[16,2048]{1,0:T(8,128)S(1)} custom-call(bf16[128,256]{1,0:T(8,128)(2,1)S(1)} %get-tuple-element.37.even_ref, bf16[128,256]{1,0:T(8,128)(2,1)S(1)} %get-tuple-element.38.odd_ref, bf16[256,4096]{1,0:T(8,128)(2,1)S(1)} %get-tuple-element.39.cos_ref, bf16[256,4096]{1,0:T(8,128)(2,1)S(1)} %get-tuple-element.40.sin_ref, ...), custom_call_target="tpu_custom_call" | custom-call | flops 536870912 | bytes 2097152 | tf_op jit(solution)/shard_map/project/pallas_call | solution.py:566
  13.6 2.8 %collective-permute-start.4 = (f32[16,2048]{1,0:T(8,128)S(1)}, f32[16,2048]{1,0:T(8,128)S(1)}, u32[]{:S(2)}, u32[]{:S(2)}) collective-permute-start(f32[16,2048]{1,0:T(8,128)S(1)} %project.3), channel_id=1, source_target_pairs={{0,1},{1,0},{2,3},{3,2},{4,5},{5,4},{6,7},{7,6},{8,9},{9,8},{10,11... | collective-permute-start | bytes 393224 | tf_op jit(solution)/shard_map/ppermute | solution.py:578
  16.3 0.5 %project.2 = f32[16,2048]{1,0:T(8,128)S(1)} custom-call(bf16[128,256]{1,0:T(8,128)(2,1)S(1)} %get-tuple-element.37.even_ref, bf16[128,256]{1,0:T(8,128)(2,1)S(1)} %get-tuple-element.38.odd_ref, bf16[256,4096]{1,0:T(8,128)(2,1)S(1)} %get-tuple-element.39.cos_ref, bf16[256,4096]{1,0:T(8,128)(2,1)S(1)} %get-tuple-element.40.sin_ref, ...), custom_call_target="tpu_custom_call" | custom-call | flops 536870912 | bytes 2097152 | tf_op jit(solution)/shard_map/project/pallas_call | solution.py:566
  16.8 0.5 %collective-permute-done.4 = f32[16,2048]{1,0:T(8,128)S(1)} collective-permute-done((f32[16,2048]{1,0:T(8,128)S(1)}, f32[16,2048]{1,0:T(8,128)S(1)}, u32[]{:S(2)}, u32[]{:S(2)}) %collective-permute-start.4) | collective-permute-done | bytes 131104 | tf_op jit(solution)/shard_map/ppermute | solution.py:578
  17.4 2.7 %collective-permute-start.7 = (f32[16,512]{1,0:T(8,128)S(1)}, f32[16,512]{1,0:T(8,128)S(1)}, u32[]{:S(2)}, u32[]{:S(2)}) collective-permute-start(f32[16,512]{1,0:T(8,128)S(1)} %get-tuple-element.42), channel_id=1, source_target_pairs={{0,12},{4,0},{8,4},{12,8},{1,13},{5,1},{9,5},{13,9},{2,14},{6,2},{... | collective-permute-start | bytes 98312 | tf_op jit(solution)/shard_map/ppermute | solution.py:633
  20.1 1.6 %collective-permute-start.6 = (f32[16,512]{1,0:T(8,128)S(1)}, f32[16,512]{1,0:T(8,128)S(1)}, u32[]{:S(2)}, u32[]{:S(2)}) collective-permute-start(f32[16,512]{1,0:T(8,128)S(1)} %get-tuple-element.43), channel_id=1, source_target_pairs={{0,4},{4,8},{8,12},{12,0},{1,5},{5,9},{9,13},{13,1},{2,6},{6,10},{... | collective-permute-start | bytes 98312 | tf_op jit(solution)/shard_map/ppermute | solution.py:633
  21.6 2.6 %collective-permute-start.5 = (f32[16,512]{1,0:T(8,128)S(1)}, f32[16,512]{1,0:T(8,128)S(1)}, u32[]{:S(2)}, u32[]{:S(2)}) collective-permute-start(f32[16,512]{1,0:T(8,128)S(1)} %get-tuple-element.41), channel_id=1, source_target_pairs={{0,8},{4,12},{8,0},{12,4},{1,9},{5,13},{9,1},{13,5},{2,10},{6,14},... | collective-permute-start | bytes 98312 | tf_op jit(solution)/shard_map/ppermute | solution.py:633
  24.2 0.0 collective-permute-done.7
  24.3 1.8 %collective-permute-done.6 = f32[16,512]{1,0:T(8,128)S(1)} collective-permute-done((f32[16,512]{1,0:T(8,128)S(1)}, f32[16,512]{1,0:T(8,128)S(1)}, u32[]{:S(2)}, u32[]{:S(2)}) %collective-permute-start.6) | collective-permute-done | bytes 32800 | tf_op jit(solution)/shard_map/ppermute | solution.py:633
  26.0 0.8 %collective-permute-done.5 = f32[16,512]{1,0:T(8,128)S(1)} collective-permute-done((f32[16,512]{1,0:T(8,128)S(1)}, f32[16,512]{1,0:T(8,128)S(1)}, u32[]{:S(2)}, u32[]{:S(2)}) %collective-permute-start.5) | collective-permute-done | bytes 32800 | tf_op jit(solution)/shard_map/ppermute | solution.py:633
  26.8 2.7 %collective-permute-start.8 = (f32[16,256]{1,0:T(8,128)S(1)}, f32[16,256]{1,0:T(8,128)S(1)}, u32[]{:S(2)}, u32[]{:S(2)}) collective-permute-start(f32[16,256]{1,0:T(8,128)S(1)} %slice.29), channel_id=1, source_target_pairs={{0,2},{1,3},{2,0},{3,1},{4,6},{5,7},{6,4},{7,5},{8,10},{9,11},{10,... | collective-permute-start | bytes 49160 | tf_op jit(solution)/shard_map/ppermute | solution.py:578
  29.5 0.7 %copy.12 = f32[3,8,16,256]{3,2,1,0:T(8,128)} copy(f32[3,8,16,256]{3,2,1,0:T(8,128)S(1)} %get-tuple-element.44) | data formatting | bytes 786432
  30.2 0.7 %copy.13 = f32[3,8,16,256]{3,2,1,0:T(8,128)} copy(f32[3,8,16,256]{3,2,1,0:T(8,128)S(1)} %get-tuple-element.45) | data formatting | bytes 786432
  31.0 0.2 collective-permute-done.8
  31.2 0.6 %fusion.2 = f32[256,16]{0,1:T(8,128)} fusion(f32[16,256]{1,0:T(8,128)S(1)} %collective-permute-done.8, f32[16,512]{1,0:T(8,128)S(1)} %fusion.1), kind=kLoop, calls=%fused_computation.4 | loop fusion | flops 4096 | bytes 49152 | tf_op jit(solution)/shard_map/transpose | solution.py:662
  (4 shorter events, 0.0 us)
Async XLA Ops:
  0.6 9.8 %copy-start = (s32[2,16,256]{2,1,0:T(8,128)S(1)}, s32[2,16,256]{2,1,0:T(8,128)}, u32[]{:S(2)}) copy-start(s32[2,16,256]{2,1,0:T(8,128)} %surface_ref.3) | copy-start | bytes 98308
  3.2 3.0 %collective-permute-start = (f32[24,128]{1,0:T(8,128)S(1)}, f32[24,128]{1,0:T(8,128)S(1)}, u32[]{:S(2)}, u32[]{:S(2)}) collective-permute-start(f32[24,128]{1,0:T(8,128)S(1)} %get-tuple-element.26), channel_id=1, source_target_pairs={{0,1},{1,0},{2,3},{3,2},{4,5},{5,4},{6,7},{7,6},{8,9},{9,8},{10,11... | collective-permute-start | bytes 36872 | tf_op jit(solution)/shard_map/ppermute | solution.py:578
  3.8 2.5 %collective-permute-start.1 = (f32[24,128]{1,0:T(8,128)S(1)}, f32[24,128]{1,0:T(8,128)S(1)}, u32[]{:S(2)}, u32[]{:S(2)}) collective-permute-start(f32[24,128]{1,0:T(8,128)S(1)} %get-tuple-element.27), channel_id=1, source_target_pairs={{1,2},{2,1},{5,6},{6,5},{9,10},{10,9},{13,14},{14,13},{17,18},{18,... | collective-permute-start | bytes 36872 | tf_op jit(solution)/shard_map/ppermute | solution.py:583
  7.1 5.4 %collective-permute-start.2 = (f32[5,8,384]{2,1,0:T(8,128)S(1)}, f32[5,8,384]{2,1,0:T(8,128)S(1)}, u32[]{:S(2)}, u32[]{:S(2)}) collective-permute-start(f32[5,8,384]{2,1,0:T(8,128)S(1)} %get-tuple-element.33.own_one_ref), channel_id=1, source_target_pairs={{0,4},{4,0},{8,12},{12,8},{1,5},{5,1},{9,13},{13,9},{2,6},{6,2},{1... | collective-permute-start | bytes 184328 | tf_op jit(solution)/shard_map/ppermute | solution.py:578
  9.7 2.7 %collective-permute-start.3 = (f32[5,8,384]{2,1,0:T(8,128)S(1)}, f32[5,8,384]{2,1,0:T(8,128)S(1)}, u32[]{:S(2)}, u32[]{:S(2)}) collective-permute-start(f32[5,8,384]{2,1,0:T(8,128)S(1)} %get-tuple-element.34.own_two_ref), channel_id=1, source_target_pairs={{4,8},{8,4},{5,9},{9,5},{6,10},{10,6},{7,11},{11,7},{20,24},{24,20... | collective-permute-start | bytes 184328 | tf_op jit(solution)/shard_map/ppermute | solution.py:583
  13.6 3.8 %collective-permute-start.4 = (f32[16,2048]{1,0:T(8,128)S(1)}, f32[16,2048]{1,0:T(8,128)S(1)}, u32[]{:S(2)}, u32[]{:S(2)}) collective-permute-start(f32[16,2048]{1,0:T(8,128)S(1)} %project.3), channel_id=1, source_target_pairs={{0,1},{1,0},{2,3},{3,2},{4,5},{5,4},{6,7},{7,6},{8,9},{9,8},{10,11... | collective-permute-start | bytes 393224 | tf_op jit(solution)/shard_map/ppermute | solution.py:578
  17.4 6.9 %collective-permute-start.7 = (f32[16,512]{1,0:T(8,128)S(1)}, f32[16,512]{1,0:T(8,128)S(1)}, u32[]{:S(2)}, u32[]{:S(2)}) collective-permute-start(f32[16,512]{1,0:T(8,128)S(1)} %get-tuple-element.42), channel_id=1, source_target_pairs={{0,12},{4,0},{8,4},{12,8},{1,13},{5,1},{9,5},{13,9},{2,14},{6,2},{... | collective-permute-start | bytes 98312 | tf_op jit(solution)/shard_map/ppermute | solution.py:633
  20.1 5.9 %collective-permute-start.6 = (f32[16,512]{1,0:T(8,128)S(1)}, f32[16,512]{1,0:T(8,128)S(1)}, u32[]{:S(2)}, u32[]{:S(2)}) collective-permute-start(f32[16,512]{1,0:T(8,128)S(1)} %get-tuple-element.43), channel_id=1, source_target_pairs={{0,4},{4,8},{8,12},{12,0},{1,5},{5,9},{9,13},{13,1},{2,6},{6,10},{... | collective-permute-start | bytes 98312 | tf_op jit(solution)/shard_map/ppermute | solution.py:633
  21.6 5.2 %collective-permute-start.5 = (f32[16,512]{1,0:T(8,128)S(1)}, f32[16,512]{1,0:T(8,128)S(1)}, u32[]{:S(2)}, u32[]{:S(2)}) collective-permute-start(f32[16,512]{1,0:T(8,128)S(1)} %get-tuple-element.41), channel_id=1, source_target_pairs={{0,8},{4,12},{8,0},{12,4},{1,9},{5,13},{9,1},{13,5},{2,10},{6,14},... | collective-permute-start | bytes 98312 | tf_op jit(solution)/shard_map/ppermute | solution.py:633
  26.8 4.4 %collective-permute-start.8 = (f32[16,256]{1,0:T(8,128)S(1)}, f32[16,256]{1,0:T(8,128)S(1)}, u32[]{:S(2)}, u32[]{:S(2)}) collective-permute-start(f32[16,256]{1,0:T(8,128)S(1)} %slice.29), channel_id=1, source_target_pairs={{0,2},{1,3},{2,0},{3,1},{4,6},{5,7},{6,4},{7,5},{8,10},{9,11},{10,... | collective-permute-start | bytes 49160 | tf_op jit(solution)/shard_map/ppermute | solution.py:578

commit v5 on v4

--- a/solution.py
+++ b/solution.py
@@ -14,7 +14,8 @@
 LANES = 128
 GROUPS = 2
 TABLE_CHUNK = 256
-SLOTS = 24
+SLOT = 40
+PACKED = LANES // SLOT
 VMEM = pltpu.CompilerParams(vmem_limit_bytes=24 * 1024 * 1024)
 
 
@@ -43,8 +44,8 @@
     return 2.0 * sin_half * cos_half, 1.0 - 2.0 * sin_half * sin_half
 
 
-def prepare_body(e_in, h_in, p_in, q_in, eps_in, mat_in, poles_in, waves_in, one_ref, two_ref, d_ref, g_ref, k_ref,
-                 e_ref, h_ref, waves_ref, p_ref, q_ref, eps_ref, mat_ref, poles_ref, table_ref, up_ref, down_ref, sems, small_sems):
+def prepare_body(e_in, h_in, p_in, q_in, eps_in, mat_in, poles_in, waves_in, message_ref, d_ref, g_ref, k_ref,
+                 e_ref, h_ref, waves_ref, p_ref, q_ref, eps_ref, mat_ref, poles_ref, table_ref, sems, small_sems):
     levels, rows, width = eps_ref.shape
     last = width - LANES
     pairs = ((e_in, e_ref), (h_in, h_ref), (p_in, p_ref), (q_in, q_ref), (eps_in, eps_ref), (mat_in, mat_ref))
@@ -70,13 +71,14 @@
     table_b = jnp.broadcast_to(-(1.0 - 0.5 * gamma_dt) / denominator, tile)
     table_c = jnp.broadcast_to(strength * omega_dt * omega_dt / denominator, tile)
     lane = lane_index(tile)
-    even = lax.rem(lax.axis_index("gy"), 2) == 0
     for z in range(levels):
         if z % group == 0:
             for copy in copies[z // group * 6 : z // group * 6 + 6]:
                 copy.wait()
-        up = jnp.zeros(tile, jnp.float32)
-        down = jnp.zeros(tile, jnp.float32)
+        if z % PACKED == 0:
+            message = jnp.zeros(tile, jnp.float32)
+        base = z % PACKED * SLOT
+        edges = []
         for start in range(0, width, LANES):
             cut = slice(start, start + LANES)
             number = mat_ref[z, :, cut]
@@ -96,31 +98,26 @@
                 g_ref[i, z, :, cut] = ((a * new - new) + b * now) * inv
                 items.append(local)
             items.append(half)
-            for k, item in enumerate(items):
-                if start == 0:
-                    moved = pltpu.roll(item, 2 * k, 1) if k else item
-                    down = jnp.where((lane >= 2 * k) & (lane < 2 * k + 2), moved, down)
-                if start == last:
-                    moved = pltpu.roll(item, LANES - 2 * k, 1) if k else item
-                    up = jnp.where((lane >= LANES - 2 - 2 * k) & (lane < LANES - 2 * k), moved, up)
-        up_ref[z * rows : (z + 1) * rows] = up
-        down_ref[z * rows : (z + 1) * rows] = down
-    up = up_ref[...].T[LANES - SLOTS :]
-    down = down_ref[...].T[:SLOTS]
-    one_ref[...] = jnp.where(even, up, down)
-    two_ref[...] = jnp.where(even, down, up)
+            if start in (0, last):
+                edges.append(items)
+        for k, (left, right) in enumerate(zip(edges[0], edges[-1])):
+            at = base + 4 * k
+            item = pltpu.roll(jnp.where(lane < 2, left, right), at + 2, 1)
+            message = jnp.where((lane >= at) & (lane < at + 4), item, message)
+        if z % PACKED == PACKED - 1 or z == levels - 1:
+            message_ref[z // PACKED] = message
     waves_copy.wait()
 
 
 def prepare(e_field, h_field, pol_now, pol_old, eps_inf, materials, poles, waves):
     levels, rows, width = eps_inf.shape
-    message = jax.ShapeDtypeStruct((SLOTS, levels * rows), jnp.float32)
+    message = jax.ShapeDtypeStruct((-(-levels // PACKED), rows, LANES), jnp.float32)
     field = jax.ShapeDtypeStruct(e_field.shape, jnp.float32)
     pair = jax.ShapeDtypeStruct((2, levels, rows, width), jnp.float32)
     arrays = (e_field, h_field, pol_now, pol_old, eps_inf, materials, poles, waves)
     return pl.pallas_call(
         prepare_body,
-        out_shape=(message, message, field, field, pair, field, field, jax.ShapeDtypeStruct(waves.shape, jnp.float32)),
+        out_shape=(message, field, field, pair, field, field, jax.ShapeDtypeStruct(waves.shape, jnp.float32)),
         in_specs=[pl.BlockSpec(memory_space=pltpu.HBM)] * 8,
         scratch_shapes=[
             pltpu.VMEM(e_field.shape, jnp.float32),
@@ -129,8 +126,6 @@
             pltpu.VMEM(eps_inf.shape, jnp.int32),
             pltpu.VMEM(poles.shape, jnp.float32),
             pltpu.VMEM((8, LANES), jnp.float32),
-            pltpu.VMEM((levels * rows, LANES), jnp.float32),
-            pltpu.VMEM((levels * rows, LANES), jnp.float32),
             pltpu.SemaphoreType.DMA((GROUPS, 6)),
             pltpu.SemaphoreType.DMA((2,)),
         ],
@@ -139,24 +134,24 @@
     )(*(pltpu.with_memory_space_constraint(array, pltpu.HBM) for array in arrays))
 
 
-def read_wide(own_ref, index, z, halo_ref, item):
-    both = halo_ref[z]
+def read_wide(own_ref, index, z, messages, item):
+    both = messages[z // PACKED]
     lane = lane_index(both.shape)
-    shift = 2 * item
-    late = pltpu.roll(both, LANES - shift, 1) if item else both
-    early = pltpu.roll(both, shift, 1) if item else both
-    halo = jnp.where(lane < 2, late, jnp.where(lane >= LANES - 2, early, 0.0))
+    both = pltpu.roll(both, LANES - 2 - (z % PACKED * SLOT + 4 * item), 1)
+    halo = jnp.where((lane < 2) | (lane >= LANES - 2), both, 0.0)
     return jnp.concatenate([own_ref[index, z], halo], axis=1)
 
 
-def read_y_messages(one_ref, two_ref, halo_ref):
+def read_y_messages(one_ref, two_ref):
     place = lax.axis_index("gy")
     even = lax.rem(place, 2) == 0
-    one, two = one_ref[...], two_ref[...]
-    before = jnp.where(place > 0, jnp.where(even, two, one), 0.0)
-    after = jnp.where(place < lax.axis_size("gy") - 1, jnp.where(even, one, two), 0.0)
-    blank = jnp.zeros((LANES - 2 * SLOTS, one.shape[1]), jnp.float32)
-    halo_ref[...] = jnp.concatenate([after, blank, before], axis=0).T.reshape(halo_ref.shape)
+    messages = []
+    for k in range(one_ref.shape[0]):
+        one, two = one_ref[k], two_ref[k]
+        before = jnp.where(place > 0, jnp.where(even, two, one), 0.0)
+        after = jnp.where(place < lax.axis_size("gy") - 1, jnp.where(even, one, two), 0.0)
+        messages.append(jnp.where(lane_index(one.shape) % 4 < 2, before, after))
+    return messages
 
 
 def ahead_y(v):
@@ -201,20 +196,20 @@
     return (lane_index(shape) < width + LANES // 2) | (lax.axis_index("gy") > 0)
 
 
-def first_body(e_ref, h_ref, d_ref, k_ref, one_ref, two_ref, tie_ref, out_one_ref, out_two_ref, h1_ref, e1_ref, e0_ref, halo_ref):
+def first_body(e_ref, h_ref, d_ref, k_ref, one_ref, two_ref, tie_ref, out_one_ref, out_two_ref, h1_ref, e1_ref, e0_ref):
     del tie_ref
     _, levels, rows, width = e_ref.shape
     wide = (rows, width + LANES)
-    read_y_messages(one_ref, two_ref, halo_ref)
+    messages = read_y_messages(one_ref, two_ref)
     keep = kept_lanes(wide, width)
     zero_row = jnp.zeros((1, wide[1]), jnp.float32)
     zero = jnp.zeros(wide, jnp.float32)
     for z in range(levels):
         for i in range(3):
-            e0_ref[i, z] = read_wide(e_ref, i, z, halo_ref, i)
+            e0_ref[i, z] = read_wide(e_ref, i, z, messages, i)
     for z in range(levels):
         above = [e0_ref[i, z + 1] for i in range(2)] if z + 1 < levels else [zero, zero]
-        h_here = [read_wide(h_ref, i, z, halo_ref, 3 + i) for i in range(3)]
+        h_here = [read_wide(h_ref, i, z, messages, 3 + i) for i in range(3)]
         new = magnetic([e0_ref[i, z] for i in range(3)], above, h_here, zero_row, zero_row, keep)
         for i in range(3):
             h1_ref[i, z] = new[i]
@@ -222,9 +217,9 @@
     for z in range(levels):
         below = [h1_ref[i, z - 1] for i in range(2)] if z else [zero, zero]
         curl = curl_back([h1_ref[i, z] for i in range(3)], below, zero_row, zero_row)
-        inv.append(read_wide(k_ref, 0, z, halo_ref, 9))
+        inv.append(read_wide(k_ref, 0, z, messages, 9))
         for i in range(3):
-            e1_ref[i, z] = read_wide(d_ref, i, z, halo_ref, 6 + i) + inv[z] * curl[i]
+            e1_ref[i, z] = read_wide(d_ref, i, z, messages, 6 + i) + inv[z] * curl[i]
     even = lax.rem(lax.axis_index("gx"), 2) == 0
     keep_row = kept_lanes((1, wide[1]), width)
     end = slice(rows - 1, rows)
@@ -251,7 +246,7 @@
         first_body,
         out_shape=(message, message, field, field),
         in_specs=[vmem] * 6 + [pl.BlockSpec(memory_space=pl.ANY)],
-        scratch_shapes=[pltpu.VMEM(store, jnp.float32), pltpu.VMEM((levels, rows, LANES), jnp.float32)],
+        scratch_shapes=[pltpu.VMEM(store, jnp.float32)],
         compiler_params=VMEM,
         name="first_step",
     )(e_field, h_field, local, factors, one, two, tie)
@@ -641,11 +636,11 @@
     scale = 1.0 / math.sqrt(rows * lax.axis_size("gx") * width * lax.axis_size("gy"))
     owned = directions.shape[0] // (lax.axis_size("gx") * lax.axis_size("gy"))
     waves = directions.T if owned % TABLE_CHUNK == 0 else own_first(directions)
-    one, two, near, late, factors, e_field, h_field, waves = prepare(
+    message, near, late, factors, e_field, h_field, waves = prepare(
         e_field, h_field, pol_now, pol_old, eps_inf, materials, poles, waves
     )
-    one = swap(one, "gy", 1)
-    two = swap_other(two, "gy")
+    one = swap(message, "gy", 1)
+    two = swap_other(message, "gy")
     cos_y, sin_y, phases = tables(waves, rows, width, scale)
     own_one, own_two, h1, e1 = first_step(e_field, h_field, near, factors, one, two, phases)
     x_one = swap(own_one, "gx", 1)

time: 32 us -> 31.5 us (0.984)
  Pallas kernels: 8.8 us -> 8.21 us
    pallas_call x1, Pallas kernels: 2.59 us -> 2.15 us  [prepare(): pl.pallas_call(prepare_body, out_shape=(message, field, field, pair, fiel...]
where the time goes in v5:
time: 31.5 us; the launch traced here: 31.4 us
  starting transfers between devices  16.9 us (54%)
  Pallas kernels  8.21 us (26%)
  waiting for transfers between devices  3.29 us (10%)
  local copies, waits for them, and re-layouts  1.51 us (5%)
  between operations  0.78 us (2%)
  other arithmetic  0.63 us (2%)
    ppermute x4, starting transfers between devices, swap(): lax.ppermute(array, axis, [(i, i ^ mask) for i in range(lax.axis_size(axi...  8.76 us
    ppermute x3, starting transfers between devices, scatter_group(): got.append(lax.ppermute(far[:, step * part:(step + 1) * part], axis, pairs))  6.87 us
    ppermute x3, waiting for transfers between devices, scatter_group(): got.append(lax.ppermute(far[:, step * part:(step + 1) * part], axis, pairs))  2.54 us
    pallas_call x1, Pallas kernels, prepare(): pl.pallas_call(prepare_body, out_shape=(message, field, field, pair, fiel...  2.15 us
    pallas_call x1, Pallas kernels, inside(): pl.pallas_call(partial(inside_body, pairs=pairs), out_shape=jax.ShapeDtyp...  2.06 us
    pallas_call x1, Pallas kernels, tables(): pl.pallas_call(partial(table_body, rows=rows, width=width, scale=scale, o...  1.82 us
    unnamed x4, local copies, waits for them, and re-layouts  1.49 us
    ppermute x2, starting transfers between devices, swap_other(): return lax.ppermute(array, axis, pairs)  1.3 us
  transfers between devices with their start and end apart: 9, of which 4 were waited for; matrix products, arithmetic and copies ran while one was open for 5% of the time, Pallas kernels for 14%

profile of v5, /device:TPU:0, one launch (start us, length us, event | category | flops | bytes accessed | tf_op | source)
XLA Modules:
  0.0 31.4 jit_solution(10638381140712596301)
XLA Ops:
  0.6 0.0 copy-start
  0.6 2.2 %prepare.1 = (f32[3,16,128]{2,1,0:T(8,128)S(1)}, f32[3,8,16,256]{3,2,1,0:T(8,128)S(1)}, f32[3,8,16,256]{3,2,1,0:T(8,128)S(1)}, f32[2,8,16,256]{3,2,1,0:T(8,128)S...) custom-call(f32[3,8,16,256]{3,2,1,0:T(8,128)} %e_in.1, ...), custom_call_target="tpu_custom_call" | custom-call | tf_op jit(solution)/shard_map/prepare/pallas_call | solution.py:118
  2.8 0.5 %collective-permute-start = (f32[3,16,128]{2,1,0:T(8,128)S(1)}, f32[3,16,128]{2,1,0:T(8,128)S(1)}, u32[]{:S(2)}, u32[]{:S(2)}) collective-permute-start(f32[3,16,128]{2,1,0:T(8,128)S(1)} %get-tuple-element.25), channel_id=1, source_target_pairs={{0,1},{1,0},{2,3},{3,2},{4,5},{5,4},{6,7},{7,6},{8,9},{9,8},{10,11... | collective-permute-start | bytes 73736 | tf_op jit(solution)/shard_map/ppermute | solution.py:573
  3.3 0.7 %collective-permute-start.1 = (f32[3,16,128]{2,1,0:T(8,128)S(1)}, f32[3,16,128]{2,1,0:T(8,128)S(1)}, u32[]{:S(2)}, u32[]{:S(2)}) collective-permute-start(f32[3,16,128]{2,1,0:T(8,128)S(1)} %get-tuple-element.25), channel_id=1, source_target_pairs={{1,2},{2,1},{5,6},{6,5},{9,10},{10,9},{13,14},{14,13},{17,18},{18,... | collective-permute-start | bytes 73736 | tf_op jit(solution)/shard_map/ppermute | solution.py:578
  4.0 1.8 %tables.1 = (bf16[256,4096]{1,0:T(8,128)(2,1)S(1)}, bf16[256,4096]{1,0:T(8,128)(2,1)S(1)}, f32[32,4096]{1,0:T(8,128)S(1)}) custom-call(f32[2,4096]{1,0:T(2,128)S(1)} %get-tuple-element.26.waves_ref), custom_call_target="tpu_custom_call" | custom-call | flops 41943040 | bytes 4194304 | tf_op jit(solution)/shard_map/tables/pallas_call | solution.py:540
  5.8 0.0 collective-permute-done.one_ref
  5.8 0.0 collective-permute-done.1.two_ref
  5.8 0.6 %first_step.1 = (f32[5,8,384]{2,1,0:T(8,128)S(1)}, f32[5,8,384]{2,1,0:T(8,128)S(1)}, f32[3,8,16,384]{3,2,1,0:T(8,128)S(1)}, f32[3,8,16,384]{3,2,1,0:T(8,128)S(1)}) custom-call(f32[3,8,16,256]{3,2,1,0:T(8,128)S(1)} %get-tuple-element.21.e_ref, f32[3,8,16,256]{3,2,1,0:T(8,128)S(1)} %get-tuple-element.22.h_ref, f32[3,8,16,256]{3,2,1,0:T(8,128)S(1)} %get-tuple-element.23.d_ref, ...), custom_call_target="tpu_custom_call" | custom-call | tf_op jit(solution)/shard_map/first_step/pallas_call | solution.py:245
  6.4 2.7 %collective-permute-start.2 = (f32[5,8,384]{2,1,0:T(8,128)S(1)}, f32[5,8,384]{2,1,0:T(8,128)S(1)}, u32[]{:S(2)}, u32[]{:S(2)}) collective-permute-start(f32[5,8,384]{2,1,0:T(8,128)S(1)} %get-tuple-element.31.own_one_ref), channel_id=1, source_target_pairs={{0,4},{4,0},{8,12},{12,8},{1,5},{5,1},{9,13},{13,9},{2,6},{6,2},{1... | collective-permute-start | bytes 184328 | tf_op jit(solution)/shard_map/ppermute | solution.py:573
  9.1 0.7 %collective-permute-start.3 = (f32[5,8,384]{2,1,0:T(8,128)S(1)}, f32[5,8,384]{2,1,0:T(8,128)S(1)}, u32[]{:S(2)}, u32[]{:S(2)}) collective-permute-start(f32[5,8,384]{2,1,0:T(8,128)S(1)} %get-tuple-element.32.own_two_ref), channel_id=1, source_target_pairs={{4,8},{8,4},{5,9},{9,5},{6,10},{10,6},{7,11},{11,7},{20,24},{24,20... | collective-permute-start | bytes 184328 | tf_op jit(solution)/shard_map/ppermute | solution.py:578
  9.8 0.0 copy-done
  9.8 2.1 %inside.1.inner_ref = f32[16,4096]{1,0:T(8,128)S(1)} custom-call(f32[3,8,16,384]{3,2,1,0:T(8,128)S(1)} %get-tuple-element.28.h1_in.h1_ref, f32[3,8,16,384]{3,2,1,0:T(8,128)S(1)} %get-tuple-element.29.e1_in.e1_ref, f32[3,8,16,256]{3,2,1,0:T(8,128)S(1)} %get-tuple-element.30.g_ref, f32[2,8,16,256]{3,2,1,0:T(8,128)S(1)} %get-tuple-element.24.k_ref, ...), custom_call_target="tpu_custom_call" | custom-call | flops 1610612736 | bytes 4194304 | tf_op jit(solution)/shard_map/inside/pallas_call | solution.py:349
  11.8 0.0 collective-permute-done.2.x_one_ref
  11.8 0.0 collective-permute-done.3.x_two_ref
  11.9 0.6 %second_step.1 = (f32[3,8,16,256]{3,2,1,0:T(8,128)S(1)}, f32[3,8,16,256]{3,2,1,0:T(8,128)S(1)}, bf16[128,256]{1,0:T(8,128)(2,1)S(1)}, bf16[128,256]{1,0:T(8,128)(2,1)S(1)}) custom-call(f32[3,8,16,384]{3,2,1,0:T(8,128)S(1)} %get-tuple-element.28.h1_in.h1_ref, f32[3,8,16,384]{3,2,1,0:T(8,128)S(1)} %get-tuple-element.29.e1_in.e1_ref, ...), custom_call_target="tpu_custom_call" | custom-call | tf_op jit(solution)/shard_map/second_step/pallas_call | solution.py:471
  12.5 0.5 %project.3 = f32[16,2048]{1,0:T(8,128)S(1)} custom-call(bf16[128,256]{1,0:T(8,128)(2,1)S(1)} %get-tuple-element.35.even_ref, bf16[128,256]{1,0:T(8,128)(2,1)S(1)} %get-tuple-element.36.odd_ref, bf16[256,4096]{1,0:T(8,128)(2,1)S(1)} %get-tuple-element.37.cos_ref, bf16[256,4096]{1,0:T(8,128)(2,1)S(1)} %get-tuple-element.38.sin_ref, ...), custom_call_target="tpu_custom_call" | custom-call | flops 536870912 | bytes 2097152 | tf_op jit(solution)/shard_map/project/pallas_call | solution.py:561
  13.0 2.9 %collective-permute-start.4 = (f32[16,2048]{1,0:T(8,128)S(1)}, f32[16,2048]{1,0:T(8,128)S(1)}, u32[]{:S(2)}, u32[]{:S(2)}) collective-permute-start(f32[16,2048]{1,0:T(8,128)S(1)} %project.3), channel_id=1, source_target_pairs={{0,1},{1,0},{2,3},{3,2},{4,5},{5,4},{6,7},{7,6},{8,9},{9,8},{10,11... | collective-permute-start | bytes 393224 | tf_op jit(solution)/shard_map/ppermute | solution.py:573
  15.9 0.5 %project.2 = f32[16,2048]{1,0:T(8,128)S(1)} custom-call(bf16[128,256]{1,0:T(8,128)(2,1)S(1)} %get-tuple-element.35.even_ref, bf16[128,256]{1,0:T(8,128)(2,1)S(1)} %get-tuple-element.36.odd_ref, bf16[256,4096]{1,0:T(8,128)(2,1)S(1)} %get-tuple-element.37.cos_ref, bf16[256,4096]{1,0:T(8,128)(2,1)S(1)} %get-tuple-element.38.sin_ref, ...), custom_call_target="tpu_custom_call" | custom-call | flops 536870912 | bytes 2097152 | tf_op jit(solution)/shard_map/project/pallas_call | solution.py:561
  16.3 0.5 %collective-permute-done.4 = f32[16,2048]{1,0:T(8,128)S(1)} collective-permute-done((f32[16,2048]{1,0:T(8,128)S(1)}, f32[16,2048]{1,0:T(8,128)S(1)}, u32[]{:S(2)}, u32[]{:S(2)}) %collective-permute-start.4) | collective-permute-done | bytes 131104 | tf_op jit(solution)/shard_map/ppermute | solution.py:573
  16.9 2.7 %collective-permute-start.7 = (f32[16,512]{1,0:T(8,128)S(1)}, f32[16,512]{1,0:T(8,128)S(1)}, u32[]{:S(2)}, u32[]{:S(2)}) collective-permute-start(f32[16,512]{1,0:T(8,128)S(1)} %get-tuple-element.40), channel_id=1, source_target_pairs={{0,12},{4,0},{8,4},{12,8},{1,13},{5,1},{9,5},{13,9},{2,14},{6,2},{... | collective-permute-start | bytes 98312 | tf_op jit(solution)/shard_map/ppermute | solution.py:628
  19.6 1.6 %collective-permute-start.6 = (f32[16,512]{1,0:T(8,128)S(1)}, f32[16,512]{1,0:T(8,128)S(1)}, u32[]{:S(2)}, u32[]{:S(2)}) collective-permute-start(f32[16,512]{1,0:T(8,128)S(1)} %get-tuple-element.41), channel_id=1, source_target_pairs={{0,4},{4,8},{8,12},{12,0},{1,5},{5,9},{9,13},{13,1},{2,6},{6,10},{... | collective-permute-start | bytes 98312 | tf_op jit(solution)/shard_map/ppermute | solution.py:628
  21.1 2.6 %collective-permute-start.5 = (f32[16,512]{1,0:T(8,128)S(1)}, f32[16,512]{1,0:T(8,128)S(1)}, u32[]{:S(2)}, u32[]{:S(2)}) collective-permute-start(f32[16,512]{1,0:T(8,128)S(1)} %get-tuple-element.39), channel_id=1, source_target_pairs={{0,8},{4,12},{8,0},{12,4},{1,9},{5,13},{9,1},{13,5},{2,10},{6,14},... | collective-permute-start | bytes 98312 | tf_op jit(solution)/shard_map/ppermute | solution.py:628
  23.8 0.0 collective-permute-done.7
  23.8 1.8 %collective-permute-done.6 = f32[16,512]{1,0:T(8,128)S(1)} collective-permute-done((f32[16,512]{1,0:T(8,128)S(1)}, f32[16,512]{1,0:T(8,128)S(1)}, u32[]{:S(2)}, u32[]{:S(2)}) %collective-permute-start.6) | collective-permute-done | bytes 32800 | tf_op jit(solution)/shard_map/ppermute | solution.py:628
  25.5 0.8 %collective-permute-done.5 = f32[16,512]{1,0:T(8,128)S(1)} collective-permute-done((f32[16,512]{1,0:T(8,128)S(1)}, f32[16,512]{1,0:T(8,128)S(1)}, u32[]{:S(2)}, u32[]{:S(2)}) %collective-permute-start.5) | collective-permute-done | bytes 32800 | tf_op jit(solution)/shard_map/ppermute | solution.py:628
  26.3 2.7 %collective-permute-start.8 = (f32[16,256]{1,0:T(8,128)S(1)}, f32[16,256]{1,0:T(8,128)S(1)}, u32[]{:S(2)}, u32[]{:S(2)}) collective-permute-start(f32[16,256]{1,0:T(8,128)S(1)} %slice.29), channel_id=1, source_target_pairs={{0,2},{1,3},{2,0},{3,1},{4,6},{5,7},{6,4},{7,5},{8,10},{9,11},{10,... | collective-permute-start | bytes 49160 | tf_op jit(solution)/shard_map/ppermute | solution.py:573
  29.0 0.7 %copy.12 = f32[3,8,16,256]{3,2,1,0:T(8,128)} copy(f32[3,8,16,256]{3,2,1,0:T(8,128)S(1)} %get-tuple-element.42) | data formatting | bytes 786432
  29.8 0.7 %copy.13 = f32[3,8,16,256]{3,2,1,0:T(8,128)} copy(f32[3,8,16,256]{3,2,1,0:T(8,128)S(1)} %get-tuple-element.43) | data formatting | bytes 786432
  30.5 0.2 collective-permute-done.8
  30.7 0.6 %fusion.2 = f32[256,16]{0,1:T(8,128)} fusion(f32[16,256]{1,0:T(8,128)S(1)} %collective-permute-done.8, f32[16,512]{1,0:T(8,128)S(1)} %fusion.1), kind=kLoop, calls=%fused_computation.4 | loop fusion | flops 4096 | bytes 49152 | tf_op jit(solution)/shard_map/transpose | solution.py:657
  (4 shorter events, 0.0 us)
Async XLA Ops:
  0.6 9.1 %copy-start = (s32[2,16,256]{2,1,0:T(8,128)S(1)}, s32[2,16,256]{2,1,0:T(8,128)}, u32[]{:S(2)}) copy-start(s32[2,16,256]{2,1,0:T(8,128)} %surface_ref.3) | copy-start | bytes 98308
  2.8 3.0 %collective-permute-start = (f32[3,16,128]{2,1,0:T(8,128)S(1)}, f32[3,16,128]{2,1,0:T(8,128)S(1)}, u32[]{:S(2)}, u32[]{:S(2)}) collective-permute-start(f32[3,16,128]{2,1,0:T(8,128)S(1)} %get-tuple-element.25), channel_id=1, source_target_pairs={{0,1},{1,0},{2,3},{3,2},{4,5},{5,4},{6,7},{7,6},{8,9},{9,8},{10,11... | collective-permute-start | bytes 73736 | tf_op jit(solution)/shard_map/ppermute | solution.py:573
  3.3 2.5 %collective-permute-start.1 = (f32[3,16,128]{2,1,0:T(8,128)S(1)}, f32[3,16,128]{2,1,0:T(8,128)S(1)}, u32[]{:S(2)}, u32[]{:S(2)}) collective-permute-start(f32[3,16,128]{2,1,0:T(8,128)S(1)} %get-tuple-element.25), channel_id=1, source_target_pairs={{1,2},{2,1},{5,6},{6,5},{9,10},{10,9},{13,14},{14,13},{17,18},{18,... | collective-permute-start | bytes 73736 | tf_op jit(solution)/shard_map/ppermute | solution.py:578
  6.4 5.4 %collective-permute-start.2 = (f32[5,8,384]{2,1,0:T(8,128)S(1)}, f32[5,8,384]{2,1,0:T(8,128)S(1)}, u32[]{:S(2)}, u32[]{:S(2)}) collective-permute-start(f32[5,8,384]{2,1,0:T(8,128)S(1)} %get-tuple-element.31.own_one_ref), channel_id=1, source_target_pairs={{0,4},{4,0},{8,12},{12,8},{1,5},{5,1},{9,13},{13,9},{2,6},{6,2},{1... | collective-permute-start | bytes 184328 | tf_op jit(solution)/shard_map/ppermute | solution.py:573
  9.1 2.8 %collective-permute-start.3 = (f32[5,8,384]{2,1,0:T(8,128)S(1)}, f32[5,8,384]{2,1,0:T(8,128)S(1)}, u32[]{:S(2)}, u32[]{:S(2)}) collective-permute-start(f32[5,8,384]{2,1,0:T(8,128)S(1)} %get-tuple-element.32.own_two_ref), channel_id=1, source_target_pairs={{4,8},{8,4},{5,9},{9,5},{6,10},{10,6},{7,11},{11,7},{20,24},{24,20... | collective-permute-start | bytes 184328 | tf_op jit(solution)/shard_map/ppermute | solution.py:578
  13.0 3.9 %collective-permute-start.4 = (f32[16,2048]{1,0:T(8,128)S(1)}, f32[16,2048]{1,0:T(8,128)S(1)}, u32[]{:S(2)}, u32[]{:S(2)}) collective-permute-start(f32[16,2048]{1,0:T(8,128)S(1)} %project.3), channel_id=1, source_target_pairs={{0,1},{1,0},{2,3},{3,2},{4,5},{5,4},{6,7},{7,6},{8,9},{9,8},{10,11... | collective-permute-start | bytes 393224 | tf_op jit(solution)/shard_map/ppermute | solution.py:573
  16.9 6.9 %collective-permute-start.7 = (f32[16,512]{1,0:T(8,128)S(1)}, f32[16,512]{1,0:T(8,128)S(1)}, u32[]{:S(2)}, u32[]{:S(2)}) collective-permute-start(f32[16,512]{1,0:T(8,128)S(1)} %get-tuple-element.40), channel_id=1, source_target_pairs={{0,12},{4,0},{8,4},{12,8},{1,13},{5,1},{9,5},{13,9},{2,14},{6,2},{... | collective-permute-start | bytes 98312 | tf_op jit(solution)/shard_map/ppermute | solution.py:628
  19.6 5.9 %collective-permute-start.6 = (f32[16,512]{1,0:T(8,128)S(1)}, f32[16,512]{1,0:T(8,128)S(1)}, u32[]{:S(2)}, u32[]{:S(2)}) collective-permute-start(f32[16,512]{1,0:T(8,128)S(1)} %get-tuple-element.41), channel_id=1, source_target_pairs={{0,4},{4,8},{8,12},{12,0},{1,5},{5,9},{9,13},{13,1},{2,6},{6,10},{... | collective-permute-start | bytes 98312 | tf_op jit(solution)/shard_map/ppermute | solution.py:628
  21.1 5.2 %collective-permute-start.5 = (f32[16,512]{1,0:T(8,128)S(1)}, f32[16,512]{1,0:T(8,128)S(1)}, u32[]{:S(2)}, u32[]{:S(2)}) collective-permute-start(f32[16,512]{1,0:T(8,128)S(1)} %get-tuple-element.39), channel_id=1, source_target_pairs={{0,8},{4,12},{8,0},{12,4},{1,9},{5,13},{9,1},{13,5},{2,10},{6,14},... | collective-permute-start | bytes 98312 | tf_op jit(solution)/shard_map/ppermute | solution.py:628
  26.3 4.4 %collective-permute-start.8 = (f32[16,256]{1,0:T(8,128)S(1)}, f32[16,256]{1,0:T(8,128)S(1)}, u32[]{:S(2)}, u32[]{:S(2)}) collective-permute-start(f32[16,256]{1,0:T(8,128)S(1)} %slice.29), channel_id=1, source_target_pairs={{0,2},{1,3},{2,0},{3,1},{4,6},{5,7},{6,4},{7,5},{8,10},{9,11},{10,... | collective-permute-start | bytes 49160 | tf_op jit(solution)/shard_map/ppermute | solution.py:573

commit v6 on v5

--- a/solution.py
+++ b/solution.py
@@ -49,12 +49,12 @@
     levels, rows, width = eps_ref.shape
     last = width - LANES
     pairs = ((e_in, e_ref), (h_in, h_ref), (p_in, p_ref), (q_in, q_ref), (eps_in, eps_ref), (mat_in, mat_ref))
-    group = levels // GROUPS
     poles_copy = pltpu.make_async_copy(poles_in, poles_ref, small_sems.at[0])
     poles_copy.start()
     copies = []
+    cuts = (0, PACKED, levels)
     for part in range(GROUPS):
-        cut = pl.ds(part * group, group)
+        cut = pl.ds(cuts[part], cuts[part + 1] - cuts[part])
         for k, (source, target) in enumerate(pairs):
             at = (slice(None), cut) if len(source.shape) == 4 else (cut,)
             copy = pltpu.make_async_copy(source.at[at], target.at[at], sems.at[part, k])
@@ -72,8 +72,8 @@
     table_c = jnp.broadcast_to(strength * omega_dt * omega_dt / denominator, tile)
     lane = lane_index(tile)
     for z in range(levels):
-        if z % group == 0:
-            for copy in copies[z // group * 6 : z // group * 6 + 6]:
+        if z in cuts:
+            for copy in copies[cuts.index(z) * 6 : cuts.index(z) * 6 + 6]:
                 copy.wait()
         if z % PACKED == 0:
             message = jnp.zeros(tile, jnp.float32)
@@ -336,7 +336,7 @@
             store_plane(plane_ref, surface_ref, 1, layer, i, new)
             store_plane(plane_ref, surface_ref, 1, layer, 2 + i, h2[i])
     split_planes(plane_ref, split_refs, rows, pairs)
-    chunk = 256
+    chunk = 512
     for at in range(0, out_ref.shape[1], chunk):
         cut = slice(at, at + chunk)
         out_ref[0:8, cut], out_ref[8:16, cut] = project_chunk(split_refs, cos_ref, sin_ref, phase_ref, cut, pairs)
@@ -548,7 +548,7 @@
 
 
 def project_body(even_ref, odd_ref, cos_ref, sin_ref, phase_ref, inner_ref, out_ref, *, start, pairs):
-    chunk = 256
+    chunk = 512
     for at in range(0, out_ref.shape[1], chunk):
         cut, to = slice(start + at, start + at + chunk), slice(at, at + chunk)
         real, imag = project_chunk((even_ref, odd_ref), cos_ref, sin_ref, phase_ref, cut, pairs)

time: 31.5 us -> 31.5 us (level)
  no operation moved by 1% of the time
where the time goes in v6:
time: 31.5 us; the launch traced here: 31.4 us
  starting transfers between devices  16.8 us (53%)
  Pallas kernels  8.34 us (26%)
  waiting for transfers between devices  3.36 us (11%)
  local copies, waits for them, and re-layouts  1.51 us (5%)
  between operations  0.77 us (2%)
  other arithmetic  0.63 us (2%)
    ppermute x4, starting transfers between devices, swap(): lax.ppermute(array, axis, [(i, i ^ mask) for i in range(lax.axis_size(axi...  8.67 us
    ppermute x3, starting transfers between devices, scatter_group(): got.append(lax.ppermute(far[:, step * part:(step + 1) * part], axis, pairs))  6.79 us
    ppermute x3, waiting for transfers between devices, scatter_group(): got.append(lax.ppermute(far[:, step * part:(step + 1) * part], axis, pairs))  2.62 us
    pallas_call x1, Pallas kernels, prepare(): pl.pallas_call(prepare_body, out_shape=(message, field, field, pair, fiel...  2.17 us
    pallas_call x1, Pallas kernels, inside(): pl.pallas_call(partial(inside_body, pairs=pairs), out_shape=jax.ShapeDtyp...  2.15 us
    pallas_call x1, Pallas kernels, tables(): pl.pallas_call(partial(table_body, rows=rows, width=width, scale=scale, o...  1.82 us
    unnamed x4, local copies, waits for them, and re-layouts  1.49 us
    ppermute x2, starting transfers between devices, swap_other(): return lax.ppermute(array, axis, pairs)  1.3 us
  transfers between devices with their start and end apart: 9, of which 4 were waited for; matrix products, arithmetic and copies ran while one was open for 5% of the time, Pallas kernels for 14%

profile of v6, /device:TPU:0, one launch (start us, length us, event | category | flops | bytes accessed | tf_op | source)
XLA Modules:
  0.0 31.4 jit_solution(1441586952548943243)
XLA Ops:
  0.6 0.0 copy-start
  0.6 2.2 %prepare.1 = (f32[3,16,128]{2,1,0:T(8,128)S(1)}, f32[3,8,16,256]{3,2,1,0:T(8,128)S(1)}, f32[3,8,16,256]{3,2,1,0:T(8,128)S(1)}, f32[2,8,16,256]{3,2,1,0:T(8,128)S...) custom-call(f32[3,8,16,256]{3,2,1,0:T(8,128)} %e_in.1, ...), custom_call_target="tpu_custom_call" | custom-call | tf_op jit(solution)/shard_map/prepare/pallas_call | solution.py:118
  2.8 0.5 %collective-permute-start = (f32[3,16,128]{2,1,0:T(8,128)S(1)}, f32[3,16,128]{2,1,0:T(8,128)S(1)}, u32[]{:S(2)}, u32[]{:S(2)}) collective-permute-start(f32[3,16,128]{2,1,0:T(8,128)S(1)} %get-tuple-element.25), channel_id=1, source_target_pairs={{0,1},{1,0},{2,3},{3,2},{4,5},{5,4},{6,7},{7,6},{8,9},{9,8},{10,11... | collective-permute-start | bytes 73736 | tf_op jit(solution)/shard_map/ppermute | solution.py:573
  3.3 0.7 %collective-permute-start.1 = (f32[3,16,128]{2,1,0:T(8,128)S(1)}, f32[3,16,128]{2,1,0:T(8,128)S(1)}, u32[]{:S(2)}, u32[]{:S(2)}) collective-permute-start(f32[3,16,128]{2,1,0:T(8,128)S(1)} %get-tuple-element.25), channel_id=1, source_target_pairs={{1,2},{2,1},{5,6},{6,5},{9,10},{10,9},{13,14},{14,13},{17,18},{18,... | collective-permute-start | bytes 73736 | tf_op jit(solution)/shard_map/ppermute | solution.py:578
  4.0 1.8 %tables.1 = (bf16[256,4096]{1,0:T(8,128)(2,1)S(1)}, bf16[256,4096]{1,0:T(8,128)(2,1)S(1)}, f32[32,4096]{1,0:T(8,128)S(1)}) custom-call(f32[2,4096]{1,0:T(2,128)S(1)} %get-tuple-element.26.waves_ref), custom_call_target="tpu_custom_call" | custom-call | flops 41943040 | bytes 4194304 | tf_op jit(solution)/shard_map/tables/pallas_call | solution.py:540
  5.8 0.0 collective-permute-done.one_ref
  5.8 0.0 collective-permute-done.1.two_ref
  5.8 0.6 %first_step.1 = (f32[5,8,384]{2,1,0:T(8,128)S(1)}, f32[5,8,384]{2,1,0:T(8,128)S(1)}, f32[3,8,16,384]{3,2,1,0:T(8,128)S(1)}, f32[3,8,16,384]{3,2,1,0:T(8,128)S(1)}) custom-call(f32[3,8,16,256]{3,2,1,0:T(8,128)S(1)} %get-tuple-element.21.e_ref, f32[3,8,16,256]{3,2,1,0:T(8,128)S(1)} %get-tuple-element.22.h_ref, f32[3,8,16,256]{3,2,1,0:T(8,128)S(1)} %get-tuple-element.23.d_ref, ...), custom_call_target="tpu_custom_call" | custom-call | tf_op jit(solution)/shard_map/first_step/pallas_call | solution.py:245
  6.4 2.7 %collective-permute-start.2 = (f32[5,8,384]{2,1,0:T(8,128)S(1)}, f32[5,8,384]{2,1,0:T(8,128)S(1)}, u32[]{:S(2)}, u32[]{:S(2)}) collective-permute-start(f32[5,8,384]{2,1,0:T(8,128)S(1)} %get-tuple-element.31.own_one_ref), channel_id=1, source_target_pairs={{0,4},{4,0},{8,12},{12,8},{1,5},{5,1},{9,13},{13,9},{2,6},{6,2},{1... | collective-permute-start | bytes 184328 | tf_op jit(solution)/shard_map/ppermute | solution.py:573
  9.1 0.7 %collective-permute-start.3 = (f32[5,8,384]{2,1,0:T(8,128)S(1)}, f32[5,8,384]{2,1,0:T(8,128)S(1)}, u32[]{:S(2)}, u32[]{:S(2)}) collective-permute-start(f32[5,8,384]{2,1,0:T(8,128)S(1)} %get-tuple-element.32.own_two_ref), channel_id=1, source_target_pairs={{4,8},{8,4},{5,9},{9,5},{6,10},{10,6},{7,11},{11,7},{20,24},{24,20... | collective-permute-start | bytes 184328 | tf_op jit(solution)/shard_map/ppermute | solution.py:578
  9.8 0.0 copy-done
  9.8 2.1 %inside.1.inner_ref = f32[16,4096]{1,0:T(8,128)S(1)} custom-call(f32[3,8,16,384]{3,2,1,0:T(8,128)S(1)} %get-tuple-element.28.h1_in.h1_ref, f32[3,8,16,384]{3,2,1,0:T(8,128)S(1)} %get-tuple-element.29.e1_in.e1_ref, f32[3,8,16,256]{3,2,1,0:T(8,128)S(1)} %get-tuple-element.30.g_ref, f32[2,8,16,256]{3,2,1,0:T(8,128)S(1)} %get-tuple-element.24.k_ref, ...), custom_call_target="tpu_custom_call" | custom-call | flops 1610612736 | bytes 4194304 | tf_op jit(solution)/shard_map/inside/pallas_call | solution.py:349
  11.9 0.0 collective-permute-done.2.x_one_ref
  11.9 0.0 collective-permute-done.3.x_two_ref
  12.0 0.6 %second_step.1 = (f32[3,8,16,256]{3,2,1,0:T(8,128)S(1)}, f32[3,8,16,256]{3,2,1,0:T(8,128)S(1)}, bf16[128,256]{1,0:T(8,128)(2,1)S(1)}, bf16[128,256]{1,0:T(8,128)(2,1)S(1)}) custom-call(f32[3,8,16,384]{3,2,1,0:T(8,128)S(1)} %get-tuple-element.28.h1_in.h1_ref, f32[3,8,16,384]{3,2,1,0:T(8,128)S(1)} %get-tuple-element.29.e1_in.e1_ref, ...), custom_call_target="tpu_custom_call" | custom-call | tf_op jit(solution)/shard_map/second_step/pallas_call | solution.py:471
  12.6 0.5 %project.3 = f32[16,2048]{1,0:T(8,128)S(1)} custom-call(bf16[128,256]{1,0:T(8,128)(2,1)S(1)} %get-tuple-element.35.even_ref, bf16[128,256]{1,0:T(8,128)(2,1)S(1)} %get-tuple-element.36.odd_ref, bf16[256,4096]{1,0:T(8,128)(2,1)S(1)} %get-tuple-element.37.cos_ref, bf16[256,4096]{1,0:T(8,128)(2,1)S(1)} %get-tuple-element.38.sin_ref, ...), custom_call_target="tpu_custom_call" | custom-call | flops 536870912 | bytes 2097152 | tf_op jit(solution)/shard_map/project/pallas_call | solution.py:561
  13.1 2.9 %collective-permute-start.4 = (f32[16,2048]{1,0:T(8,128)S(1)}, f32[16,2048]{1,0:T(8,128)S(1)}, u32[]{:S(2)}, u32[]{:S(2)}) collective-permute-start(f32[16,2048]{1,0:T(8,128)S(1)} %project.3), channel_id=1, source_target_pairs={{0,1},{1,0},{2,3},{3,2},{4,5},{5,4},{6,7},{7,6},{8,9},{9,8},{10,11... | collective-permute-start | bytes 393224 | tf_op jit(solution)/shard_map/ppermute | solution.py:573
  16.0 0.5 %project.2 = f32[16,2048]{1,0:T(8,128)S(1)} custom-call(bf16[128,256]{1,0:T(8,128)(2,1)S(1)} %get-tuple-element.35.even_ref, bf16[128,256]{1,0:T(8,128)(2,1)S(1)} %get-tuple-element.36.odd_ref, bf16[256,4096]{1,0:T(8,128)(2,1)S(1)} %get-tuple-element.37.cos_ref, bf16[256,4096]{1,0:T(8,128)(2,1)S(1)} %get-tuple-element.38.sin_ref, ...), custom_call_target="tpu_custom_call" | custom-call | flops 536870912 | bytes 2097152 | tf_op jit(solution)/shard_map/project/pallas_call | solution.py:561
  16.5 0.5 %collective-permute-done.4 = f32[16,2048]{1,0:T(8,128)S(1)} collective-permute-done((f32[16,2048]{1,0:T(8,128)S(1)}, f32[16,2048]{1,0:T(8,128)S(1)}, u32[]{:S(2)}, u32[]{:S(2)}) %collective-permute-start.4) | collective-permute-done | bytes 131104 | tf_op jit(solution)/shard_map/ppermute | solution.py:573
  17.0 2.6 %collective-permute-start.7 = (f32[16,512]{1,0:T(8,128)S(1)}, f32[16,512]{1,0:T(8,128)S(1)}, u32[]{:S(2)}, u32[]{:S(2)}) collective-permute-start(f32[16,512]{1,0:T(8,128)S(1)} %get-tuple-element.40), channel_id=1, source_target_pairs={{0,12},{4,0},{8,4},{12,8},{1,13},{5,1},{9,5},{13,9},{2,14},{6,2},{... | collective-permute-start | bytes 98312 | tf_op jit(solution)/shard_map/ppermute | solution.py:628
  19.6 1.6 %collective-permute-start.6 = (f32[16,512]{1,0:T(8,128)S(1)}, f32[16,512]{1,0:T(8,128)S(1)}, u32[]{:S(2)}, u32[]{:S(2)}) collective-permute-start(f32[16,512]{1,0:T(8,128)S(1)} %get-tuple-element.41), channel_id=1, source_target_pairs={{0,4},{4,8},{8,12},{12,0},{1,5},{5,9},{9,13},{13,1},{2,6},{6,10},{... | collective-permute-start | bytes 98312 | tf_op jit(solution)/shard_map/ppermute | solution.py:628
  21.3 2.5 %collective-permute-start.5 = (f32[16,512]{1,0:T(8,128)S(1)}, f32[16,512]{1,0:T(8,128)S(1)}, u32[]{:S(2)}, u32[]{:S(2)}) collective-permute-start(f32[16,512]{1,0:T(8,128)S(1)} %get-tuple-element.39), channel_id=1, source_target_pairs={{0,8},{4,12},{8,0},{12,4},{1,9},{5,13},{9,1},{13,5},{2,10},{6,14},... | collective-permute-start | bytes 98312 | tf_op jit(solution)/shard_map/ppermute | solution.py:628
  23.8 0.0 collective-permute-done.7
  23.8 1.8 %collective-permute-done.6 = f32[16,512]{1,0:T(8,128)S(1)} collective-permute-done((f32[16,512]{1,0:T(8,128)S(1)}, f32[16,512]{1,0:T(8,128)S(1)}, u32[]{:S(2)}, u32[]{:S(2)}) %collective-permute-start.6) | collective-permute-done | bytes 32800 | tf_op jit(solution)/shard_map/ppermute | solution.py:628
  25.6 0.9 %collective-permute-done.5 = f32[16,512]{1,0:T(8,128)S(1)} collective-permute-done((f32[16,512]{1,0:T(8,128)S(1)}, f32[16,512]{1,0:T(8,128)S(1)}, u32[]{:S(2)}, u32[]{:S(2)}) %collective-permute-start.5) | collective-permute-done | bytes 32800 | tf_op jit(solution)/shard_map/ppermute | solution.py:628
  26.5 2.6 %collective-permute-start.8 = (f32[16,256]{1,0:T(8,128)S(1)}, f32[16,256]{1,0:T(8,128)S(1)}, u32[]{:S(2)}, u32[]{:S(2)}) collective-permute-start(f32[16,256]{1,0:T(8,128)S(1)} %slice.29), channel_id=1, source_target_pairs={{0,2},{1,3},{2,0},{3,1},{4,6},{5,7},{6,4},{7,5},{8,10},{9,11},{10,... | collective-permute-start | bytes 49160 | tf_op jit(solution)/shard_map/ppermute | solution.py:573
  29.1 0.7 %copy.12 = f32[3,8,16,256]{3,2,1,0:T(8,128)} copy(f32[3,8,16,256]{3,2,1,0:T(8,128)S(1)} %get-tuple-element.42) | data formatting | bytes 786432
  29.8 0.7 %copy.13 = f32[3,8,16,256]{3,2,1,0:T(8,128)} copy(f32[3,8,16,256]{3,2,1,0:T(8,128)S(1)} %get-tuple-element.43) | data formatting | bytes 786432
  30.5 0.2 collective-permute-done.8
  30.8 0.6 %fusion.2 = f32[256,16]{0,1:T(8,128)} fusion(f32[16,256]{1,0:T(8,128)S(1)} %collective-permute-done.8, f32[16,512]{1,0:T(8,128)S(1)} %fusion.1), kind=kLoop, calls=%fused_computation.4 | loop fusion | flops 4096 | bytes 49152 | tf_op jit(solution)/shard_map/transpose | solution.py:657
  (4 shorter events, 0.0 us)
Async XLA Ops:
  0.6 9.1 %copy-start = (s32[2,16,256]{2,1,0:T(8,128)S(1)}, s32[2,16,256]{2,1,0:T(8,128)}, u32[]{:S(2)}) copy-start(s32[2,16,256]{2,1,0:T(8,128)} %surface_ref.3) | copy-start | bytes 98308
  2.8 3.0 %collective-permute-start = (f32[3,16,128]{2,1,0:T(8,128)S(1)}, f32[3,16,128]{2,1,0:T(8,128)S(1)}, u32[]{:S(2)}, u32[]{:S(2)}) collective-permute-start(f32[3,16,128]{2,1,0:T(8,128)S(1)} %get-tuple-element.25), channel_id=1, source_target_pairs={{0,1},{1,0},{2,3},{3,2},{4,5},{5,4},{6,7},{7,6},{8,9},{9,8},{10,11... | collective-permute-start | bytes 73736 | tf_op jit(solution)/shard_map/ppermute | solution.py:573
  3.3 2.5 %collective-permute-start.1 = (f32[3,16,128]{2,1,0:T(8,128)S(1)}, f32[3,16,128]{2,1,0:T(8,128)S(1)}, u32[]{:S(2)}, u32[]{:S(2)}) collective-permute-start(f32[3,16,128]{2,1,0:T(8,128)S(1)} %get-tuple-element.25), channel_id=1, source_target_pairs={{1,2},{2,1},{5,6},{6,5},{9,10},{10,9},{13,14},{14,13},{17,18},{18,... | collective-permute-start | bytes 73736 | tf_op jit(solution)/shard_map/ppermute | solution.py:578
  6.4 5.5 %collective-permute-start.2 = (f32[5,8,384]{2,1,0:T(8,128)S(1)}, f32[5,8,384]{2,1,0:T(8,128)S(1)}, u32[]{:S(2)}, u32[]{:S(2)}) collective-permute-start(f32[5,8,384]{2,1,0:T(8,128)S(1)} %get-tuple-element.31.own_one_ref), channel_id=1, source_target_pairs={{0,4},{4,0},{8,12},{12,8},{1,5},{5,1},{9,13},{13,9},{2,6},{6,2},{1... | collective-permute-start | bytes 184328 | tf_op jit(solution)/shard_map/ppermute | solution.py:573
  9.1 2.8 %collective-permute-start.3 = (f32[5,8,384]{2,1,0:T(8,128)S(1)}, f32[5,8,384]{2,1,0:T(8,128)S(1)}, u32[]{:S(2)}, u32[]{:S(2)}) collective-permute-start(f32[5,8,384]{2,1,0:T(8,128)S(1)} %get-tuple-element.32.own_two_ref), channel_id=1, source_target_pairs={{4,8},{8,4},{5,9},{9,5},{6,10},{10,6},{7,11},{11,7},{20,24},{24,20... | collective-permute-start | bytes 184328 | tf_op jit(solution)/shard_map/ppermute | solution.py:578
  13.1 3.9 %collective-permute-start.4 = (f32[16,2048]{1,0:T(8,128)S(1)}, f32[16,2048]{1,0:T(8,128)S(1)}, u32[]{:S(2)}, u32[]{:S(2)}) collective-permute-start(f32[16,2048]{1,0:T(8,128)S(1)} %project.3), channel_id=1, source_target_pairs={{0,1},{1,0},{2,3},{3,2},{4,5},{5,4},{6,7},{7,6},{8,9},{9,8},{10,11... | collective-permute-start | bytes 393224 | tf_op jit(solution)/shard_map/ppermute | solution.py:573
  17.0 6.8 %collective-permute-start.7 = (f32[16,512]{1,0:T(8,128)S(1)}, f32[16,512]{1,0:T(8,128)S(1)}, u32[]{:S(2)}, u32[]{:S(2)}) collective-permute-start(f32[16,512]{1,0:T(8,128)S(1)} %get-tuple-element.40), channel_id=1, source_target_pairs={{0,12},{4,0},{8,4},{12,8},{1,13},{5,1},{9,5},{13,9},{2,14},{6,2},{... | collective-permute-start | bytes 98312 | tf_op jit(solution)/shard_map/ppermute | solution.py:628
  19.6 5.9 %collective-permute-start.6 = (f32[16,512]{1,0:T(8,128)S(1)}, f32[16,512]{1,0:T(8,128)S(1)}, u32[]{:S(2)}, u32[]{:S(2)}) collective-permute-start(f32[16,512]{1,0:T(8,128)S(1)} %get-tuple-element.41), channel_id=1, source_target_pairs={{0,4},{4,8},{8,12},{12,0},{1,5},{5,9},{9,13},{13,1},{2,6},{6,10},{... | collective-permute-start | bytes 98312 | tf_op jit(solution)/shard_map/ppermute | solution.py:628
  21.3 5.2 %collective-permute-start.5 = (f32[16,512]{1,0:T(8,128)S(1)}, f32[16,512]{1,0:T(8,128)S(1)}, u32[]{:S(2)}, u32[]{:S(2)}) collective-permute-start(f32[16,512]{1,0:T(8,128)S(1)} %get-tuple-element.39), channel_id=1, source_target_pairs={{0,8},{4,12},{8,0},{12,4},{1,9},{5,13},{9,1},{13,5},{2,10},{6,14},... | collective-permute-start | bytes 98312 | tf_op jit(solution)/shard_map/ppermute | solution.py:628
  26.5 4.3 %collective-permute-start.8 = (f32[16,256]{1,0:T(8,128)S(1)}, f32[16,256]{1,0:T(8,128)S(1)}, u32[]{:S(2)}, u32[]{:S(2)}) collective-permute-start(f32[16,256]{1,0:T(8,128)S(1)} %slice.29), channel_id=1, source_target_pairs={{0,2},{1,3},{2,0},{3,1},{4,6},{5,7},{6,4},{7,5},{8,10},{9,11},{10,... | collective-permute-start | bytes 49160 | tf_op jit(solution)/shard_map/ppermute | solution.py:573
